TPU v7x, 32 devices: a whole 2x2x4 slice. The times are simulated.
32 devices in a mesh: shard: 8 (over z, x), dp: 4 (over y, core).
Axes of the slice: x: 2, y: 2, z: 4, core: 2. Of those that a mesh axis runs over, the one named last changes fastest.
Arguments:
- source: float32 [384, 6, 6, 512], P(('shard', 'dp')), may hold values from -6 to 6
- index_map: int32 [384], P(('shard', 'dp')), may hold values from 0 to 11
- crop_offsets: int32 [384, 2], P(('shard', 'dp')), may hold values from 0 to 2
- flip_flags: int32 [384], P(('shard', 'dp')), may hold values from 0 to 1
- labels: int32 [384], P(('shard', 'dp')), may hold values from 0 to 9
- valid_mask: int32 [384], P(('shard', 'dp')), may hold values from 0 to 1, as said below
- conv_weights: float32 [2, 512, 4608], P(None, 'shard'), may hold values from -0.09375 to 0.09375
- norm_params: float32 [4, 512], P(None, 'shard'), may hold values from -2 to 2, as said below
- head_weights: float32 [512, 10], P('shard'), may hold values from -0.75 to 0.75
- decay_rates: float32 [2, 512, 4608], P(None, 'shard'), may hold values from 0.01 to 0.08
- conv_first: float32 [2, 512, 4608], P(None, 'shard'), may hold values from -0.0390625 to 0.0390625
- conv_second: float32 [2, 512, 4608], P(None, 'shard'), may hold values from 6.457908e-06 to 2.5831632e-05
- norm_first: float32 [4, 512], P(None, 'shard'), may hold values from -0.03125 to 0.03125
- norm_second: float32 [4, 512], P(None, 'shard'), may hold values from 4.1666667e-06 to 1.6666667e-05
- head_first: float32 [512, 10], P('shard'), may hold values from -0.5 to 0.5
- head_second: float32 [512, 10], P('shard'), may hold values from 0.0014648438 to 0.005859375
Outputs:
- loss_sum: float32 [], replicated
- label_total: float32 [], replicated
- conv_updated: float32 [2, 512, 4608], P(None, 'shard')
- conv_moment_one: float32 [2, 512, 4608], P(None, 'shard')
- conv_moment_two: float32 [2, 512, 4608], P(None, 'shard')
- norm_updated: float32 [4, 512], P(None, 'shard')
- norm_moment_one: float32 [4, 512], P(None, 'shard')
- norm_moment_two: float32 [4, 512], P(None, 'shard')
- head_updated: float32 [512, 10], P('shard')
- head_moment_one: float32 [512, 10], P('shard')
- head_moment_two: float32 [512, 10], P('shard')
- hyper_gradient: float32 [2, 512, 4608], P(None, 'shard')
Inputs may be any that keep to these rules, and one draw needn't show every extreme that they name: `valid_mask`: the last image always counts. `norm_params`: rows 0 and 2 are gains, rows 1 and 3 biases.
All inputs are finite; a program needn't handle non-finite values.
Results may differ from a plain program's by a relative error of at most 0.0003.
Values sent between devices are 32-bit elements; how exact they have to be, the bound alone decides.
A program may use at most 256 MiB of HBM per device.

v0:
```python
import jax
import jax.numpy as jnp
from jax import lax
from jax.sharding import PartitionSpec as P

MAP = 4
NEUMANN = 3
STEP = 5


norm_eps = 1e-05
neumann_rate = 10.0
beta_first = 0.5
beta_second = 0.5
adam_eps = 1e-08
decoupled = 0.01


def crop_image(single, offsets, flipped):
    window = lax.dynamic_slice(
        single, (offsets[0], offsets[1], jnp.int32(0)), (MAP, MAP, single.shape[2])
    )
    return jnp.where(flipped == 1, window[:, ::-1, :], window)


def convolve(inputs, kernel):
    padded = jnp.pad(inputs, ((0, 0), (1, 1), (1, 1), (0, 0)))
    taps = [
        padded[:, shift_y : shift_y + MAP, shift_x : shift_x + MAP, :]
        for shift_y in range(3)
        for shift_x in range(3)
    ]
    patches = jnp.concatenate(taps, axis=3)
    return jnp.einsum("bhwk,ck->bhwc", patches, kernel, precision=lax.Precision.HIGHEST)


def channel_sums(hidden):
    return jnp.stack([jnp.sum(hidden, axis=(0, 1, 2)), jnp.sum(hidden * hidden, axis=(0, 1, 2))])


def normalize(hidden, totals, gain, shift, count_rows):
    average = totals[0] / count_rows
    spread = totals[1] / count_rows - average * average
    return (hidden - average) * lax.rsqrt(spread + norm_eps) * gain + shift


def cross_terms(head_matrix, params, hidden, totals, images, labels, valid, count_rows):
    block = jax.nn.silu(normalize(hidden, totals, params[2], params[3], count_rows) + images)
    pooled = jnp.mean(block, axis=(1, 2))
    logits = jnp.dot(pooled, head_matrix, precision=lax.Precision.HIGHEST)
    highest = jnp.max(logits, axis=1, keepdims=True)
    logsum = highest[:, 0] + jnp.log(jnp.sum(jnp.exp(logits - highest), axis=1))
    classes = jnp.arange(logits.shape[1], dtype=jnp.int32)
    target = jnp.sum(jnp.where(labels[:, None] == classes[None, :], logits, 0.0), axis=1)
    return jnp.sum(valid * (logsum - target))


def first_section(kernel, images):
    hidden = convolve(images, kernel)
    return (hidden, channel_sums(hidden))


def second_section(kernel, params, hidden, totals, count_rows):
    activated = jax.nn.silu(normalize(hidden, totals, params[0], params[1], count_rows))
    output = convolve(activated, kernel)
    return (output, channel_sums(output))


def third_back(head_matrix, params, hidden, totals, context):
    images, labels, valid, total_valid, count_rows = context
    cross, pull = jax.vjp(
        lambda matrix, norm_part, hidden_part, totals_part: cross_terms(
            matrix, norm_part, hidden_part, totals_part, images, labels, valid, count_rows
        ),
        head_matrix,
        params,
        hidden,
        totals,
    )
    return (cross,) + tuple(pull(jnp.ones_like(cross) / total_valid))


def second_back(kernel, params, hidden, totals, grad_output, grad_sums, count_rows):
    unused, pull = jax.vjp(
        lambda kernel_part, norm_part, hidden_part, totals_part: second_section(
            kernel_part, norm_part, hidden_part, totals_part, count_rows
        ),
        kernel,
        params,
        hidden,
        totals,
    )
    return tuple(pull((grad_output, grad_sums)))


def first_back(kernel, images, grad_output, grad_sums):
    unused, pull = jax.vjp(lambda kernel_part: first_section(kernel_part, images), kernel)
    return pull((grad_output, grad_sums))[0]


def lift(function, primals, tangents):
    if tangents is None:
        result = function(*primals)
        nothing = tuple((None for member in result)) if isinstance(result, tuple) else None
        return (result, nothing)
    return jax.jvp(function, primals, tangents)


def channel_total(value, tangent):
    stacked = value[None] if tangent is None else jnp.stack([value, tangent])
    summed = lax.psum(stacked, ("shard", "dp"))
    return (summed[0], None if tangent is None else summed[1])


def back_total(value, tangent):
    stacked = value[None] if tangent is None else jnp.stack([value, tangent])
    summed = lax.psum(stacked, ("shard", "dp"))
    return (summed[0], None if tangent is None else summed[1])


def run_pass(weights, tangents, context):
    images, labels, valid, total_valid, count_rows = context
    dual = tangents is not None
    conv_full, norm_full, head_full = weights
    conv_tan, norm_tan, head_tan = tangents if dual else weights

    def choose(*members):
        return members if dual else None

    (hidden_one, sums_one), (tan_hidden_one, tan_sums_one) = lift(
        lambda kernel: first_section(kernel, images), (conv_full[0],), choose(conv_tan[0])
    )
    totals_one, tan_totals_one = channel_total(sums_one, tan_sums_one)
    (hidden_two, sums_two), (tan_hidden_two, tan_sums_two) = lift(
        lambda kernel, params, hidden, totals: second_section(
            kernel, params, hidden, totals, count_rows
        ),
        (conv_full[1], norm_full, hidden_one, totals_one),
        choose(conv_tan[1], norm_tan, tan_hidden_one, tan_totals_one),
    )
    totals_two, tan_totals_two = channel_total(sums_two, tan_sums_two)
    outputs, tan_outputs = lift(
        lambda matrix, params, hidden, totals: third_back(matrix, params, hidden, totals, context),
        (head_full, norm_full, hidden_two, totals_two),
        choose(head_tan, norm_tan, tan_hidden_two, tan_totals_two),
    )
    cross_local, grad_head, grad_norm_two, grad_hidden_two, grad_totals_two = outputs
    tan_cross, tan_head, tan_norm_two, tan_grad_hidden_two, tan_grad_totals_two = tan_outputs
    back_two, tan_back_two = back_total(grad_totals_two, tan_grad_totals_two)
    outputs, tan_outputs = lift(
        lambda kernel, params, hidden, totals, grad_hidden, grad_sums: second_back(
            kernel, params, hidden, totals, grad_hidden, grad_sums, count_rows
        ),
        (conv_full[1], norm_full, hidden_one, totals_one, grad_hidden_two, back_two),
        choose(
            conv_tan[1], norm_tan, tan_hidden_one, tan_totals_one, tan_grad_hidden_two, tan_back_two
        ),
    )
    grad_kernel_two, grad_norm_one, grad_hidden_one, grad_totals_one = outputs
    tan_kernel_two, tan_norm_one, tan_grad_hidden_one, tan_grad_totals_one = tan_outputs
    back_one, tan_back_one = back_total(grad_totals_one, tan_grad_totals_one)
    grad_kernel_one, tan_kernel_one = lift(
        lambda kernel, grad_hidden, grad_sums: first_back(kernel, images, grad_hidden, grad_sums),
        (conv_full[0], grad_hidden_one, back_one),
        choose(conv_tan[0], tan_grad_hidden_one, tan_back_one),
    )
    grads = (
        jnp.stack([grad_kernel_one, grad_kernel_two]),
        grad_norm_one + grad_norm_two,
        grad_head,
    )
    tan_grads = None
    if dual:
        tan_grads = (
            jnp.stack([tan_kernel_one, tan_kernel_two]),
            tan_norm_one + tan_norm_two,
            tan_head,
        )
    return (grads, tan_grads, cross_local)


def reduce_shares(whole):
    shares = (
        lax.psum_scatter(whole[0], "shard", scatter_dimension=1, tiled=True),
        lax.psum_scatter(whole[1], "shard", scatter_dimension=1, tiled=True),
        lax.psum_scatter(whole[2], "shard", scatter_dimension=0, tiled=True),
    )
    return lax.psum((shares[0], shares[1], shares[2]), "dp")


def adamw(weight, grad, first, second, rate):
    first = beta_first * first + (1.0 - beta_first) * grad
    second = beta_second * second + (1.0 - beta_second) * grad * grad
    first_hat = first / (1.0 - beta_first**STEP)
    second_hat = second / (1.0 - beta_second**STEP)
    update = first_hat / (jnp.sqrt(second_hat) + adam_eps) + decoupled * weight
    return (weight - rate * update, first, second)


def shards(
    source,
    index_map,
    crop_offsets,
    flip_flags,
    labels,
    valid_mask,
    conv_weights,
    norm_params,
    head_weights,
    decay_rates,
    conv_first,
    conv_second,
    norm_first,
    norm_second,
    head_first,
    head_second,
):
    picked = source[index_map]
    images = jax.vmap(crop_image)(picked, crop_offsets, flip_flags)
    valid = valid_mask.astype(jnp.float32)
    label_total = lax.psum(jnp.sum(valid), ("shard", "dp"))
    count_rows = float(images.shape[0] * MAP * MAP * lax.axis_size("shard") * lax.axis_size("dp"))
    context = (images, labels, valid, label_total, count_rows)
    whole = (
        lax.all_gather(conv_weights, "shard", axis=1, tiled=True),
        lax.all_gather(norm_params, "shard", axis=1, tiled=True),
        lax.all_gather(head_weights, "shard", axis=0, tiled=True),
    )
    grads_whole, unused, cross_local = run_pass(whole, None, context)
    loss_sum = lax.psum(cross_local, ("shard", "dp"))
    grads = reduce_shares(grads_whole)
    grads = (grads[0] + decay_rates * conv_weights, grads[1], grads[2])
    vector = grads
    series = grads
    for turn in range(NEUMANN):
        joined = (
            lax.all_gather(conv_weights, "shard", axis=1, tiled=True),
            lax.all_gather(norm_params, "shard", axis=1, tiled=True),
            lax.all_gather(head_weights, "shard", axis=0, tiled=True),
            lax.all_gather(vector[0], "shard", axis=1, tiled=True),
            lax.all_gather(vector[1], "shard", axis=1, tiled=True),
            lax.all_gather(vector[2], "shard", axis=0, tiled=True),
        )
        current = (joined[0], joined[1], joined[2])
        direction = (joined[3], joined[4], joined[5])
        unused_grads, product_whole, unused_cross = run_pass(current, direction, context)
        product = reduce_shares(product_whole)
        product = (product[0] + decay_rates * vector[0], product[1], product[2])
        vector = tuple(
            (previous - neumann_rate * change for previous, change in zip(vector, product))
        )
        series = tuple((summed + change for summed, change in zip(series, vector)))
    hyper_gradient = -neumann_rate * conv_weights * series[0]
    conv_new, conv_one, conv_two = adamw(conv_weights, grads[0], conv_first, conv_second, 0.015)
    norm_new, norm_one, norm_two = adamw(norm_params, grads[1], norm_first, norm_second, 0.3)
    head_new, head_one, head_two = adamw(head_weights, grads[2], head_first, head_second, 0.13)
    return (
        loss_sum,
        label_total,
        conv_new,
        conv_one,
        conv_two,
        norm_new,
        norm_one,
        norm_two,
        head_new,
        head_one,
        head_two,
        hyper_gradient,
    )


def solution(mesh):
    in_specs = (
        P(("shard", "dp"), None, None, None),
        P(("shard", "dp")),
        P(("shard", "dp"), None),
        P(("shard", "dp")),
        P(("shard", "dp")),
        P(("shard", "dp")),
        P(None, "shard", None),
        P(None, "shard"),
        P("shard", None),
        P(None, "shard", None),
        P(None, "shard", None),
        P(None, "shard", None),
        P(None, "shard"),
        P(None, "shard"),
        P("shard", None),
        P("shard", None),
    )
    out_specs = (
        P(),
        P(),
        P(None, "shard", None),
        P(None, "shard", None),
        P(None, "shard", None),
        P(None, "shard"),
        P(None, "shard"),
        P(None, "shard"),
        P("shard", None),
        P("shard", None),
        P("shard", None),
        P(None, "shard", None),
    )
    return jax.shard_map(shards, mesh=mesh, in_specs=in_specs, out_specs=out_specs, check_vma=False)
```

profile of v0, /device:TPU:0, one launch (start us, length us, event | category | flops | bytes accessed | tf_op | source)
XLA Modules:
  0.0 4478.0 jit_solution(11183306202578602510)
XLA Ops:
  8.0 56.7 %all-gather.1 = f32[8,64,10]{1,2,0:T(8,128)S(1)} all-gather(f32[1,64,10]{1,2,0:T(8,128)} %bitcast.893), channel_id=1, replica_groups=mesh['shard'=8,'dp'=4] {'shard'}, dimensions={0}, use_global_device_ids=true | all-gather | bytes 23040 | tf_op jit(solution)/shard_map/all_gather | solution.py:227
  64.8 30.5 all-gather
  107.5 268.5 %all-gather.13.cloned.1.call-done = f32[2,512,4608]{2,1,0:T(8,128)} async-done(((f32[2,64,4608]{2,1,0:T(8,128)}), f32[2,512,4608]{2,1,0:T(8,128)}) %all-gather.13.cloned.1.call-update) | async-done | bytes 18874384 | tf_op jit(solution)/shard_map/all_gather | solution.py:225
  376.0 11.4 fusion.390
  387.4 39.5 psum.196
  427.7 12.5 fusion.389
  440.2 41.1 all-reduce.118
  487.2 39.5 psum.200
  526.7 12.9 convolution_bitcast_fusion.3
  549.9 41.2 psum.201
  608.7 313.2 %reduce-scatter.23.cloned.1.call-done = f32[2,64,4608]{2,1,0:T(8,128)} async-done(((f32[2,512,4608]{2,1,0:T(8,128)}), f32[2,64,4608]{2,1,0:T(8,128)}) %reduce-scatter.23.cloned.1.call-update) | async-done | bytes 2359312 | tf_op jit(solution)/shard_map/reduce_scatter | solution.py:184
  924.4 54.7 %all-reduce.127.cloned.1.call-done = f32[2,64,4608]{2,1,0:T(8,128)} async-done(((f32[2,64,4608]{2,1,0:T(8,128)}), f32[2,64,4608]{2,1,0:T(8,128)}) %all-reduce.127.cloned.1.call-update) | async-done | bytes 2359312 | tf_op jit(solution)/shard_map/psum | solution.py:188
  987.7 55.9 %reduce-scatter.31.cloned.1.call-done = f32[64,4]{1,0:T(8,128)} async-done(((f32[512,4]{1,0:T(8,128)}), f32[64,4]{1,0:T(8,128)}) %reduce-scatter.31.cloned.1.call-update) | async-done | bytes 1040
  1044.5 62.7 %reduce-scatter.33.cloned.1.call-done = f32[64,10]{1,0:T(8,128)} async-done(((f32[512,10]{1,0:T(8,128)}), f32[64,10]{1,0:T(8,128)}) %reduce-scatter.33.cloned.1.call-update) | async-done | bytes 2576
  1118.7 45.2 %all-gather.2 = f32[8,64,4]{1,2,0:T(4,128)S(1)} all-gather(f32[1,64,4]{1,2,0:T(4,128)S(1)} %bitcast.930), channel_id=1, replica_groups=mesh['shard'=8,'dp'=4] {'shard'}, dimensions={0}, use_global_device_ids=true | all-gather | bytes 9216 | tf_op jit(solution)/shard_map/all_gather | solution.py:241
  1164.0 36.9 all-gather.3
  1201.0 271.2 %all-gather.15.cloned.1.call-done = f32[2,512,4608]{2,1,0:T(8,128)} async-done(((f32[2,64,4608]{2,1,0:T(8,128)}), f32[2,512,4608]{2,1,0:T(8,128)}) %all-gather.15.cloned.1.call-update) | async-done | bytes 18874384 | tf_op jit(solution)/shard_map/all_gather | solution.py:240
  1472.2 11.4 fusion.388
  1483.7 39.8 psum.205
  1524.9 14.1 fusion.381
  1558.3 41.0 psum.206
  1604.3 39.4 psum.207
  1645.4 12.1 fusion.437
  1657.6 12.7 fusion.6
  1679.2 12.3 fusion.15
  1707.1 41.3 psum.208
  1748.5 11.6 convolution_bitcast_fusion.2
  1767.3 312.7 %reduce-scatter.25.cloned.1.call-done = f32[2,64,4608]{2,1,0:T(8,128)} async-done(((f32[2,512,4608]{2,1,0:T(8,128)}), f32[2,64,4608]{2,1,0:T(8,128)}) %reduce-scatter.25.cloned.1.call-update) | async-done | bytes 2359312 | tf_op jit(solution)/shard_map/reduce_scatter | solution.py:184
  2082.5 54.7 %all-reduce.129.cloned.1.call-done = f32[2,64,4608]{2,1,0:T(8,128)} async-done(((f32[2,64,4608]{2,1,0:T(8,128)}), f32[2,64,4608]{2,1,0:T(8,128)}) %all-reduce.129.cloned.1.call-update) | async-done | bytes 2359312 | tf_op jit(solution)/shard_map/psum | solution.py:188
  2141.5 60.4 %reduce-scatter.35.cloned.1.call-done = f32[64,4]{1,0:T(8,128)} async-done(((f32[512,4]{1,0:T(8,128)}), f32[64,4]{1,0:T(8,128)}) %reduce-scatter.35.cloned.1.call-update) | async-done | bytes 1040
  2202.7 62.6 %reduce-scatter.37.cloned.1.call-done = f32[64,10]{1,0:T(8,128)} async-done(((f32[512,10]{1,0:T(8,128)}), f32[64,10]{1,0:T(8,128)}) %reduce-scatter.37.cloned.1.call-update) | async-done | bytes 2576
  2276.9 44.7 all-gather.4
  2322.4 36.2 all-gather.5
  2359.4 270.6 %all-gather.17.cloned.1.call-done = f32[2,512,4608]{2,1,0:T(8,128)} async-done(((f32[2,64,4608]{2,1,0:T(8,128)}), f32[2,512,4608]{2,1,0:T(8,128)}) %all-gather.17.cloned.1.call-update) | async-done | bytes 18874384 | tf_op jit(solution)/shard_map/all_gather | solution.py:240
  2630.0 12.2 fusion.386
  2642.2 39.8 psum.210
  2686.5 13.1 fusion.375
  2719.7 41.0 psum.212
  2772.0 39.4 psum.214
  2813.7 12.1 fusion.438
  2825.8 12.7 fusion.5
  2847.4 12.3 fusion.14
  2876.1 41.3 psum.215
  2917.4 11.5 convolution_bitcast_fusion.1
  2928.8 11.0 pad_maximum_fusion.2
  2940.0 312.7 %reduce-scatter.27.cloned.1.call-done = f32[2,64,4608]{2,1,0:T(8,128)} async-done(((f32[2,512,4608]{2,1,0:T(8,128)}), f32[2,64,4608]{2,1,0:T(8,128)}) %reduce-scatter.27.cloned.1.call-update) | async-done | bytes 2359312 | tf_op jit(solution)/shard_map/reduce_scatter | solution.py:184
  3255.2 54.7 %all-reduce.131.cloned.1.call-done = f32[2,64,4608]{2,1,0:T(8,128)} async-done(((f32[2,64,4608]{2,1,0:T(8,128)}), f32[2,64,4608]{2,1,0:T(8,128)}) %all-reduce.131.cloned.1.call-update) | async-done | bytes 2359312 | tf_op jit(solution)/shard_map/psum | solution.py:188
  3316.0 58.4 %reduce-scatter.39.cloned.1.call-done = f32[64,4]{1,0:T(8,128)} async-done(((f32[512,4]{1,0:T(8,128)}), f32[64,4]{1,0:T(8,128)}) %reduce-scatter.39.cloned.1.call-update) | async-done | bytes 1040
  3375.2 62.7 %reduce-scatter.41.cloned.1.call-done = f32[64,10]{1,0:T(8,128)} async-done(((f32[512,10]{1,0:T(8,128)}), f32[64,10]{1,0:T(8,128)}) %reduce-scatter.41.cloned.1.call-update) | async-done | bytes 2576
  3448.9 45.2 %all-gather.6 = f32[8,64,4]{1,2,0:T(4,128)S(1)} all-gather(f32[1,64,4]{1,2,0:T(4,128)S(1)} %subtract_bitcast_fusion.1), channel_id=1, replica_groups=mesh['shard'=8,'dp'=4] {'shard'}, dimensions={0}, use_global_device_ids=true | all-gather | bytes 9216 | tf_op jit(solution)/shard_map/all_gather | solution.py:241
  3494.1 36.9 all-gather.7
  3531.1 271.2 %all-gather.19.cloned.1.call-done = f32[2,512,4608]{2,1,0:T(8,128)} async-done(((f32[2,64,4608]{2,1,0:T(8,128)}), f32[2,512,4608]{2,1,0:T(8,128)}) %all-gather.19.cloned.1.call-update) | async-done | bytes 18874384 | tf_op jit(solution)/shard_map/all_gather | solution.py:240
  3802.4 11.4 fusion.384
  3813.8 39.8 psum.217
  3857.0 13.1 fusion.373
  3870.1 10.9 fusion.17
  3889.4 41.0 psum.219
  3935.8 39.6 psum.221
  3977.3 12.1 fusion.439
  4021.4 12.3 fusion.4
  4033.7 41.1 all-reduce.117
  4074.9 11.2 convolution_bitcast_fusion
  4093.0 313.5 %reduce-scatter.29.cloned.1.call-done = f32[2,64,4608]{2,1,0:T(8,128)} async-done(((f32[2,512,4608]{2,1,0:T(8,128)}), f32[2,64,4608]{2,1,0:T(8,128)}) %reduce-scatter.29.cloned.1.call-update) | async-done | bytes 2359312 | tf_op jit(solution)/shard_map/reduce_scatter | solution.py:184
  4406.6 57.1 %all-reduce.133.cloned.1.call-done = f32[2,64,4608]{2,1,0:T(8,128)} async-done(((f32[2,64,4608]{2,1,0:T(8,128)}), f32[2,64,4608]{2,1,0:T(8,128)}) %all-reduce.133.cloned.1.call-update) | async-done | bytes 2359312 | tf_op jit(solution)/shard_map/psum | solution.py:188
  (694 shorter events, 296.4 us)
Async XLA Ops:
  7.2 368.8 %all-gather.13.cloned.1.call-start = ((), (), s32[]{:S(2)}) async-start(), calls=%async_computation.10 | async-start | bytes 21233664 | tf_op jit(solution)/shard_map/all_gather | solution.py:225
  8.0 913.9 %reduce-scatter.23.cloned.1.call-start = ((), (), s32[]{:S(2)}) async-start(), calls=%async_computation.11 | async-start | bytes 21233664 | tf_op jit(solution)/shard_map/reduce_scatter | solution.py:184
  64.8 418.3 %copy-start.16 = (f32[512,10]{0,1:T(8,128)}, f32[512,10]{0,1:T(8,128)S(1)}, u32[]{:S(2)}) copy-start(f32[512,10]{0,1:T(8,128)S(1)} %reshape.2240) | copy-start | bytes 61444
  98.6 383.4 %copy-start.5 = (f32[12,4,4,512]{3,0,2,1:T(8,128)}, f32[12,4,4,512]{3,0,2,1:T(8,128)S(1)}, u32[]{:S(2)}) copy-start(f32[12,4,4,512]{3,0,2,1:T(8,128)S(1)} %gather_fusion.1) | copy-start | bytes 1179652
  99.3 1500.1 %copy-start.55 = (pred[12]{0:T(512)(128)(4,1)}, pred[12]{0:T(512)(128)(4,1)S(1)}, u32[]{:S(2)}) copy-start(pred[12]{0:T(512)(128)(4,1)S(1)} %broadcast_compare_fusion.4) | copy-start | bytes 40
  482.0 1599.3 %copy-start.40 = (f32[12]{0:T(128)}, f32[12]{0:T(128)S(1)}, u32[]{:S(2)}) copy-start(f32[12]{0:T(128)S(1)} %get-tuple-element.263) | copy-start | bytes 148
  482.5 440.5 %copy-start.63 = (f32[12]{0:T(128)}, f32[12]{0:T(128)S(1)}, u32[]{:S(2)}) copy-start(f32[12]{0:T(128)S(1)} %get-tuple-element.447) | copy-start | bytes 148
  608.6 313.4 %copy-start.88 = (f32[512]{0:T(512)S(1)}, f32[512]{0:T(512)}, u32[]{:S(2)}) copy-start(f32[512]{0:T(512)} %get-tuple-element.131) | copy-start | bytes 6148
  608.6 313.4 %copy-start.89 = (f32[512]{0:T(512)S(1)}, f32[512]{0:T(512)}, u32[]{:S(2)}) copy-start(f32[512]{0:T(512)} %get-tuple-element.171) | copy-start | bytes 6148
  608.6 314.4 %copy-start.100 = (f32[12]{0:T(128)S(1)}, f32[12]{0:T(128)}, u32[]{:S(2)}) copy-start(f32[12]{0:T(128)} %copy-done.99) | copy-start | bytes 148
  608.6 314.4 %copy-start.106 = (f32[12]{0:T(128)S(1)}, f32[12]{0:T(128)}, u32[]{:S(2)}) copy-start(f32[12]{0:T(128)} %copy-done.105) | copy-start | bytes 148
  608.7 370.5 %copy-start.4 = (f32[2,64,4608]{2,1,0:T(8,128)S(1)}, f32[2,64,4608]{2,1,0:T(8,128)}, u32[]{:S(2)}) copy-start(f32[2,64,4608]{2,1,0:T(8,128)} %param.35) | copy-start | bytes 7077892
  608.7 370.5 %all-reduce.127.cloned.1.call-start = ((), (), s32[]{:S(2)}) async-start(), calls=%async_computation.12 | async-start | bytes 4718592 | tf_op jit(solution)/shard_map/psum | solution.py:188
  921.9 121.7 %reduce-scatter.31.cloned.1.call-start = ((), (), s32[]{:S(2)}) async-start(), calls=%async_computation.22 | async-start | bytes 294912
  922.9 184.2 %reduce-scatter.33.cloned.1.call-start = ((), (), s32[]{:S(2)}) async-start(), calls=%async_computation.23 | async-start | bytes 294912
  924.3 547.8 %all-gather.15.cloned.1.call-start = ((), (), s32[]{:S(2)}) async-start(), calls=%async_computation.13 | async-start | bytes 21233664 | tf_op jit(solution)/shard_map/all_gather | solution.py:240
  987.7 1092.3 %reduce-scatter.25.cloned.1.call-start = ((), (), s32[]{:S(2)}) async-start(), calls=%async_computation.14 | async-start | bytes 21233664 | tf_op jit(solution)/shard_map/reduce_scatter | solution.py:184
  1118.1 365.6 %copy-start.35 = (f32[64,10]{0,1:T(8,128)}, f32[64,10]{0,1:T(8,128)S(1)}, u32[]{:S(2)}) copy-start(f32[64,10]{0,1:T(8,128)S(1)} %get-tuple-element.202) | copy-start | bytes 7684
  1767.2 312.9 %copy-start.84 = (f32[512]{0:T(512)S(1)}, f32[512]{0:T(512)}, u32[]{:S(2)}) copy-start(f32[512]{0:T(512)} %get-tuple-element.110) | copy-start | bytes 6148
  1767.2 312.9 %copy-start.85 = (f32[512]{0:T(512)S(1)}, f32[512]{0:T(512)}, u32[]{:S(2)}) copy-start(f32[512]{0:T(512)} %get-tuple-element.159) | copy-start | bytes 6148
  1767.2 312.9 %copy-start.90 = (f32[512]{0:T(512)S(1)}, f32[512]{0:T(512)}, u32[]{:S(2)}) copy-start(f32[512]{0:T(512)} %get-tuple-element.114) | copy-start | bytes 6148
  1767.2 312.9 %copy-start.91 = (f32[512]{0:T(512)S(1)}, f32[512]{0:T(512)}, u32[]{:S(2)}) copy-start(f32[512]{0:T(512)} %get-tuple-element.158) | copy-start | bytes 6148
  1767.2 313.9 %copy-start.32 = (f32[12,10]{0,1:T(8,128)S(1)}, f32[12,10]{0,1:T(8,128)}, u32[]{:S(2)}) copy-start(f32[12,10]{0,1:T(8,128)} %copy-done.31) | copy-start | bytes 1444
  1767.2 313.8 %copy-start.102 = (f32[12]{0:T(128)S(1)}, f32[12]{0:T(128)}, u32[]{:S(2)}) copy-start(f32[12]{0:T(128)} %copy-done.101) | copy-start | bytes 148
  1767.2 314.1 %copy-start.28 = (f32[12,512]{1,0:T(8,128)S(1)}, f32[12,512]{1,0:T(8,128)}, u32[]{:S(2)}) copy-start(f32[12,512]{1,0:T(8,128)} %copy-done.27) | copy-start | bytes 73732
  1767.2 314.1 %copy-start.59 = (f32[12]{0:T(128)S(1)}, f32[12]{0:T(128)}, u32[]{:S(2)}) copy-start(f32[12]{0:T(128)} %copy-done.58) | copy-start | bytes 148
  1767.2 314.1 %copy-start.77 = (f32[12]{0:T(128)S(1)}, f32[12]{0:T(128)}, u32[]{:S(2)}) copy-start(f32[12]{0:T(128)} %copy-done.76) | copy-start | bytes 148
  1767.2 314.1 %copy-start.81 = (f32[12]{0:T(128)S(1)}, f32[12]{0:T(128)}, u32[]{:S(2)}) copy-start(f32[12]{0:T(128)} %copy-done.80) | copy-start | bytes 148
  1767.3 369.9 %copy-start.2 = (f32[2,64,4608]{2,1,0:T(8,128)S(1)}, f32[2,64,4608]{2,1,0:T(8,128)}, u32[]{:S(2)}) copy-start(f32[2,64,4608]{2,1,0:T(8,128)} %get-tuple-element.212) | copy-start | bytes 7077892
  1767.3 369.9 %all-reduce.129.cloned.1.call-start = ((), (), s32[]{:S(2)}) async-start(), calls=%async_computation.15 | async-start | bytes 4718592 | tf_op jit(solution)/shard_map/psum | solution.py:188
  2080.0 121.9 %reduce-scatter.35.cloned.1.call-start = ((), (), s32[]{:S(2)}) async-start(), calls=%async_computation.24 | async-start | bytes 294912
  2081.2 184.1 %reduce-scatter.37.cloned.1.call-start = ((), (), s32[]{:S(2)}) async-start(), calls=%async_computation.25 | async-start | bytes 294912
  2082.4 193.9 %copy-start.66 = (f32[4,64]{1,0:T(4,128)S(1)}, f32[4,64]{1,0:T(4,128)}, u32[]{:S(2)}) copy-start(f32[4,64]{1,0:T(4,128)} %copy-done.65) | copy-start | bytes 3076
  2082.4 239.3 %copy-start.36 = (f32[64,10]{0,1:T(8,128)S(1)}, f32[64,10]{0,1:T(8,128)}, u32[]{:S(2)}) copy-start(f32[64,10]{0,1:T(8,128)} %copy-done.35) | copy-start | bytes 7684
  2082.4 239.3 %copy-start.45 = (f32[64,10]{0,1:T(8,128)S(1)}, f32[64,10]{0,1:T(8,128)}, u32[]{:S(2)}) copy-start(f32[64,10]{0,1:T(8,128)} %param.34) | copy-start | bytes 7684
  2082.4 239.3 %copy-start.94 = (f32[64,10]{0,1:T(8,128)S(1)}, f32[64,10]{0,1:T(8,128)}, u32[]{:S(2)}) copy-start(f32[64,10]{0,1:T(8,128)} %param.40) | copy-start | bytes 7684
  2082.5 239.3 %copy-start.95 = (f32[64,10]{0,1:T(8,128)S(1)}, f32[64,10]{0,1:T(8,128)}, u32[]{:S(2)}) copy-start(f32[64,10]{0,1:T(8,128)} %param.41) | copy-start | bytes 7684
  2082.5 547.5 %all-gather.17.cloned.1.call-start = ((), (), s32[]{:S(2)}) async-start(), calls=%async_computation.16 | async-start | bytes 21233664 | tf_op jit(solution)/shard_map/all_gather | solution.py:240
  2141.5 1111.2 %reduce-scatter.27.cloned.1.call-start = ((), (), s32[]{:S(2)}) async-start(), calls=%async_computation.17 | async-start | bytes 21233664 | tf_op jit(solution)/shard_map/reduce_scatter | solution.py:184
  2359.4 322.8 %copy-start.72 = (f32[1,512]{1,0:T(1,128)}, f32[1,512]{1,0:T(1,128)S(1)}, u32[]{:S(2)}) copy-start(f32[1,512]{1,0:T(1,128)S(1)} %get-tuple-element.384) | copy-start | bytes 6148
  2359.4 322.8 %copy-start.74 = (f32[1,512]{1,0:T(1,128)}, f32[1,512]{1,0:T(1,128)S(1)}, u32[]{:S(2)}) copy-start(f32[1,512]{1,0:T(1,128)S(1)} %get-tuple-element.383) | copy-start | bytes 6148
  2359.4 401.4 %copy-start.44 = (f32[1,512]{1,0:T(1,128)}, f32[1,512]{1,0:T(1,128)S(1)}, u32[]{:S(2)}) copy-start(f32[1,512]{1,0:T(1,128)S(1)} %get-tuple-element.381) | copy-start | bytes 6148
  2359.4 401.4 %copy-start.62 = (f32[1,512]{1,0:T(1,128)}, f32[1,512]{1,0:T(1,128)S(1)}, u32[]{:S(2)}) copy-start(f32[1,512]{1,0:T(1,128)S(1)} %get-tuple-element.382) | copy-start | bytes 6148
  2939.8 312.9 %copy-start.86 = (f32[512]{0:T(512)S(1)}, f32[512]{0:T(512)}, u32[]{:S(2)}) copy-start(f32[512]{0:T(512)} %get-tuple-element.108) | copy-start | bytes 6148
  2939.8 312.9 %copy-start.87 = (f32[512]{0:T(512)S(1)}, f32[512]{0:T(512)}, u32[]{:S(2)}) copy-start(f32[512]{0:T(512)} %get-tuple-element.149) | copy-start | bytes 6148
  2939.8 312.9 %copy-start.92 = (f32[512]{0:T(512)S(1)}, f32[512]{0:T(512)}, u32[]{:S(2)}) copy-start(f32[512]{0:T(512)} %get-tuple-element.112) | copy-start | bytes 6148
  2939.8 312.9 %copy-start.93 = (f32[512]{0:T(512)S(1)}, f32[512]{0:T(512)}, u32[]{:S(2)}) copy-start(f32[512]{0:T(512)} %get-tuple-element.148) | copy-start | bytes 6148
  2939.8 313.9 %copy-start.34 = (f32[12,10]{0,1:T(8,128)S(1)}, f32[12,10]{0,1:T(8,128)}, u32[]{:S(2)}) copy-start(f32[12,10]{0,1:T(8,128)} %copy-done.33) | copy-start | bytes 1444
  2939.8 313.8 %copy-start.104 = (f32[12]{0:T(128)S(1)}, f32[12]{0:T(128)}, u32[]{:S(2)}) copy-start(f32[12]{0:T(128)} %copy-done.103) | copy-start | bytes 148
  2939.8 314.1 %copy-start.30 = (f32[12,512]{1,0:T(8,128)S(1)}, f32[12,512]{1,0:T(8,128)}, u32[]{:S(2)}) copy-start(f32[12,512]{1,0:T(8,128)} %copy-done.29) | copy-start | bytes 73732
  2939.9 314.1 %copy-start.39 = (s32[12]{0:T(128)S(1)}, s32[12]{0:T(128)}, u32[]{:S(2)}) copy-start(s32[12]{0:T(128)} %param.30) | copy-start | bytes 148
  2939.9 314.1 %copy-start.41 = (f32[12]{0:T(128)S(1)}, f32[12]{0:T(128)}, u32[]{:S(2)}) copy-start(f32[12]{0:T(128)} %copy-done.40) | copy-start | bytes 148
  2939.9 314.1 %copy-start.61 = (f32[12]{0:T(128)S(1)}, f32[12]{0:T(128)}, u32[]{:S(2)}) copy-start(f32[12]{0:T(128)} %copy-done.60) | copy-start | bytes 148
  2939.9 314.1 %copy-start.79 = (f32[12]{0:T(128)S(1)}, f32[12]{0:T(128)}, u32[]{:S(2)}) copy-start(f32[12]{0:T(128)} %copy-done.78) | copy-start | bytes 148
  2939.9 314.1 %copy-start.83 = (f32[12]{0:T(128)S(1)}, f32[12]{0:T(128)}, u32[]{:S(2)}) copy-start(f32[12]{0:T(128)} %copy-done.82) | copy-start | bytes 148
  2939.9 370.0 %all-reduce.131.cloned.1.call-start = ((), (), s32[]{:S(2)}) async-start(), calls=%async_computation.18 | async-start | bytes 4718592 | tf_op jit(solution)/shard_map/psum | solution.py:188
  3252.7 121.7 %reduce-scatter.39.cloned.1.call-start = ((), (), s32[]{:S(2)}) async-start(), calls=%async_computation.26 | async-start | bytes 294912
  3253.9 184.0 %reduce-scatter.41.cloned.1.call-start = ((), (), s32[]{:S(2)}) async-start(), calls=%async_computation.27 | async-start | bytes 294912
  3255.1 239.0 %copy-start.37 = (f32[64,10]{0,1:T(8,128)S(1)}, f32[64,10]{0,1:T(8,128)}, u32[]{:S(2)}) copy-start(f32[64,10]{0,1:T(8,128)} %copy-done.35) | copy-start | bytes 7684
  3255.1 239.0 %copy-start.47 = (f32[64,10]{0,1:T(8,128)S(1)}, f32[64,10]{0,1:T(8,128)}, u32[]{:S(2)}) copy-start(f32[64,10]{0,1:T(8,128)} %copy-done.46) | copy-start | bytes 7684
  3255.1 547.2 %all-gather.19.cloned.1.call-start = ((), (), s32[]{:S(2)}) async-start(), calls=%async_computation.19 | async-start | bytes 21233664 | tf_op jit(solution)/shard_map/all_gather | solution.py:240
  3315.3 1091.2 %reduce-scatter.29.cloned.1.call-start = ((), (), s32[]{:S(2)}) async-start(), calls=%async_computation.20 | async-start | bytes 21233664 | tf_op jit(solution)/shard_map/reduce_scatter | solution.py:184
  4092.9 370.7 %copy-start.3 = (f32[2,64,4608]{2,1,0:T(8,128)S(1)}, f32[2,64,4608]{2,1,0:T(8,128)}, u32[]{:S(2)}) copy-start(f32[2,64,4608]{2,1,0:T(8,128)} %get-tuple-element.212) | copy-start | bytes 7077892
  4092.9 370.7 %all-reduce.133.cloned.1.call-start = ((), (), s32[]{:S(2)}) async-start(), calls=%async_computation.21 | async-start | bytes 4718592 | tf_op jit(solution)/shard_map/psum | solution.py:188
  (117 other events, 3812.0 us)
Sparse Core Ops, SparseCore 0:
  9.6 366.3 all-gather.12
  608.8 313.0 reduce-scatter.22
  924.3 54.7 all-reduce.126
  982.3 61.2 reduce-scatter.30
  1046.8 60.2 reduce-scatter.32
  1109.1 363.0 all-gather.14
  1767.4 312.5 reduce-scatter.24
  2082.4 54.7 all-reduce.128
  2140.5 61.3 reduce-scatter.34
  2205.1 60.2 reduce-scatter.36
  2266.9 363.0 all-gather.16
  2940.0 312.5 reduce-scatter.26
  3255.0 54.8 all-reduce.130
  3313.1 61.2 reduce-scatter.38
  3377.6 60.2 reduce-scatter.40
  3439.3 363.0 all-gather.18
  4093.0 313.4 reduce-scatter.28
  4408.8 54.8 all-reduce.132
where the time goes:
time: 4490 us; the launch traced here: 4480 us
  waiting for transfers between devices  2920 us (65%)
  blocking collectives  1010 us (22%)
  matrix products  394 us (9%)
  other arithmetic  98.2 us (2%)
    reduce_scatter x4, waiting for transfers between devices, reduce_shares(): lax.psum_scatter(whole[0], 'shard', scatter_dimension=1, tiled=True)  1250 us
    all_gather x3, waiting for transfers between devices, shards(): lax.all_gather(vector[0], 'shard', axis=1, tiled=True)  813 us
    dot_general x35, matrix products, convolve(): jnp.einsum('bhwk,ck->bhwc', patches, kernel, precision=lax.Precision.HIGH...  386 us
    unnamed x24, waiting for transfers between devices  364 us
    psum x8, blocking collectives, channel_total(): summed = lax.psum(stacked, ('shard', 'dp'))  323 us
    psum x7, blocking collectives, back_total(): summed = lax.psum(stacked, ('shard', 'dp'))  282 us
    all_gather x1, waiting for transfers between devices, shards(): lax.all_gather(conv_weights, 'shard', axis=1, tiled=True)  268 us
    psum x4, waiting for transfers between devices, reduce_shares(): return lax.psum((shares[0], shares[1], shares[2]), 'dp')  221 us
  transfers between devices with their start and end apart: 18, of which 18 were waited for; matrix products, arithmetic and copies ran while one was open for 1% of the time, Pallas kernels for 0%

commit v1 on v0

v1 whole, which is shorter than its diff:
```python
import jax
import jax.numpy as jnp
from jax import lax
from jax.sharding import PartitionSpec as P

MAP = 4
NEUMANN = 3
STEP = 5
TAPS = 9

norm_eps = 1e-05
neumann_rate = 10.0
beta_first = 0.5
beta_second = 0.5
adam_eps = 1e-08
decoupled = 0.01
HIGH = lax.Precision.HIGH


def crop_image(single, offsets, flipped):
    window = lax.dynamic_slice(
        single, (offsets[0], offsets[1], jnp.int32(0)), (MAP, MAP, single.shape[2])
    )
    return jnp.where(flipped == 1, window[:, ::-1, :], window)


def patches(maps):
    count, width = maps.shape[2:]
    padded = jnp.pad(maps, ((1, 1), (1, 1), (0, 0), (0, 0)))
    taps = [padded[dy : dy + MAP, dx : dx + MAP] for dy in range(3) for dx in range(3)]
    return jnp.concatenate(taps, axis=3).reshape(MAP * MAP * count, TAPS * width)


def fold(columns, count):
    width = columns.shape[1] // TAPS
    whole = columns.reshape(MAP, MAP, count, TAPS, width)
    padded = jnp.pad(whole, ((1, 1), (1, 1), (0, 0), (0, 0), (0, 0)))
    total = 0.0
    for dy in range(3):
        for dx in range(3):
            total = total + padded[2 - dy : 2 - dy + MAP, 2 - dx : 2 - dx + MAP, :, dy * 3 + dx]
    return total.reshape(MAP * MAP * count, width)


def dot(left, right, dims):
    return lax.dot_general(
        left, right, ((dims[0], dims[1]), ((), ())), precision=HIGH, preferred_element_type=jnp.float32
    )


def adamw(weight, grad, first, second, rate):
    first = beta_first * first + (1.0 - beta_first) * grad
    second = beta_second * second + (1.0 - beta_second) * grad * grad
    first_hat = first / (1.0 - beta_first**STEP)
    second_hat = second / (1.0 - beta_second**STEP)
    update = first_hat / (jnp.sqrt(second_hat) + adam_eps) + decoupled * weight
    return (weight - rate * update, first, second)


def silu_parts(value):
    gate = jax.nn.sigmoid(value)
    slope = gate * (1.0 - gate)
    first = gate + value * slope
    second = slope * (2.0 + value * (1.0 - 2.0 * gate))
    return value * gate, first, second


class Links:
    def __init__(self):
        self.shards = lax.axis_size("shard")
        self.copies = lax.axis_size("dp")
        self.parts = 4 if self.shards % 4 == 0 else 1
        self.members = self.shards // self.parts
        index = lax.axis_index("shard")
        self.part = index // self.members
        self.member = index % self.members
        self.across = [
            [p * self.members + m for p in range(self.parts)] for m in range(self.members)
        ]
        self.within = [
            [p * self.members + m for m in range(self.members)] for p in range(self.parts)
        ]

    def sum_rows(self, value):
        value = lax.psum(value, "dp")
        gathered = lax.all_gather(value, "shard", axis_index_groups=self.within)
        return jnp.sum(gathered, axis=0)

    def sum_parts(self, value):
        return jnp.sum(lax.all_gather(value, "shard", axis_index_groups=self.across), axis=0)

    def gather_parts(self, value, axis):
        return lax.all_gather(value, "shard", axis_index_groups=self.across, axis=axis, tiled=True)

    def gather_members(self, value, axis):
        return lax.all_gather(value, "shard", axis_index_groups=self.within, axis=axis, tiled=True)

    def scatter_parts(self, value, axis):
        return lax.psum_scatter(
            value, "shard", axis_index_groups=self.across, scatter_dimension=axis, tiled=True
        )

    def to_inner(self, value):
        rows, channels = value.shape[0], value.shape[1] // TAPS
        width = channels // self.parts
        cut = value.reshape(rows, TAPS, self.parts, width).transpose(2, 0, 1, 3)
        moved = lax.all_to_all(cut, "shard", 0, 0, axis_index_groups=self.across, tiled=True)
        whole = self.gather_members(moved, 1)
        return whole.reshape(channels, TAPS * width)

    def to_outer(self, value):
        channels, width = value.shape[0], value.shape[1] // TAPS
        rows = channels // self.shards
        cut = value.reshape(self.parts, self.members, rows, TAPS * width)
        cut = lax.dynamic_index_in_dim(cut, self.member, 1, keepdims=False)
        moved = lax.all_to_all(cut, "shard", 0, 0, axis_index_groups=self.across, tiled=True)
        moved = moved.reshape(self.parts, rows, TAPS, width).transpose(1, 2, 0, 3)
        return moved.reshape(rows, TAPS * channels)

    def own_rows(self, value, axis=0):
        size = value.shape[axis] // self.members
        return lax.dynamic_slice_in_dim(value, self.member * size, size, axis)


def moments(hidden, rows, links):
    totals = links.sum_rows(jnp.stack([jnp.sum(hidden, axis=0), jnp.sum(hidden * hidden, axis=0)]))
    average = totals[0] / rows
    scale = lax.rsqrt(totals[1] / rows - average * average + norm_eps)
    return (hidden - average) * scale, scale


def moments_tangent(normal, scale, tangent, rows, links):
    totals = links.sum_rows(
        jnp.stack([jnp.sum(tangent, axis=0), jnp.sum(tangent * normal, axis=0)])
    )
    average, cross = totals[0] / rows, totals[1] / rows
    return scale * (tangent - average - normal * cross), -scale * scale * cross


def shards(
    source,
    index_map,
    crop_offsets,
    flip_flags,
    labels,
    valid_mask,
    conv_weights,
    norm_params,
    head_weights,
    decay_rates,
    conv_first,
    conv_second,
    norm_first,
    norm_second,
    head_first,
    head_second,
):
    links = Links()
    own_images = source.shape[0]
    channels = source.shape[3]
    rows = float(own_images * MAP * MAP * links.shards * links.copies)
    count = own_images * links.parts
    width = channels // links.parts
    first_column = links.part * width

    picked = source[index_map]
    images = jax.vmap(crop_image)(picked, crop_offsets, flip_flags)
    images = images.transpose(1, 2, 0, 3)
    images = links.gather_parts(images, 2)
    labels = links.gather_parts(labels, 0)
    valid = links.gather_parts(valid_mask.astype(jnp.float32), 0)
    label_total = lax.psum(jnp.sum(valid_mask.astype(jnp.float32)), ("shard", "dp"))

    kernel_one = links.gather_members(conv_weights[0], 0)
    kernel_two = links.to_inner(conv_weights[1])
    decay_one = links.gather_members(decay_rates[0], 0)
    decay_two = links.to_inner(decay_rates[1])
    norms = links.gather_members(norm_params, 1)
    head = links.gather_members(head_weights, 0)
    gain_one, shift_one, gain_two, shift_two = norms[0], norms[1], norms[2], norms[3]

    def pool(value):
        return jnp.sum(value.reshape(MAP * MAP, count, width), axis=0) / (MAP * MAP)

    def spread(value):
        whole = jnp.broadcast_to(value[None] / (MAP * MAP), (MAP * MAP, count, width))
        return whole.reshape(MAP * MAP * count, width)

    columns = patches(images)
    own_columns = lax.dynamic_slice_in_dim(
        images.reshape(MAP * MAP * count, channels), first_column, width, 1
    )

    hidden_one = dot(columns, kernel_one, ((1,), (1,)))
    normal_one, scale_one = moments(hidden_one, rows, links)
    active, slope_one, bend_one = silu_parts(normal_one * gain_one + shift_one)
    active_columns = patches(active.reshape(MAP, MAP, count, width))
    hidden_two = links.scatter_parts(dot(active_columns, kernel_two, ((1,), (1,))), 1)
    normal_two, scale_two = moments(hidden_two, rows, links)
    block, slope_two, bend_two = silu_parts(normal_two * gain_two + shift_two + own_columns)
    pooled = pool(block)
    logits = links.sum_parts(dot(pooled, head, ((1,), (0,))))
    highest = jnp.max(logits, axis=1, keepdims=True)
    powers = jnp.exp(logits - highest)
    total = jnp.sum(powers, axis=1, keepdims=True)
    chances = powers / total
    classes = jnp.arange(logits.shape[1], dtype=jnp.int32)
    chosen = (labels[:, None] == classes[None, :]).astype(jnp.float32)
    cross = highest[:, 0] + jnp.log(total[:, 0]) - jnp.sum(chosen * logits, axis=1)
    loss_sum = links.sum_rows(jnp.sum(valid * cross)[None])[0]
    weights = (valid / label_total)[:, None]
    pull_logits = weights * (chances - chosen)
    grad_head = dot(pooled, pull_logits, ((0,), (0,)))
    pull_block = spread(dot(pull_logits, head, ((1,), (1,))))
    pull_two = pull_block * slope_two
    sums_two = links.sum_rows(
        jnp.stack([jnp.sum(pull_two * normal_two, axis=0), jnp.sum(pull_two, axis=0)])
    )
    centred_two = pull_two - sums_two[1] / rows - normal_two * (sums_two[0] / rows)
    factor_two = scale_two * gain_two
    pull_hidden_two = links.gather_parts(factor_two * centred_two, 1)
    grad_two = dot(pull_hidden_two, active_columns, ((0,), (0,)))
    pull_active = fold(dot(pull_hidden_two, kernel_two, ((1,), (0,))), count)
    pull_one = pull_active * slope_one
    sums_one = links.sum_rows(
        jnp.stack([jnp.sum(pull_one * normal_one, axis=0), jnp.sum(pull_one, axis=0)])
    )
    centred_one = pull_one - sums_one[1] / rows - normal_one * (sums_one[0] / rows)
    factor_one = scale_one * gain_one
    grad_one = dot(factor_one * centred_one, columns, ((0,), (0,)))

    grad_one = links.sum_rows(grad_one) + decay_one * kernel_one
    grad_two = links.sum_rows(grad_two) + decay_two * kernel_two
    grad_head = links.sum_rows(grad_head)
    grad_norm = jnp.concatenate([sums_one, sums_two])

    def product(vector):
        move_one, move_two, move_norm, move_head = vector
        tan_hidden = dot(columns, move_one, ((1,), (1,)))
        tan_normal_one, tan_scale_one = moments_tangent(
            normal_one, scale_one, tan_hidden, rows, links
        )
        tan_inner = move_norm[0] * normal_one + gain_one * tan_normal_one + move_norm[1]
        tan_active = slope_one * tan_inner
        tan_columns = patches(tan_active.reshape(MAP, MAP, count, width))
        tan_hidden = links.scatter_parts(
            dot(tan_columns, kernel_two, ((1,), (1,))) + dot(active_columns, move_two, ((1,), (1,))),
            1,
        )
        tan_normal_two, tan_scale_two = moments_tangent(
            normal_two, scale_two, tan_hidden, rows, links
        )
        tan_outer = move_norm[2] * normal_two + gain_two * tan_normal_two + move_norm[3]
        tan_pooled = pool(slope_two * tan_outer)
        tan_logits = links.sum_parts(
            dot(tan_pooled, head, ((1,), (0,))) + dot(pooled, move_head, ((1,), (0,)))
        )
        tan_chances = chances * (tan_logits - jnp.sum(chances * tan_logits, axis=1, keepdims=True))
        tan_pull = weights * tan_chances
        out_head = dot(tan_pooled, pull_logits, ((0,), (0,))) + dot(pooled, tan_pull, ((0,), (0,)))
        tan_block = spread(
            dot(tan_pull, head, ((1,), (1,))) + dot(pull_logits, move_head, ((1,), (1,)))
        )
        tan_two = tan_block * slope_two + pull_block * bend_two * tan_outer
        tan_sums_two = links.sum_rows(
            jnp.stack(
                [
                    jnp.sum(tan_two * normal_two + pull_two * tan_normal_two, axis=0),
                    jnp.sum(tan_two, axis=0),
                ]
            )
        )
        tan_factor = tan_scale_two * gain_two + scale_two * move_norm[2]
        tan_hidden = tan_factor * centred_two + factor_two * (
            tan_two
            - tan_sums_two[1] / rows
            - tan_normal_two * (sums_two[0] / rows)
            - normal_two * (tan_sums_two[0] / rows)
        )
        tan_hidden = links.gather_parts(tan_hidden, 1)
        out_two = dot(tan_hidden, active_columns, ((0,), (0,))) + dot(
            pull_hidden_two, tan_columns, ((0,), (0,))
        )
        tan_pull_active = fold(
            dot(tan_hidden, kernel_two, ((1,), (0,))) + dot(pull_hidden_two, move_two, ((1,), (0,))),
            count,
        )
        tan_one = tan_pull_active * slope_one + pull_active * bend_one * tan_inner
        tan_sums_one = links.sum_rows(
            jnp.stack(
                [
                    jnp.sum(tan_one * normal_one + pull_one * tan_normal_one, axis=0),
                    jnp.sum(tan_one, axis=0),
                ]
            )
        )
        tan_factor = tan_scale_one * gain_one + scale_one * move_norm[0]
        tan_hidden = tan_factor * centred_one + factor_one * (
            tan_one
            - tan_sums_one[1] / rows
            - tan_normal_one * (sums_one[0] / rows)
            - normal_one * (tan_sums_one[0] / rows)
        )
        out_one = dot(tan_hidden, columns, ((0,), (0,)))
        return (
            links.sum_rows(out_one) + decay_one * move_one,
            links.sum_rows(out_two) + decay_two * move_two,
            jnp.concatenate([tan_sums_one, tan_sums_two]),
            links.sum_rows(out_head),
        )

    vector = (grad_one, grad_two, grad_norm, grad_head)
    series_one, series_two = grad_one, grad_two
    for turn in range(NEUMANN):
        change = product(vector)
        vector = tuple(
            previous - neumann_rate * moved for previous, moved in zip(vector, change)
        )
        series_one, series_two = series_one + vector[0], series_two + vector[1]

    series = jnp.stack([links.own_rows(series_one), links.to_outer(series_two)])
    hyper_gradient = -neumann_rate * conv_weights * series
    grads = jnp.stack([links.own_rows(grad_one), links.to_outer(grad_two)])
    conv_new, conv_one, conv_two = adamw(conv_weights, grads, conv_first, conv_second, 0.015)
    norm_new, norm_one, norm_two = adamw(
        norm_params, links.own_rows(grad_norm, 1), norm_first, norm_second, 0.3
    )
    head_new, head_one, head_two = adamw(
        head_weights, links.own_rows(grad_head), head_first, head_second, 0.13
    )
    return (
        loss_sum,
        label_total,
        conv_new,
        conv_one,
        conv_two,
        norm_new,
        norm_one,
        norm_two,
        head_new,
        head_one,
        head_two,
        hyper_gradient,
    )


def solution(mesh):
    images = P(("shard", "dp"))
    rows = P(None, "shard")
    head = P("shard")
    in_specs = (images,) * 6 + (rows, rows, head, rows, rows, rows, rows, rows, head, head)
    out_specs = (P(), P()) + (rows,) * 6 + (head,) * 3 + (rows,)
    return jax.shard_map(shards, mesh=mesh, in_specs=in_specs, out_specs=out_specs, check_vma=False)
```

time: 4490 us -> 2080 us (0.46)
  waiting for transfers between devices: 2920 us -> 1090 us
  blocking collectives: 1010 us -> 399 us
  matrix products: 394 us -> 211 us
  other arithmetic: 98.2 us -> 220 us
  local copies, waits for them, and re-layouts: 38.8 us -> 116 us
    reduce_scatter x4, waiting for transfers between devices: 1250 us -> 99.6 us  [scatter_parts(): lax.psum_scatter(value, 'shard', axis_index_groups=self.across, scatter_d...]
    psum x19 -> x17, blocking collectives: 676 us -> 154 us  [the longest x16 112 us: sum_rows(): value = lax.psum(value, 'dp')]
    all_gather x4 -> x17, waiting for transfers between devices: 1080 us -> 608 us  [the longest x8 368 us: sum_rows(): gathered = lax.all_gather(value, 'shard', axis_index_groups=self.within)]
    unnamed x24 -> x25, waiting for transfers between devices: 364 us -> 3.3 us
    dot_general x59 -> x48, matrix products: 393 us -> 211 us  [dot(): lax.dot_general(left, right, ((dims[0], dims[1]), ((), ())), precision=HI...]
    all_gather x8 -> x25, blocking collectives: 332 us -> 159 us  [the longest x19 94.3 us: sum_rows(): gathered = lax.all_gather(value, 'shard', axis_index_groups=self.within)]
    psum x4, waiting for transfers between devices: 221 us -> 327 us  [sum_rows(): value = lax.psum(value, 'dp')]
    reduce_sum x22 -> x54, other arithmetic: 25.1 us -> 88.1 us  [the longest x28 55.1 us: sum_rows(): return jnp.sum(gathered, axis=0)]
  transfers between devices with their start and end apart: 18 -> 27, of which waited for: 18 -> 24; matrix products, arithmetic and copies ran while one was open for 1% -> 8% of each run, Pallas kernels for 0% -> 0%
where the time goes in v1:
time: 2080 us; the launch traced here: 2060 us
  waiting for transfers between devices  1090 us (52%)
  blocking collectives  399 us (19%)
  other arithmetic  220 us (11%)
  matrix products  211 us (10%)
  local copies, waits for them, and re-layouts  116 us (6%)
    all_gather x8, waiting for transfers between devices, sum_rows(): gathered = lax.all_gather(value, 'shard', axis_index_groups=self.within)  368 us
    psum x4, waiting for transfers between devices, sum_rows(): value = lax.psum(value, 'dp')  327 us
    dot_general x48, matrix products, dot(): lax.dot_general(left, right, ((dims[0], dims[1]), ((), ())), precision=HI...  211 us
    all_gather x5, waiting for transfers between devices, gather_parts(): lax.all_gather(value, 'shard', axis_index_groups=self.across, axis=axis,...  139 us
    psum x16, blocking collectives, sum_rows(): value = lax.psum(value, 'dp')  112 us
    all_gather x4, waiting for transfers between devices, gather_members(): lax.all_gather(value, 'shard', axis_index_groups=self.within, axis=axis,...  101 us
    reduce_scatter x4, waiting for transfers between devices, scatter_parts(): lax.psum_scatter(value, 'shard', axis_index_groups=self.across, scatter_d...  99.6 us
    all_gather x19, blocking collectives, sum_rows(): gathered = lax.all_gather(value, 'shard', axis_index_groups=self.within)  94.3 us
  transfers between devices with their start and end apart: 27, of which 24 were waited for; matrix products, arithmetic and copies ran while one was open for 8% of the time, Pallas kernels for 0%

profile of v1, /device:TPU:0, one launch (start us, length us, event | category | flops | bytes accessed | tf_op | source)
XLA Modules:
  0.0 2062.4 jit_solution(4312360007437107699)
XLA Ops:
  19.6 6.3 all-to-all-start
  30.3 49.4 %all-to-all-done = f32[4,64,9,128]{3,1,2,0:T(8,128)S(1)} async-done(((f32[4,64,9,128]{3,1,2,0:T(8,128)}), f32[4,64,9,128]{3,1,2,0:T(8,128)S(1)}, u32[]{:S(2)}, u32[]{:S(2)}) %all-to-all-start) | async-done | bytes 1179680 | tf_op jit(solution)/shard_map/all_to_all | solution.py:107
  97.4 19.9 all-gather.60.cloned.1.call-done
  117.3 9.5 fusion.235
  126.9 7.0 psum.203
  140.7 14.9 all-gather.32.cloned.1.call-done
  159.8 6.1 fusion.227
  168.5 41.8 %psum.206 = f32[]{:T(128)} all-reduce(f32[]{:T(128)} %get-tuple-element.178), channel_id=1, replica_groups=mesh['shard'=8,'dp'=4] {'shard','dp'}, use_global_device_ids=true, to_apply=%region_18.19 | all-reduce | flops 1 | bytes 8 | tf_op jit(solution)/shard_map/psum | solution.py:172
  217.1 8.7 all-reduce.10
  225.7 10.1 all-reduce.9
  254.6 13.9 all-gather.8
  275.3 6.4 psum.207
  295.2 32.4 %all-gather.34.cloned.1.call-done = f32[768,512]{1,0:T(8,128)} async-done(((f32[768,128]{1,0:T(8,128)}), f32[768,512]{1,0:T(8,128)}) %all-gather.34.cloned.1.call-update) | async-done | bytes 1572880 | tf_op jit(solution)/shard_map/all_gather | solution.py:93
  335.7 7.5 psum.208
  351.2 11.7 convolution_bitcast_fusion.3
  375.5 29.4 %all_to_all.20 = f32[4,64,9,128]{3,1,2,0:T(8,128)S(1)} all-to-all(f32[4,64,9,128]{3,1,2,0:T(8,128)S(1)} %copy.79), channel_id=1, replica_groups={{0,8,16,24},{4,12,20,28},{1,9,17,25},{5,13,21,29},{2,10,18,26},{6,14,22..., dimensions={0} | all-to-all | bytes 2359296 | tf_op jit(solution)/shard_map/all_to_all | solution.py:107
  406.7 52.9 %all-reduce.31.cloned.1.call-done = (f32[1,128,4608]{2,1,0:T(8,128)}, f32[1,512,1152]{2,1,0:T(8,128)}) async-done(((f32[1,128,4608]{2,1,0:T(8,128)}, f32[1,512,1152]{2,1,0:T(8,128)}), (f32[1,128,4608]{2,1,0:T(8,128)}, f32[1,512,1152]{2,1,0:T(8,128)})) %all-reduce.31.cloned.1.call-update) | async-done | bytes 4718608 | tf_op jit(solution)/shard_map/psum | solution.py:85
  464.0 33.3 %all-gather.40.cloned.1.call-done = f32[4,128,9,128]{3,0,2,1:T(4,128)} async-done(((f32[4,64,9,128]{3,0,2,1:T(4,128)}), f32[4,128,9,128]{3,0,2,1:T(4,128)}) %all-gather.40.cloned.1.call-update) | async-done | bytes 2359312 | tf_op jit(solution)/shard_map/all_gather | solution.py:96
  501.5 60.1 %all-gather.36.cloned.1.call-done = f32[2,128,4608]{2,1,0:T(8,128)} async-done(((f32[1,128,4608]{2,1,0:T(8,128)}), f32[2,128,4608]{2,1,0:T(8,128)}) %all-gather.36.cloned.1.call-update) | async-done | bytes 4718608 | tf_op jit(solution)/shard_map/all_gather | solution.py:86
  565.9 33.4 %all-gather.62.cloned.1.call-done = f32[1,128,4608]{2,1,0:T(8,128)} async-done(((f32[1,64,4608]{2,1,0:T(8,128)}), f32[1,128,4608]{2,1,0:T(8,128)}) %all-gather.62.cloned.1.call-update) | async-done | bytes 2359312 | tf_op jit(solution)/shard_map/all_gather | solution.py:96
  602.8 10.7 fusion.233
  614.1 7.5 psum.212
  637.4 25.9 %all-gather.38.cloned.1.call-done = f32[2,512,1152]{2,1,0:T(8,128)} async-done(((f32[1,512,1152]{2,1,0:T(8,128)}), f32[2,512,1152]{2,1,0:T(8,128)}) %all-gather.38.cloned.1.call-update) | async-done | bytes 4718608 | tf_op jit(solution)/shard_map/all_gather | solution.py:86
  680.2 34.0 %reduce-scatter.7.cloned.1.call-done = f32[768,128]{1,0:T(8,128)} async-done(((f32[768,512]{1,0:T(8,128)}), f32[768,128]{1,0:T(8,128)}) %reduce-scatter.7.cloned.1.call-update) | async-done | bytes 393232 | tf_op jit(solution)/shard_map/reduce_scatter | solution.py:99
  716.0 7.3 all-reduce.15
  742.7 13.9 all-gather.9
  764.1 6.3 psum.214
  780.4 35.8 %all-gather.42.cloned.1.call-done = f32[768,512]{1,0:T(8,128)} async-done(((f32[768,128]{1,0:T(8,128)}), f32[768,512]{1,0:T(8,128)}) %all-gather.42.cloned.1.call-update) | async-done | bytes 1572880 | tf_op jit(solution)/shard_map/all_gather | solution.py:93
  832.8 8.7 fusion.46
  843.4 7.5 psum.215
  858.5 12.1 convolution_bitcast_fusion.2
  880.2 91.3 %all-reduce.29.cloned.1.call-done = (f32[1,128,4608]{2,1,0:T(8,128)}, f32[1,512,1152]{2,1,0:T(8,128)}) async-done(((f32[1,128,4608]{2,1,0:T(8,128)}, f32[1,512,1152]{2,1,0:T(8,128)}), (f32[1,128,4608]{2,1,0:T(8,128)}, f32[1,512,1152]{2,1,0:T(8,128)})) %all-reduce.29.cloned.1.call-update) | async-done | bytes 4718608 | tf_op jit(solution)/shard_map/psum | solution.py:85
  974.6 61.1 %all-gather.46.cloned.1.call-done = f32[2,512,1152]{2,1,0:T(8,128)} async-done(((f32[1,512,1152]{2,1,0:T(8,128)}), f32[2,512,1152]{2,1,0:T(8,128)}) %all-gather.46.cloned.1.call-update) | async-done | bytes 4718608 | tf_op jit(solution)/shard_map/all_gather | solution.py:86
  1040.0 6.6 fusion.7
  1046.6 53.2 %all-gather.44.cloned.1.call-done = f32[2,128,4608]{2,1,0:T(8,128)} async-done(((f32[1,128,4608]{2,1,0:T(8,128)}), f32[2,128,4608]{2,1,0:T(8,128)}) %all-gather.44.cloned.1.call-update) | async-done | bytes 4718608 | tf_op jit(solution)/shard_map/all_gather | solution.py:86
  1107.7 10.6 fusion.231
  1118.9 7.5 psum.217
  1146.9 32.8 %reduce-scatter.9.cloned.1.call-done = f32[768,128]{1,0:T(8,128)} async-done(((f32[768,512]{1,0:T(8,128)}), f32[768,128]{1,0:T(8,128)}) %reduce-scatter.9.cloned.1.call-update) | async-done | bytes 393232 | tf_op jit(solution)/shard_map/reduce_scatter | solution.py:99
  1181.5 7.3 all-reduce.14
  1209.6 13.9 all-gather.10
  1231.0 6.3 psum.221
  1247.3 35.6 %all-gather.48.cloned.1.call-done = f32[768,512]{1,0:T(8,128)} async-done(((f32[768,128]{1,0:T(8,128)}), f32[768,512]{1,0:T(8,128)}) %all-gather.48.cloned.1.call-update) | async-done | bytes 1572880 | tf_op jit(solution)/shard_map/all_gather | solution.py:93
  1299.5 8.7 fusion.53
  1310.1 7.5 psum.222
  1324.8 12.1 convolution_bitcast_fusion.1
  1346.6 91.3 %all-reduce.27.cloned.1.call-done = (f32[1,128,4608]{2,1,0:T(8,128)}, f32[1,512,1152]{2,1,0:T(8,128)}) async-done(((f32[1,128,4608]{2,1,0:T(8,128)}, f32[1,512,1152]{2,1,0:T(8,128)}), (f32[1,128,4608]{2,1,0:T(8,128)}, f32[1,512,1152]{2,1,0:T(8,128)})) %all-reduce.27.cloned.1.call-update) | async-done | bytes 4718608 | tf_op jit(solution)/shard_map/psum | solution.py:85
  1440.4 61.9 %all-gather.52.cloned.1.call-done = f32[2,512,1152]{2,1,0:T(8,128)} async-done(((f32[1,512,1152]{2,1,0:T(8,128)}), f32[2,512,1152]{2,1,0:T(8,128)}) %all-gather.52.cloned.1.call-update) | async-done | bytes 4718608 | tf_op jit(solution)/shard_map/all_gather | solution.py:86
  1506.6 6.7 fusion.10
  1513.3 53.1 %all-gather.50.cloned.1.call-done = f32[2,128,4608]{2,1,0:T(8,128)} async-done(((f32[1,128,4608]{2,1,0:T(8,128)}), f32[2,128,4608]{2,1,0:T(8,128)}) %all-gather.50.cloned.1.call-update) | async-done | bytes 4718608 | tf_op jit(solution)/shard_map/all_gather | solution.py:86
  1574.3 10.6 fusion.229
  1585.4 7.5 psum.224
  1613.7 32.8 %reduce-scatter.11.cloned.1.call-done = f32[768,128]{1,0:T(8,128)} async-done(((f32[768,512]{1,0:T(8,128)}), f32[768,128]{1,0:T(8,128)}) %reduce-scatter.11.cloned.1.call-update) | async-done | bytes 393232 | tf_op jit(solution)/shard_map/reduce_scatter | solution.py:99
  1648.3 7.3 all-reduce.13
  1675.1 13.8 all-gather.11
  1709.3 35.4 %all-gather.54.cloned.1.call-done = f32[768,512]{1,0:T(8,128)} async-done(((f32[768,128]{1,0:T(8,128)}), f32[768,512]{1,0:T(8,128)}) %all-gather.54.cloned.1.call-update) | async-done | bytes 1572880 | tf_op jit(solution)/shard_map/all_gather | solution.py:93
  1761.3 8.7 fusion.60
  1772.0 7.6 all-reduce.12
  1787.0 12.0 convolution_bitcast_fusion
  1808.7 91.3 %all-reduce.25.cloned.1.call-done = (f32[1,512,1152]{2,1,0:T(8,128)}, f32[1,128,4608]{2,1,0:T(8,128)}) async-done(((f32[1,512,1152]{2,1,0:T(8,128)}, f32[1,128,4608]{2,1,0:T(8,128)}), (f32[1,512,1152]{2,1,0:T(8,128)}, f32[1,128,4608]{2,1,0:T(8,128)})) %all-reduce.25.cloned.1.call-update) | async-done | bytes 4718608 | tf_op jit(solution)/shard_map/psum | solution.py:85
  1914.4 7.8 add_multiply_fusion
  1922.2 42.1 %all-gather.58.cloned.1.call-done = f32[2,512,1152]{2,1,0:T(8,128)} async-done(((f32[1,512,1152]{2,1,0:T(8,128)}), f32[2,512,1152]{2,1,0:T(8,128)}) %all-gather.58.cloned.1.call-update) | async-done | bytes 4718608 | tf_op jit(solution)/shard_map/all_gather | solution.py:86
  1972.3 33.2 %all_to_all.21 = f32[4,64,1152]{2,1,0:T(8,128)} all-to-all(f32[4,64,1152]{2,1,0:T(8,128)S(1)} %get-tuple-element.87), channel_id=1, replica_groups={{0,8,16,24},{4,12,20,28},{1,9,17,25},{5,13,21,29},{2,10,18,26},{6,14,22..., dimensions={0} | all-to-all | bytes 2359296 | tf_op jit(solution)/shard_map/all_to_all | solution.py:116
  2018.0 10.6 all-gather.56.cloned.1.call-done
  2048.4 7.0 multiply_subtract_fusion.3
  (608 shorter events, 525.6 us)
Async XLA Ops:
  7.2 73.6 %all-gather.30.cloned.1.call-start = ((), (), s32[]{:S(2)}) async-start(), calls=%async_computation.8 | async-start | bytes 1966080 | tf_op jit(solution)/shard_map/all_gather | solution.py:93
  15.1 102.2 %all-gather.60.cloned.1.call-start = ((), (), s32[]{:S(2)}) async-start(), calls=%async_computation.27 | async-start | bytes 3538944 | tf_op jit(solution)/shard_map/all_gather | solution.py:96
  19.6 60.1 %all-to-all-start = ((f32[4,64,9,128]{3,1,2,0:T(8,128)}), f32[4,64,9,128]{3,1,2,0:T(8,128)S(1)}, u32[]{:S(2)}, u32[]{:S(2)}) async-start(f32[4,64,9,128]{3,1,2,0:T(8,128)} %copy.75), calls=%async_computation | async-start | bytes 2359296 | tf_op jit(solution)/shard_map/all_to_all | solution.py:107
  25.9 129.7 %all-gather.32.cloned.1.call-start = ((), (), s32[]{:S(2)}) async-start(), calls=%async_computation.9 | async-start | bytes 3538944 | tf_op jit(solution)/shard_map/all_gather | solution.py:96
  30.3 108.0 %copy-start.99 = (f32[128,4]{0,1:T(4,128)}, f32[128,4]{0,1:T(4,128)S(1)}, u32[]{:S(2)}) copy-start(f32[128,4]{0,1:T(4,128)S(1)} %reshape.293) | copy-start | bytes 6148
  80.8 156.3 %reduce-scatter.5.cloned.1.call-start = ((), (), s32[]{:S(2)}) async-start(), calls=%async_computation.10 | async-start | bytes 1966080 | tf_op jit(solution)/shard_map/reduce_scatter | solution.py:99
  83.2 12.8 copy-start.5
  126.9 12.5 copy-start.6
  159.8 50.4 %copy-start.97 = (f32[64,10]{0,1:T(8,128)S(1)}, f32[64,10]{0,1:T(8,128)}, u32[]{:S(2)}) copy-start(f32[64,10]{0,1:T(8,128)} %param.24) | copy-start | bytes 7684
  165.9 161.6 %all-gather.34.cloned.1.call-start = ((), (), s32[]{:S(2)}) async-start(), calls=%async_computation.11 | async-start | bytes 1966080 | tf_op jit(solution)/shard_map/all_gather | solution.py:93
  291.9 167.7 %all-reduce.31.cloned.1.call-start = ((), (), s32[]{:S(2)}) async-start(), calls=%async_computation.32 | async-start | bytes 9437184 | tf_op jit(solution)/shard_map/psum | solution.py:85
  351.1 11.7 copy-start.102
  351.2 11.7 copy-start.104
  351.2 11.7 copy-start.15
  367.9 129.5 %all-gather.40.cloned.1.call-start = ((), (), s32[]{:S(2)}) async-start(), calls=%async_computation.14 | async-start | bytes 3538944 | tf_op jit(solution)/shard_map/all_gather | solution.py:96
  406.7 154.9 %all-gather.36.cloned.1.call-start = ((), (), s32[]{:S(2)}) async-start(), calls=%async_computation.12 | async-start | bytes 7077888 | tf_op jit(solution)/shard_map/all_gather | solution.py:86
  459.6 139.6 %all-gather.62.cloned.1.call-start = ((), (), s32[]{:S(2)}) async-start(), calls=%async_computation.28 | async-start | bytes 3538944 | tf_op jit(solution)/shard_map/all_gather | solution.py:96
  460.3 203.0 %all-gather.38.cloned.1.call-start = ((), (), s32[]{:S(2)}) async-start(), calls=%async_computation.13 | async-start | bytes 7077888 | tf_op jit(solution)/shard_map/all_gather | solution.py:86
  460.9 253.3 %reduce-scatter.7.cloned.1.call-start = ((), (), s32[]{:S(2)}) async-start(), calls=%async_computation.15 | async-start | bytes 1966080 | tf_op jit(solution)/shard_map/reduce_scatter | solution.py:99
  602.8 10.7 copy-start.26
  678.7 137.5 %all-gather.42.cloned.1.call-start = ((), (), s32[]{:S(2)}) async-start(), calls=%async_computation.16 | async-start | bytes 1966080 | tf_op jit(solution)/shard_map/all_gather | solution.py:93
  780.1 191.4 %all-reduce.29.cloned.1.call-start = ((), (), s32[]{:S(2)}) async-start(), calls=%async_computation.31 | async-start | bytes 9437184 | tf_op jit(solution)/shard_map/psum | solution.py:85
  858.5 12.1 copy-start.54
  880.1 155.6 %all-gather.46.cloned.1.call-start = ((), (), s32[]{:S(2)}) async-start(), calls=%async_computation.18 | async-start | bytes 7077888 | tf_op jit(solution)/shard_map/all_gather | solution.py:86
  971.5 128.3 %all-gather.44.cloned.1.call-start = ((), (), s32[]{:S(2)}) async-start(), calls=%async_computation.17 | async-start | bytes 7077888 | tf_op jit(solution)/shard_map/all_gather | solution.py:86
  972.1 207.6 %reduce-scatter.9.cloned.1.call-start = ((), (), s32[]{:S(2)}) async-start(), calls=%async_computation.19 | async-start | bytes 1966080 | tf_op jit(solution)/shard_map/reduce_scatter | solution.py:99
  1107.7 10.6 copy-start.28
  1144.5 138.4 %all-gather.48.cloned.1.call-start = ((), (), s32[]{:S(2)}) async-start(), calls=%async_computation.20 | async-start | bytes 1966080 | tf_op jit(solution)/shard_map/all_gather | solution.py:93
  1246.8 191.1 %all-reduce.27.cloned.1.call-start = ((), (), s32[]{:S(2)}) async-start(), calls=%async_computation.30 | async-start | bytes 9437184 | tf_op jit(solution)/shard_map/psum | solution.py:85
  1324.8 12.1 copy-start.55
  1346.5 155.7 %all-gather.52.cloned.1.call-start = ((), (), s32[]{:S(2)}) async-start(), calls=%async_computation.22 | async-start | bytes 7077888 | tf_op jit(solution)/shard_map/all_gather | solution.py:86
  1437.9 128.4 %all-gather.50.cloned.1.call-start = ((), (), s32[]{:S(2)}) async-start(), calls=%async_computation.21 | async-start | bytes 7077888 | tf_op jit(solution)/shard_map/all_gather | solution.py:86
  1438.5 207.9 %reduce-scatter.11.cloned.1.call-start = ((), (), s32[]{:S(2)}) async-start(), calls=%async_computation.23 | async-start | bytes 1966080 | tf_op jit(solution)/shard_map/reduce_scatter | solution.py:99
  1574.3 10.6 copy-start.42
  1611.2 133.5 %all-gather.54.cloned.1.call-start = ((), (), s32[]{:S(2)}) async-start(), calls=%async_computation.24 | async-start | bytes 1966080 | tf_op jit(solution)/shard_map/all_gather | solution.py:93
  1692.4 16.3 copy-start.81
  1692.4 16.3 copy-start.83
  1708.5 191.6 %all-reduce.25.cloned.1.call-start = ((), (), s32[]{:S(2)}) async-start(), calls=%async_computation.29 | async-start | bytes 9437184 | tf_op jit(solution)/shard_map/psum | solution.py:85
  1761.2 8.9 copy-start.50
  1761.2 8.9 copy-start.67
  1761.2 8.9 copy-start.78
  1761.3 8.9 copy-start.90
  1761.3 8.9 copy-start.95
  1761.3 8.9 copy-start.109
  1761.3 8.9 copy-start.111
  1761.3 8.9 copy-start.127
  1761.3 8.9 copy-start.128
  1770.1 16.9 copy-start.101
  1770.1 16.9 copy-start.103
  1787.0 12.1 copy-start.53
  1808.6 155.6 %all-gather.58.cloned.1.call-start = ((), (), s32[]{:S(2)}) async-start(), calls=%async_computation.26 | async-start | bytes 7077888 | tf_op jit(solution)/shard_map/all_gather | solution.py:86
  1900.0 128.5 %all-gather.56.cloned.1.call-start = ((), (), s32[]{:S(2)}) async-start(), calls=%async_computation.25 | async-start | bytes 7077888 | tf_op jit(solution)/shard_map/all_gather | solution.py:86
  1922.2 46.4 %copy-start.41 = (f32[4,2,64,1152]{3,2,1,0:T(8,128)S(1)}, f32[4,2,64,1152]{3,2,1,0:T(8,128)}, u32[]{:S(2)}) copy-start(f32[4,2,64,1152]{3,2,1,0:T(8,128)} %reshape.228) | copy-start | bytes 7077892
  1972.2 36.8 %copy-start.140 = (u32[32]{0:T(128)S(1)}, u32[32]{0:T(128)}, u32[]{:S(2)}) copy-start(u32[32]{0:T(128)} %constant.205) | copy-start | bytes 388
  1972.2 37.4 %copy-start.79 = (f32[128,10]{0,1:T(8,128)S(1)}, f32[128,10]{0,1:T(8,128)}, u32[]{:S(2)}) copy-start(f32[128,10]{0,1:T(8,128)} %reduce_sum.705) | copy-start | bytes 15364
  1972.3 37.4 %copy-start.98 = (f32[64,10]{0,1:T(8,128)S(1)}, f32[64,10]{0,1:T(8,128)}, u32[]{:S(2)}) copy-start(f32[64,10]{0,1:T(8,128)} %param.24) | copy-start | bytes 7684
  1972.3 37.4 %copy-start.120 = (f32[64,10]{0,1:T(8,128)S(1)}, f32[64,10]{0,1:T(8,128)}, u32[]{:S(2)}) copy-start(f32[64,10]{0,1:T(8,128)} %param.30) | copy-start | bytes 7684
  1972.3 37.4 %copy-start.121 = (f32[64,10]{0,1:T(8,128)S(1)}, f32[64,10]{0,1:T(8,128)}, u32[]{:S(2)}) copy-start(f32[64,10]{0,1:T(8,128)} %param.31) | copy-start | bytes 7684
  1972.3 39.4 %copy-start.123 = (f32[4,64]{1,0:T(4,128)S(1)}, f32[4,64]{1,0:T(4,128)}, u32[]{:S(2)}) copy-start(f32[4,64]{1,0:T(4,128)} %param.23) | copy-start | bytes 3076
  1972.3 39.4 %copy-start.124 = (f32[4,128]{1,0:T(4,128)S(1)}, f32[4,128]{1,0:T(4,128)}, u32[]{:S(2)}) copy-start(f32[4,128]{1,0:T(4,128)} %get-tuple-element.130) | copy-start | bytes 6148
  1972.3 39.4 %copy-start.134 = (f32[4,64]{1,0:T(4,128)S(1)}, f32[4,64]{1,0:T(4,128)}, u32[]{:S(2)}) copy-start(f32[4,64]{1,0:T(4,128)} %param.28) | copy-start | bytes 3076
  1972.3 39.4 %copy-start.135 = (f32[4,64]{1,0:T(4,128)S(1)}, f32[4,64]{1,0:T(4,128)}, u32[]{:S(2)}) copy-start(f32[4,64]{1,0:T(4,128)} %param.29) | copy-start | bytes 3076
  2005.5 37.4 %all-to-all-start.3 = ((f32[4,64,1152]{2,1,0:T(8,128)}), f32[4,64,1152]{2,1,0:T(8,128)S(1)}, u32[]{:S(2)}, u32[]{:S(2)}) async-start(f32[4,64,1152]{2,1,0:T(8,128)} %get-tuple-element.86), calls=%async_computation.7 | async-start | bytes 2359296 | tf_op jit(solution)/shard_map/all_to_all | solution.py:116
  2018.0 14.9 copy-start.27
  (105 other events, 451.7 us)
Sparse Core Ops, SparseCore 0:
  15.2 64.6 all-gather.29
  82.1 35.2 all-gather.59
  119.4 36.0 all-gather.31
  166.1 36.2 reduce-scatter.4
  292.0 35.5 all-gather.33
  368.0 91.5 all-reduce.30
  461.1 36.1 all-gather.39
  498.9 62.6 all-gather.35
  563.1 36.0 all-gather.61
  600.6 62.6 all-gather.37
  678.8 35.3 reduce-scatter.6
  780.2 35.8 all-gather.41
  880.2 91.2 all-reduce.28
  972.9 62.7 all-gather.45
  1037.1 62.6 all-gather.43
  1144.6 35.1 reduce-scatter.8
  1246.9 35.9 all-gather.47
  1346.7 91.2 all-reduce.26
  1439.4 62.7 all-gather.51
  1503.7 62.6 all-gather.49
  1611.4 35.0 reduce-scatter.10
  1708.6 36.0 all-gather.53
  1808.7 91.2 all-reduce.24
  1901.4 62.7 all-gather.57
  1965.8 62.7 all-gather.55

commit v2 on v1

--- a/solution.py
+++ b/solution.py
@@ -1,6 +1,10 @@
+import functools
+
 import jax
 import jax.numpy as jnp
 from jax import lax
+from jax.experimental import pallas as pl
+from jax.experimental.pallas import tpu as pltpu
 from jax.sharding import PartitionSpec as P
 
 MAP = 4
@@ -46,6 +50,903 @@
     return lax.dot_general(
         left, right, ((dims[0], dims[1]), ((), ())), precision=HIGH, preferred_element_type=jnp.float32
     )
+
+
+MESH_ID = pl.DeviceIdType.MESH
+LANES = 128
+
+
+def halves(value):
+    high = value.astype(jnp.bfloat16)
+    return high, (value - high.astype(jnp.float32)).astype(jnp.bfloat16)
+
+
+def halves_outside(value):
+    high = lax.reduce_precision(value, 8, 7)
+    return high.astype(jnp.bfloat16), (value - high).astype(jnp.bfloat16)
+
+
+def mul(left, right, dims=((1,), (0,))):
+    return lax.dot_general(left, right, (dims, ((), ())), preferred_element_type=jnp.float32)
+
+
+def mul_exact(left, right, dims=((1,), (0,))):
+    return lax.dot_general(
+        left,
+        right,
+        (dims, ((), ())),
+        precision=lax.Precision.HIGHEST,
+        preferred_element_type=jnp.float32,
+    )
+
+
+def neumann_kernel(
+    rows,
+    members,
+    copies,
+    x_hi,
+    x_lo,
+    k_hi,
+    k_lo,
+    a_hi,
+    a_lo,
+    g_hi,
+    g_lo,
+    gt_hi,
+    gt_lo,
+    v1_in,
+    v2_in,
+    decay_one,
+    decay_two,
+    move_norm_in,
+    move_head_in,
+    head,
+    n1,
+    s1,
+    pb1,
+    pull1,
+    c1,
+    n2,
+    s2,
+    pb2,
+    pull2,
+    c2,
+    pooled,
+    chances,
+    weights,
+    pull_logits,
+    channel,
+    series_one,
+    gathered_two,
+    series_two,
+    v1,
+    v2,
+    v1_hi,
+    v1_lo,
+    v2_hi,
+    v2_lo,
+    b_hi,
+    b_lo,
+    t_hi,
+    t_lo,
+    tt_hi,
+    tt_lo,
+    slots,
+    partial,
+    from_low,
+    from_high,
+    flow,
+    nt1,
+    in1,
+    nt2,
+    in2,
+    fold_sum,
+    sum_one,
+    sum_two,
+    half_one,
+    half_two,
+    piece_one,
+    piece_two,
+    stats_box,
+    stats_own,
+    logit_box,
+    logit_own,
+    turned_hi,
+    turned_lo,
+    move_norm,
+    move_head,
+    load_sem,
+    stats_send,
+    stats_recv,
+    logit_send,
+    logit_recv,
+    up_send,
+    up_recv,
+    down_send,
+    down_recv,
+    ring_send,
+    ring_recv,
+    pair_send,
+    pair_recv,
+    plane_send,
+    plane_recv,
+    back_send,
+    back_recv,
+    swap_send,
+    swap_recv,
+    last_send,
+    last_recv,
+):
+    shard = lax.axis_index("shard")
+    copy = lax.axis_index("dp")
+    part = shard // members
+    me = (shard % members) * copies + copy
+    place, core = me // 2, me % 2
+    last_part = 3
+
+    def row_peer(other):
+        return (part * members + other // copies, other % copies)
+
+    def part_peer(other):
+        return (other * members + shard % members, copy)
+
+    owns = shard == me
+
+    def owner(other):
+        return (me, other)
+
+    def holder(other):
+        return (other * members + shard // copies, shard % copies)
+
+    barrier = pltpu.get_barrier_semaphore()
+    for step in range(1, 8):
+        pl.semaphore_signal(barrier, inc=1, device_id=row_peer(me ^ step), device_id_type=MESH_ID)
+    for step in range(1, 4):
+        pl.semaphore_signal(barrier, inc=1, device_id=part_peer(part ^ step), device_id_type=MESH_ID)
+    for step in range(4):
+        target, source = owner(step), holder(step)
+
+        @pl.when(jnp.logical_not(owns))
+        def _():
+            pl.semaphore_signal(barrier, inc=1, device_id=target, device_id_type=MESH_ID)
+            pl.semaphore_signal(barrier, inc=1, device_id=source, device_id_type=MESH_ID)
+
+        @pl.when(owns & (step != copy))
+        def _():
+            pl.semaphore_signal(barrier, inc=1, device_id=target, device_id_type=MESH_ID)
+
+        @pl.when(owns & (step != part))
+        def _():
+            pl.semaphore_signal(barrier, inc=1, device_id=source, device_id_type=MESH_ID)
+
+    loads = [
+        pltpu.make_async_copy(v1_in, v1, load_sem.at[0]),
+        pltpu.make_async_copy(v2_in, v2, load_sem.at[1]),
+    ]
+    for load in loads:
+        load.start()
+    move_norm[...] = move_norm_in[...]
+    move_head[...] = move_head_in[...]
+    stats_own[...] = jnp.zeros_like(stats_own)
+    b_hi[...] = jnp.zeros_like(b_hi)
+    b_lo[...] = jnp.zeros_like(b_lo)
+    for load in loads:
+        load.wait()
+    pl.semaphore_wait(barrier, 18 - 2 * owns.astype(jnp.int32))
+
+    def remote(source, target, send, recv, device):
+        return pltpu.make_async_remote_copy(
+            src_ref=source,
+            dst_ref=target,
+            send_sem=send,
+            recv_sem=recv,
+            device_id=device,
+            device_id_type=MESH_ID,
+        )
+
+    def sum_members(site, size):
+        moves = []
+        for step in range(1, 8):
+            move = remote(
+                stats_own.at[site, pl.ds(0, size)],
+                stats_box.at[site, step, pl.ds(0, size)],
+                stats_send.at[site, step],
+                stats_recv.at[site, step],
+                row_peer(me ^ step),
+            )
+            move.start()
+            moves.append(move)
+        stats_box[site, 0, pl.ds(0, size)] = stats_own[site, pl.ds(0, size)]
+        for move in moves:
+            move.wait()
+        total = stats_box[site, me, pl.ds(0, size)]
+        for other in range(1, 8):
+            total = total + stats_box[site, other ^ me, pl.ds(0, size)]
+        return total
+
+    def each_cell(body, init=None):
+        return lax.fori_loop(0, 16, body, init)
+
+    def window(ref, tap):
+        part_of = ref[pl.ds(tap // 3, 4), pl.ds(tap % 3, 4)]
+        return part_of.reshape(16 * part_of.shape[2], part_of.shape[3])
+
+    def row(ref, index):
+        return ref[index : index + 1, :]
+
+    count = n1.shape[1]
+    zero = jnp.zeros((count, LANES), jnp.float32)
+
+    def put_sums(site, first, second):
+        stats_own[site, 0:1, :] = jnp.sum(first, axis=0, keepdims=True)
+        stats_own[site, 1:2, :] = jnp.sum(second, axis=0, keepdims=True)
+
+    series_one[...] = v1[:, place, core]
+    series_two[...] = v2[me]
+
+    def turn_body(turn, nothing):
+        def split_one(tap, _):
+            for place_of in range(4):
+                for core_of in range(2):
+                    high, low = halves(v1[tap, place_of, core_of])
+                    start = (place_of * 2 + core_of) * 16
+                    v1_hi[tap, start : start + 16] = high
+                    v1_lo[tap, start : start + 16] = low
+
+        lax.fori_loop(0, 9, split_one, None)
+
+        def split_two(block, _):
+            at = pl.ds(pl.multiple_of(block * 64, 64), 64)
+            v2_hi[at], v2_lo[at] = halves(v2[block])
+
+        lax.fori_loop(0, 8, split_two, None)
+
+        def tap_one(tap, _):
+            weight = jnp.concatenate([v1_hi[tap], v1_lo[tap]], axis=0)
+            out = mul(window(x_hi, tap), weight, ((1,), (1,)))
+            out = out[:, :LANES] + out[:, LANES:] + mul(window(x_lo, tap), v1_hi[tap], ((1,), (1,)))
+            flow[...] += out.reshape(flow.shape)
+
+        flow[...] = jnp.zeros_like(flow)
+        lax.fori_loop(0, 9, tap_one, None)
+
+        def sums_forward(normal):
+            def body(cell, carry):
+                value = flow[cell]
+                return carry[0] + value, carry[1] + value * normal[cell]
+
+            return each_cell(body, (zero, zero))
+
+        put_sums(0, *sums_forward(n1))
+        total = sum_members(0, 8) * (1.0 / rows)
+        average, cross = total[0:1], total[1:2]
+        scale, gain = row(channel, 0), row(channel, 1)
+        tan_scale_one = -scale * scale * cross
+        move_gain, move_shift = row(move_norm, 0), row(move_norm, 1)
+
+        def forward_one(cell, _):
+            normal = n1[cell]
+            tangent = scale * (flow[cell] - average - normal * cross)
+            inner = move_gain * normal + gain * tangent + move_shift
+            nt1[cell] = tangent
+            in1[cell] = inner
+            high, low = halves(s1[cell] * inner)
+            b_hi[cell // 4 + 1, cell % 4 + 1] = high
+            b_lo[cell // 4 + 1, cell % 4 + 1] = low
+
+        each_cell(forward_one)
+
+        def half_of(half, _):
+            at = pl.ds(pl.multiple_of(half * 256, 256), 256)
+
+            def tap_two(tap, _):
+                lanes = pl.ds(pl.multiple_of(tap * LANES, LANES), LANES)
+                left_hi = jnp.concatenate([window(b_hi, tap), window(a_hi, tap)], axis=1)
+                left_lo = jnp.concatenate([window(b_lo, tap), window(a_lo, tap)], axis=1)
+                right_hi = jnp.concatenate([k_hi[at, lanes], v2_hi[at, lanes]], axis=1)
+                right_lo = jnp.concatenate([k_lo[at, lanes], v2_lo[at, lanes]], axis=1)
+                out = mul(
+                    jnp.concatenate([left_hi, left_hi, left_lo], axis=1),
+                    jnp.concatenate([right_hi, right_lo, right_hi], axis=1),
+                    ((1,), (1,)),
+                )
+                partial[half * 2] += out[:, :LANES].reshape(flow.shape)
+                partial[half * 2 + 1] += out[:, LANES:].reshape(flow.shape)
+
+            lax.fori_loop(0, 9, tap_two, None)
+
+        partial[...] = jnp.zeros_like(partial)
+        lax.fori_loop(0, 2, half_of, None)
+
+        for target in (3, 2, 1):
+
+            @pl.when(part < target)
+            def _():
+                @pl.when(part > 0)
+                def _():
+                    remote(
+                        from_low.at[target],
+                        from_low.at[target],
+                        up_send.at[target],
+                        up_recv.at[target],
+                        part_peer(part - 1),
+                    ).wait_recv()
+                    partial[target] += from_low[target]
+
+                remote(
+                    partial.at[target],
+                    from_low.at[target],
+                    up_send.at[target],
+                    up_recv.at[target],
+                    part_peer(part + 1),
+                ).start()
+
+            @pl.when(part > last_part - target)
+            def _():
+                goal = last_part - target
+
+                @pl.when(part < last_part)
+                def _():
+                    remote(
+                        from_high.at[goal],
+                        from_high.at[goal],
+                        down_send.at[goal],
+                        down_recv.at[goal],
+                        part_peer(part + 1),
+                    ).wait_recv()
+                    partial[goal] += from_high[goal]
+
+                remote(
+                    partial.at[goal],
+                    from_high.at[goal],
+                    down_send.at[goal],
+                    down_recv.at[goal],
+                    part_peer(part - 1),
+                ).start()
+
+        for target in range(4):
+
+            @pl.when(part == target)
+            def _():
+                total = partial[target]
+                if target > 0:
+                    remote(
+                        from_low.at[target],
+                        from_low.at[target],
+                        up_send.at[target],
+                        up_recv.at[target],
+                        part_peer(target - 1),
+                    ).wait_recv()
+                    total = total + from_low[target]
+                if target < last_part:
+                    remote(
+                        from_high.at[target],
+                        from_high.at[target],
+                        down_send.at[target],
+                        down_recv.at[target],
+                        part_peer(target + 1),
+                    ).wait_recv()
+                    total = total + from_high[target]
+                flow[...] = total
+
+        for target in (3, 2, 1):
+
+            @pl.when(part < target)
+            def _():
+                remote(
+                    partial.at[target],
+                    from_low.at[target],
+                    up_send.at[target],
+                    up_recv.at[target],
+                    part_peer(part + 1),
+                ).wait_send()
+
+            @pl.when(part > last_part - target)
+            def _():
+                goal = last_part - target
+                remote(
+                    partial.at[goal],
+                    from_high.at[goal],
+                    down_send.at[goal],
+                    down_recv.at[goal],
+                    part_peer(part - 1),
+                ).wait_send()
+
+        put_sums(1, *sums_forward(n2))
+        total = sum_members(1, 8) * (1.0 / rows)
+        average2, cross2 = total[0:1], total[1:2]
+        scale2, gain2 = row(channel, 2), row(channel, 3)
+        tan_scale_two = -scale2 * scale2 * cross2
+        move_gain2, move_shift2 = row(move_norm, 2), row(move_norm, 3)
+
+        def forward_two(cell, carry):
+            normal = n2[cell]
+            tangent = scale2 * (flow[cell] - average2 - normal * cross2)
+            inner = move_gain2 * normal + gain2 * tangent + move_shift2
+            nt2[cell] = tangent
+            in2[cell] = inner
+            return carry + s2[cell] * inner
+
+        tan_pooled = each_cell(forward_two, zero) * (1.0 / 16.0)
+        logit_own[...] = mul_exact(tan_pooled, head[...], ((1,), (1,))) + mul_exact(
+            pooled[...], move_head[...], ((1,), (1,))
+        )
+        moves = []
+        for step in range(1, 4):
+            move = remote(
+                logit_own,
+                logit_box.at[step],
+                logit_send.at[step],
+                logit_recv.at[step],
+                part_peer(part ^ step),
+            )
+            move.start()
+            moves.append(move)
+        logit_box[0] = logit_own[...]
+        for move in moves:
+            move.wait()
+        tan_logits = logit_box[part]
+        for other in range(1, 4):
+            tan_logits = tan_logits + logit_box[other ^ part]
+        chance = chances[...]
+        tan_pull = (
+            weights[...]
+            * chance
+            * (tan_logits - jnp.sum(chance * tan_logits, axis=1, keepdims=True))
+        )
+        out_head = mul_exact(pull_logits[...], tan_pooled, ((0,), (0,))) + mul_exact(
+            tan_pull, pooled[...], ((0,), (0,))
+        )
+        tan_block = (
+            mul_exact(tan_pull, head[...]) + mul_exact(pull_logits[...], move_head[...])
+        ) * (1.0 / 16.0)
+
+        def back_two(cell, carry):
+            tangent = tan_block * s2[cell] + pb2[cell] * in2[cell]
+            flow[cell] = tangent
+            return (
+                carry[0] + tangent * n2[cell] + pull2[cell] * nt2[cell],
+                carry[1] + tangent,
+            )
+
+        put_sums(2, *each_cell(back_two, (zero, zero)))
+        stats_own[2, 8:24, :] = out_head[0:16]
+        total = sum_members(2, 24)
+        out_gain2, out_shift2 = total[0:1], total[1:2]
+        move_head_new = move_head[0:16] - neumann_rate * total[8:24]
+        factor2 = scale2 * gain2
+        tan_factor2 = tan_scale_two * gain2 + scale2 * move_gain2
+        inverse = 1.0 / rows
+
+        def pull_two_body(cell, _):
+            slots[part, cell] = tan_factor2 * c2[cell] + factor2 * (
+                flow[cell]
+                - out_shift2 * inverse
+                - nt2[cell] * row(channel, 6)
+                - n2[cell] * (out_gain2 * inverse)
+            )
+
+        each_cell(pull_two_body)
+
+        def ring_up(block):
+            return remote(
+                slots.at[block],
+                slots.at[block],
+                ring_send.at[0, part - block],
+                ring_recv.at[block],
+                part_peer(part + 1),
+            )
+
+        def ring_down(block):
+            return remote(
+                slots.at[block],
+                slots.at[block],
+                ring_send.at[1, block - part],
+                ring_recv.at[block],
+                part_peer(part - 1),
+            )
+
+        @pl.when(part < last_part)
+        def _():
+            ring_up(part).start()
+
+        @pl.when(part > 0)
+        def _():
+            ring_down(part).start()
+
+        for step in range(1, 4):
+
+            @pl.when(part >= step)
+            def _():
+                remote(
+                    slots.at[part - step],
+                    slots.at[part - step],
+                    ring_send.at[0, 0],
+                    ring_recv.at[part - step],
+                    part_peer(part - 1),
+                ).wait_recv()
+
+                @pl.when(part < last_part)
+                def _():
+                    ring_up(part - step).start()
+
+            @pl.when(part + step <= last_part)
+            def _():
+                remote(
+                    slots.at[part + step],
+                    slots.at[part + step],
+                    ring_send.at[0, 0],
+                    ring_recv.at[part + step],
+                    part_peer(part + 1),
+                ).wait_recv()
+
+                @pl.when(part > 0)
+                def _():
+                    ring_down(part + step).start()
+
+        for step in range(0, 4):
+
+            @pl.when((part >= step) & (part < last_part))
+            def _():
+                ring_up(part - step).wait_send()
+
+            @pl.when((part + step <= last_part) & (part > 0))
+            def _():
+                ring_down(part + step).wait_send()
+
+        for block in range(4):
+            at = slice(block * LANES, (block + 1) * LANES)
+            value = slots[block].reshape(16 * count, LANES)
+            t_hi[:, at], t_lo[:, at] = halves(value)
+            tt_hi[at, :], tt_lo[at, :] = halves(value.T)
+
+        fold_sum[...] = jnp.zeros_like(fold_sum)
+
+        def tap_back(tap, _):
+            lanes = pl.ds(pl.multiple_of(tap * LANES, LANES), LANES)
+            active_hi, active_lo = window(a_hi, tap), window(a_lo, tap)
+            moved_hi, moved_lo = window(b_hi, tap), window(b_lo, tap)
+            left = jnp.concatenate([tt_hi[...], gt_hi[...]], axis=1)
+            right = jnp.concatenate(
+                [
+                    jnp.concatenate([active_hi, active_lo], axis=1),
+                    jnp.concatenate([moved_hi, moved_lo], axis=1),
+                ],
+                axis=0,
+            )
+            out = mul(left, right)
+            left = jnp.concatenate([tt_lo[...], gt_lo[...]], axis=1)
+            right = jnp.concatenate([active_hi, moved_hi], axis=0)
+            out = out[:, :LANES] + out[:, LANES:] + mul(left, right)
+            sum_two[:, :, :, lanes] = out.reshape(4, 2, 64, LANES)
+            left = jnp.concatenate([t_hi[...], g_hi[...]], axis=1)
+            right = jnp.concatenate(
+                [
+                    jnp.concatenate([k_hi[:, lanes], k_lo[:, lanes]], axis=1),
+                    jnp.concatenate([v2_hi[:, lanes], v2_lo[:, lanes]], axis=1),
+                ],
+                axis=0,
+            )
+            out = mul(left, right)
+            left = jnp.concatenate([t_lo[...], g_lo[...]], axis=1)
+            right = jnp.concatenate([k_hi[:, lanes], v2_hi[:, lanes]], axis=0)
+            out = out[:, :LANES] + out[:, LANES:] + mul(left, right)
+            fold_sum[pl.ds(tap // 3, 4), pl.ds(tap % 3, 4)] += out.reshape(4, 4, count, LANES)
+
+        lax.fori_loop(0, 9, tap_back, None)
+
+        def back_one(cell, carry):
+            pull = fold_sum[cell // 4 + 1, cell % 4 + 1]
+            tangent = pull * s1[cell] + pb1[cell] * in1[cell]
+            flow[cell] = tangent
+            return (
+                carry[0] + tangent * n1[cell] + pull1[cell] * nt1[cell],
+                carry[1] + tangent,
+            )
+
+        put_sums(3, *each_cell(back_one, (zero, zero)))
+        total = sum_members(3, 8)
+        out_gain, out_shift = total[0:1], total[1:2]
+        factor = scale * gain
+        tan_factor = tan_scale_one * gain + scale * move_gain
+
+        def pull_one_body(cell, _):
+            flow[cell] = tan_factor * c1[cell] + factor * (
+                flow[cell]
+                - out_shift * inverse
+                - nt1[cell] * row(channel, 4)
+                - n1[cell] * (out_gain * inverse)
+            )
+
+        each_cell(pull_one_body)
+        turned_hi[...], turned_lo[...] = halves(flow[...].reshape(16 * count, LANES).T)
+
+        def tap_weight(tap, _):
+            left = jnp.concatenate([turned_hi[...], turned_lo[...]], axis=0)
+            out = mul(left, window(x_hi, tap))
+            out = out[:LANES] + out[LANES:] + mul(turned_hi[...], window(x_lo, tap))
+            sum_one[tap] = out.reshape(sum_one.shape[1:])
+
+        lax.fori_loop(0, 9, tap_weight, None)
+
+        pair = row_peer(me ^ 1)
+        moves = [
+            remote(
+                sum_one.at[:, :, 1 - core], half_one, pair_send.at[0], pair_recv.at[0], pair
+            ),
+            remote(sum_two.at[:, 1 - core], half_two, pair_send.at[1], pair_recv.at[1], pair),
+        ]
+        for move in moves:
+            move.start()
+        for move in moves:
+            move.wait()
+
+        def add_one(tap, _):
+            for place_of in range(4):
+                half_one[tap, place_of] += sum_one[tap, place_of, core]
+
+        lax.fori_loop(0, 9, add_one, None)
+        for place_of in range(4):
+            half_two[place_of] += sum_two[place_of, core]
+        moves = []
+        for step in range(1, 4):
+            other = place ^ step
+            device = row_peer(other * 2 + core)
+            moves.append(
+                remote(
+                    half_one.at[:, other],
+                    piece_one.at[step],
+                    plane_send.at[0, step],
+                    plane_recv.at[0, step],
+                    device,
+                )
+            )
+            moves.append(
+                remote(
+                    half_two.at[other],
+                    piece_two.at[step],
+                    plane_send.at[1, step],
+                    plane_recv.at[1, step],
+                    device,
+                )
+            )
+        for move in moves:
+            move.start()
+        for move in moves:
+            move.wait()
+
+        def step_one(tap, _):
+            change = half_one[tap, place] + piece_one[1, tap] + piece_one[2, tap] + piece_one[3, tap]
+            old = v1[tap, place, core]
+            new = old - neumann_rate * (change + decay_one[tap] * old)
+            v1[tap, place, core] = new
+            series_one[tap] += new
+
+        lax.fori_loop(0, 9, step_one, None)
+        change = half_two[place] + piece_two[1] + piece_two[2] + piece_two[3]
+        old = v2[me]
+        new = old - neumann_rate * (change + decay_two[...] * old)
+        v2[me] = new
+        series_two[...] += new
+        move_norm[0:1, :] = move_gain - neumann_rate * out_gain
+        move_norm[1:2, :] = move_shift - neumann_rate * out_shift
+        move_norm[2:3, :] = move_gain2 - neumann_rate * out_gain2
+        move_norm[3:4, :] = move_shift2 - neumann_rate * out_shift2
+        move_head[0:16, :] = move_head_new
+
+        @pl.when(turn < NEUMANN - 1)
+        def _():
+            def piece_of(which, other):
+                if which == 0:
+                    return v1.at[:, other // 2, other % 2]
+                return v2.at[other]
+
+            def to_plane(which, step):
+                return remote(
+                    piece_of(which, me),
+                    piece_of(which, me),
+                    back_send.at[which, step],
+                    back_recv.at[which, step],
+                    row_peer(me ^ (2 * step)),
+                )
+
+            def to_pair(which, step):
+                piece = piece_of(which, me ^ (2 * step))
+                return remote(
+                    piece, piece, swap_send.at[which, step], swap_recv.at[which, step], pair
+                )
+
+            for which in range(2):
+                for step in range(1, 4):
+                    to_plane(which, step).start()
+                to_pair(which, 0).start()
+            for which in range(2):
+                for step in range(1, 4):
+                    piece = piece_of(which, me ^ (2 * step))
+                    remote(
+                        piece,
+                        piece,
+                        back_send.at[which, step],
+                        back_recv.at[which, step],
+                        row_peer(me ^ (2 * step)),
+                    ).wait_recv()
+                    to_pair(which, step).start()
+            for which in range(2):
+                for step in range(1, 4):
+                    to_plane(which, step).wait_send()
+                for step in range(0, 4):
+                    to_pair(which, step).wait_send()
+                    piece = piece_of(which, me ^ 1 ^ (2 * step))
+                    remote(
+                        piece, piece, swap_send.at[which, step], swap_recv.at[which, step], pair
+                    ).wait_recv()
+
+    lax.fori_loop(0, NEUMANN, turn_body, None)
+
+    for other in range(4):
+
+        @pl.when(jnp.logical_not(owns & (copy == other)))
+        def _():
+            remote(
+                series_two,
+                gathered_two.at[part],
+                last_send.at[other],
+                last_recv.at[part],
+                owner(other),
+            ).start()
+
+    @pl.when(owns)
+    def _():
+        gathered_two[part] = series_two[...]
+
+    for other in range(4):
+
+        @pl.when(jnp.logical_not(owns & (copy == other)))
+        def _():
+            remote(
+                series_two,
+                gathered_two.at[part],
+                last_send.at[other],
+                last_recv.at[part],
+                owner(other),
+            ).wait_send()
+
+        @pl.when(jnp.logical_not(owns & (part == other)))
+        def _():
+            remote(
+                series_two,
+                gathered_two.at[other],
+                last_send.at[other],
+                last_recv.at[other],
+                owner(other),
+            ).wait_recv()
+
+
+def neumann_fused(
+    links, rows, images, kernel_two, decay, vector, head, active, pull_hidden_two, maps, small, channel
+):
+    cells, count, channels = images.shape
+    width = active.shape[1]
+    me = links.member * links.copies + lax.axis_index("dp")
+    group = links.members * links.copies
+    piece, block = width // group, channels // group
+
+    def padded(value):
+        value = value.reshape(MAP, MAP, count, value.shape[-1])
+        return halves_outside(jnp.pad(value, ((1, 1), (1, 1), (0, 0), (0, 0))))
+
+    def fill(value, shape):
+        return jnp.pad(value, [(0, new - old) for new, old in zip(shape, value.shape)])
+
+    by_tap = vector[0].reshape(width, TAPS, channels).transpose(1, 0, 2)
+    decay_one = lax.dynamic_slice_in_dim(decay[0], me * piece, piece, 0)
+    decay_one = decay_one.reshape(piece, TAPS, channels).transpose(1, 0, 2)
+    decay_two = lax.dynamic_slice_in_dim(decay[1], me * block, block, 0)
+    pull_hi, pull_lo = halves_outside(pull_hidden_two)
+    operands = (
+        *padded(images),
+        *halves_outside(kernel_two),
+        *padded(active),
+        pull_hi,
+        pull_lo,
+        pull_hi.T,
+        pull_lo.T,
+        by_tap.reshape(TAPS, 4, 2, piece, channels),
+        vector[1].reshape(group, block, TAPS * width),
+        decay_one,
+        decay_two,
+        fill(vector[2], (8, width)),
+        fill(vector[3].T, (LANES, width)),
+        fill(head.T, (LANES, width)),
+        *(value.reshape(cells, count, width) for value in maps),
+        *(fill(value, (count, LANES)) for value in small),
+        channel,
+    )
+    vmem = pl.BlockSpec(memory_space=pltpu.VMEM)
+    anywhere = pl.BlockSpec(memory_space=pl.ANY)
+    in_specs = [vmem] * len(operands)
+    in_specs[10] = in_specs[11] = anywhere
+    f32, b16 = jnp.float32, jnp.bfloat16
+    row_map = pltpu.VMEM((cells, count, width), f32)
+    dma = pltpu.SemaphoreType.DMA
+    scratch = [
+        pltpu.VMEM((block, TAPS * width), f32),
+        pltpu.VMEM((TAPS, 4, 2, piece, channels), f32),
+        pltpu.VMEM((group, block, TAPS * width), f32),
+        pltpu.VMEM((TAPS, width, channels), b16),
+        pltpu.VMEM((TAPS, width, channels), b16),
+        pltpu.VMEM((channels, TAPS * width), b16),
+        pltpu.VMEM((channels, TAPS * width), b16),
+        pltpu.VMEM((MAP + 2, MAP + 2, count, width), b16),
+        pltpu.VMEM((MAP + 2, MAP + 2, count, width), b16),
+        pltpu.VMEM((cells * count, channels), b16),
+        pltpu.VMEM((cells * count, channels), b16),
+        pltpu.VMEM((channels, cells * count), b16),
+        pltpu.VMEM((channels, cells * count), b16),
+        pltpu.VMEM((4, cells, count, width), f32),
+        pltpu.VMEM((4, cells, count, width), f32),
+        pltpu.VMEM((4, cells, count, width), f32),
+        pltpu.VMEM((4, cells, count, width), f32),
+        row_map,
+        row_map,
+        row_map,
+        row_map,
+        row_map,
+        pltpu.VMEM((MAP + 2, MAP + 2, count, width), f32),
+        pltpu.VMEM((TAPS, 4, 2, piece, channels), f32),
+        pltpu.VMEM((4, 2, block, TAPS * width), f32),
+        pltpu.VMEM((TAPS, 4, piece, channels), f32),
+        pltpu.VMEM((4, block, TAPS * width), f32),
+        pltpu.VMEM((4, TAPS, piece, channels), f32),
+        pltpu.VMEM((4, block, TAPS * width), f32),
+        pltpu.VMEM((4, 8, 24, width), f32),
+        pltpu.VMEM((4, 24, width), f32),
+        pltpu.VMEM((4, count, LANES), f32),
+        pltpu.VMEM((count, LANES), f32),
+        pltpu.VMEM((width, cells * count), b16),
+        pltpu.VMEM((width, cells * count), b16),
+        pltpu.VMEM((8, width), f32),
+        pltpu.VMEM((LANES, width), f32),
+        dma((2,)),
+        dma((4, 8)),
+        dma((4, 8)),
+        dma((4,)),
+        dma((4,)),
+        dma((4,)),
+        dma((4,)),
+        dma((4,)),
+        dma((4,)),
+        dma((2, 4)),
+        dma((4,)),
+        dma((2,)),
+        dma((2,)),
+        dma((2, 4)),
+        dma((2, 4)),
+        dma((2, 4)),
+        dma((2, 4)),
+        dma((2, 4)),
+        dma((2, 4)),
+        dma((4,)),
+        dma((4,)),
+    ]
+    series_one, series_two = pl.pallas_call(
+        functools.partial(neumann_kernel, rows, links.members, links.copies),
+        out_shape=(
+            jax.ShapeDtypeStruct((TAPS, piece, channels), f32),
+            jax.ShapeDtypeStruct((4, block, TAPS * width), f32),
+        ),
+        in_specs=in_specs,
+        out_specs=(vmem, vmem),
+        scratch_shapes=scratch,
+        compiler_params=pltpu.CompilerParams(
+            collective_id=1, has_side_effects=True, vmem_limit_bytes=63 * 1024 * 1024
+        ),
+        name="neumann",
+    )(*operands)
+    series_one = lax.all_gather(series_one, "dp").transpose(0, 2, 1, 3)
+    series_one = series_one.reshape(-1, TAPS * channels)
+    series_two = series_two.reshape(4, block, TAPS, width).transpose(1, 2, 0, 3)
+    return jnp.stack([series_one, series_two.reshape(block, TAPS * channels)])
 
 
 def adamw(weight, grad, first, second, rate):
@@ -309,16 +1210,54 @@
             links.sum_rows(out_head),
         )
 
-    vector = (grad_one, grad_two, grad_norm, grad_head)
-    series_one, series_two = grad_one, grad_two
-    for turn in range(NEUMANN):
-        change = product(vector)
-        vector = tuple(
-            previous - neumann_rate * moved for previous, moved in zip(vector, change)
-        )
-        series_one, series_two = series_one + vector[0], series_two + vector[1]
-
-    series = jnp.stack([links.own_rows(series_one), links.to_outer(series_two)])
+    if links.members * links.copies == 8 and links.parts == 4:
+        series = neumann_fused(
+            links,
+            rows,
+            images=images.reshape(MAP * MAP, count, channels),
+            kernel_two=kernel_two,
+            decay=(decay_one, decay_two),
+            vector=(grad_one, grad_two, grad_norm, grad_head),
+            head=head,
+            active=active,
+            pull_hidden_two=pull_hidden_two,
+            maps=(
+                normal_one,
+                slope_one,
+                pull_active * bend_one,
+                pull_one,
+                centred_one,
+                normal_two,
+                slope_two,
+                pull_block * bend_two,
+                pull_two,
+                centred_two,
+            ),
+            small=(pooled, chances, jnp.broadcast_to(weights, chances.shape), pull_logits),
+            channel=jnp.stack(
+                [
+                    scale_one,
+                    gain_one,
+                    scale_two,
+                    gain_two,
+                    sums_one[0] / rows,
+                    sums_one[1] / rows,
+                    sums_two[0] / rows,
+                    sums_two[1] / rows,
+                ]
+            ),
+        )
+    else:
+        vector = (grad_one, grad_two, grad_norm, grad_head)
+        series_one, series_two = grad_one, grad_two
+        for turn in range(NEUMANN):
+            change = product(vector)
+            vector = tuple(
+                previous - neumann_rate * moved for previous, moved in zip(vector, change)
+            )
+            series_one, series_two = series_one + vector[0], series_two + vector[1]
+        series = jnp.stack([links.own_rows(series_one), links.to_outer(series_two)])
+
     hyper_gradient = -neumann_rate * conv_weights * series
     grads = jnp.stack([links.own_rows(grad_one), links.to_outer(grad_two)])
     conv_new, conv_one, conv_two = adamw(conv_weights, grads, conv_first, conv_second, 0.015)

time: 2080 us -> 1350 us (0.65)
  waiting for transfers between devices: 1090 us -> 291 us
  Pallas kernels: 0 us -> 600 us
  blocking collectives: 399 us -> 174 us
  matrix products: 211 us -> 40.8 us
  other arithmetic: 220 us -> 51.9 us
  local copies, waits for them, and re-layouts: 116 us -> 142 us
    pallas_call x0 -> x1, Pallas kernels: none -> 600 us  [neumann_fused(): pl.pallas_call(functools.partial(neumann_kernel, rows, links.members, lin...]
    all_gather x8 -> x2, waiting for transfers between devices: 368 us -> 69.1 us  [sum_rows(): gathered = lax.all_gather(value, 'shard', axis_index_groups=self.within)]
    psum x4 -> x1, waiting for transfers between devices: 327 us -> 54 us  [sum_rows(): value = lax.psum(value, 'dp')]
    dot_general x48 -> x8, matrix products: 211 us -> 40.8 us  [dot(): lax.dot_general(left, right, ((dims[0], dims[1]), ((), ())), precision=HI...]
    all_gather x5 -> x2, waiting for transfers between devices: 139 us -> 31.2 us  [gather_parts(): lax.all_gather(value, 'shard', axis_index_groups=self.across, axis=axis,...]
    reduce_scatter x4 -> x1, waiting for transfers between devices: 99.6 us -> 0.02 us  [scatter_parts(): lax.psum_scatter(value, 'shard', axis_index_groups=self.across, scatter_d...]
    psum x16 -> x4, blocking collectives: 112 us -> 26.3 us  [sum_rows(): value = lax.psum(value, 'dp')]
    all_gather x19 -> x5, blocking collectives: 94.3 us -> 32.1 us  [sum_rows(): gathered = lax.all_gather(value, 'shard', axis_index_groups=self.within)]
  transfers between devices with their start and end apart: 27 -> 13, of which waited for: 24 -> 9; matrix products, arithmetic and copies ran while one was open for 8% -> 12% of each run, Pallas kernels for 0% -> 0%
where the time goes in v2:
time: 1350 us; the launch traced here: 1340 us
  Pallas kernels  600 us (44%)
  waiting for transfers between devices  291 us (22%)
  blocking collectives  174 us (13%)
  local copies, waits for them, and re-layouts  142 us (11%)
  other arithmetic  51.9 us (4%)
  matrix products  40.8 us (3%)
  starting transfers between devices  26.8 us (2%)
  between operations  15.6 us (1%)
    pallas_call x1, Pallas kernels, neumann_fused(): pl.pallas_call(functools.partial(neumann_kernel, rows, links.members, lin...  600 us
    all_gather x4, waiting for transfers between devices, gather_members(): lax.all_gather(value, 'shard', axis_index_groups=self.within, axis=axis,...  78.8 us
    all_gather x2, waiting for transfers between devices, sum_rows(): gathered = lax.all_gather(value, 'shard', axis_index_groups=self.within)  69.1 us
    psum x1, waiting for transfers between devices, sum_rows(): value = lax.psum(value, 'dp')  54 us
    all_to_all x1, waiting for transfers between devices, to_inner(): lax.all_to_all(cut, 'shard', 0, 0, axis_index_groups=self.across, tiled=T...  49.4 us
    psum x1, blocking collectives, shards(): lax.psum(jnp.sum(valid_mask.astype(jnp.float32)), ('shard', 'dp'))  42.3 us
    dot_general x8, matrix products, dot(): lax.dot_general(left, right, ((dims[0], dims[1]), ((), ())), precision=HI...  40.8 us
    all_gather x5, blocking collectives, sum_rows(): gathered = lax.all_gather(value, 'shard', axis_index_groups=self.within)  32.1 us
  transfers between devices with their start and end apart: 13, of which 9 were waited for; matrix products, arithmetic and copies ran while one was open for 12% of the time, Pallas kernels for 0%

profile of v2, /device:TPU:0, one launch (start us, length us, event | category | flops | bytes accessed | tf_op | source)
XLA Modules:
  0.0 1342.4 jit_solution(15558818898827786408)
XLA Ops:
  10.4 2.1 gather_fusion.1
  19.4 6.3 all-to-all-start
  25.7 4.3 all-gather.4
  30.1 49.4 %all-to-all-done = f32[4,64,9,128]{3,1,2,0:T(8,128)S(1)} async-done(((f32[4,64,9,128]{3,1,2,0:T(8,128)}), f32[4,64,9,128]{3,1,2,0:T(8,128)S(1)}, u32[]{:S(2)}, u32[]{:S(2)}) %all-to-all-start) | async-done | bytes 1179680 | tf_op jit(solution)/shard_map/all_to_all | solution.py:1008
  81.4 2.3 copy.268
  90.1 2.1 constant_dynamic-update-slice_fusion
  97.7 19.4 %all-gather.29.cloned.1.call-done = f32[1,128,4608]{2,1,0:T(8,128)} async-done(((f32[1,64,4608]{2,1,0:T(8,128)}), f32[1,128,4608]{2,1,0:T(8,128)}) %all-gather.29.cloned.1.call-update) | async-done | bytes 2359312 | tf_op jit(solution)/shard_map/all_gather | solution.py:997
  117.1 9.5 fusion.52
  126.9 7.0 psum.63
  133.9 14.7 %all_gather.94 = f32[2,2,128]{2,1,0:T(2,128)S(1)} all-gather(f32[1,2,128]{2,1,0:T(2,128)S(1)} %psum.63), channel_id=1, replica_groups={{0,4},{8,12},{16,20},{24,28},{1,5},{9,13},{17,21},{25,29},{2,6},{10,14}..., dimensions={0}, use_global_device_ids=true | all-gather | bytes 3072 | tf_op jit(solution)/shard_map/all_gather | solution.py:987
  155.6 2.0 copy.275
  170.2 4.3 copy.283
  174.5 7.5 fusion.49
  184.1 42.3 %psum.66 = f32[]{:T(128)} all-reduce(f32[]{:T(128)} %get-tuple-element.99), channel_id=1, replica_groups=mesh['shard'=8,'dp'=4] {'shard','dp'}, use_global_device_ids=true, to_apply=%region_18.19 | all-reduce | flops 1 | bytes 8 | tf_op jit(solution)/shard_map/psum | solution.py:1073
  226.3 4.6 all-gather.5
  231.2 7.6 all-reduce.10
  238.8 10.0 all-reduce.9
  250.2 5.8 psum.64
  256.0 4.2 all_gather.98
  260.9 2.0 multiply_add_fusion.2
  263.4 13.1 all-gather.6
  280.2 5.8 psum.67
  286.0 4.2 all_gather.106
  291.9 3.3 copy.341
  296.0 31.2 %all-gather.21.cloned.1.call-done = f32[768,512]{0,1:T(8,128)} async-done(((f32[768,128]{0,1:T(8,128)}), f32[768,512]{0,1:T(8,128)}) %all-gather.21.cloned.1.call-update) | async-done | bytes 1572880 | tf_op jit(solution)/shard_map/all_gather | solution.py:994
  329.1 5.1 fusion.61
  336.5 7.7 all-reduce.12
  344.2 4.4 all_gather.109
  349.4 10.9 convolution_bitcast_fusion
  360.2 6.7 convolution_bitcast_fusion.1
  367.1 3.2 fusion.58
  370.3 2.9 reshape_squeeze.7
  374.7 29.0 %all_to_all.15 = f32[4,64,9,128]{3,1,2,0:T(8,128)S(1)} all-to-all(f32[4,64,9,128]{3,1,2,0:T(8,128)S(1)} %copy.294), channel_id=1, replica_groups={{0,8,16,24},{4,12,20,28},{1,9,17,25},{5,13,21,29},{2,10,18,26},{6,14,22..., dimensions={0} | all-to-all | bytes 2359296 | tf_op jit(solution)/shard_map/all_to_all | solution.py:1008
  405.5 54.0 %all-reduce.16.cloned.1.call-done = (f32[1,512,1152]{2,1,0:T(8,128)}, f32[1,128,4608]{2,1,0:T(8,128)}) async-done(((f32[1,512,1152]{2,1,0:T(8,128)}, f32[1,128,4608]{2,1,0:T(8,128)}), (f32[1,512,1152]{2,1,0:T(8,128)}, f32[1,128,4608]{2,1,0:T(8,128)})) %all-reduce.16.cloned.1.call-update) | async-done | bytes 4718608 | tf_op jit(solution)/shard_map/psum | solution.py:986
  463.2 34.7 %all-gather.31.cloned.1.call-done = f32[1,128,4608]{2,1,0:T(8,128)} async-done(((f32[1,64,4608]{2,1,0:T(8,128)}), f32[1,128,4608]{2,1,0:T(8,128)}) %all-gather.31.cloned.1.call-update) | async-done | bytes 2359312 | tf_op jit(solution)/shard_map/all_gather | solution.py:997
  503.3 2.0 fusion.18
  505.4 2.3 fusion.1
  507.7 3.2 copy.300
  510.9 24.6 %all-gather.27.cloned.1.call-done = f32[4,128,9,128]{3,0,2,1:T(4,128)} async-done(((f32[4,64,9,128]{3,0,2,1:T(4,128)}), f32[4,128,9,128]{3,0,2,1:T(4,128)}) %all-gather.27.cloned.1.call-update) | async-done | bytes 2359312 | tf_op jit(solution)/shard_map/all_gather | solution.py:997
  535.5 2.7 copy_multiply_fusion
  538.3 3.6 copy.298
  541.8 4.9 mul.362
  546.7 4.7 mul.336
  551.5 2.1 copy.327
  560.6 2.0 copy.319
  572.8 4.5 all_gather.117
  581.4 18.5 %all-gather.23.cloned.1.call-done = f32[2,128,4608]{2,1,0:T(8,128)} async-done(((f32[1,128,4608]{2,1,0:T(8,128)}), f32[2,128,4608]{2,1,0:T(8,128)}) %all-gather.23.cloned.1.call-update) | async-done | bytes 4718608 | tf_op jit(solution)/shard_map/all_gather | solution.py:987
  600.0 4.3 reduce_sum.221
  604.3 3.5 fusion.4
  607.8 2.2 copy.302
  610.2 3.2 copy.303
  613.4 50.6 %all-gather.25.cloned.1.call-done = f32[2,512,1152]{2,1,0:T(8,128)} async-done(((f32[1,512,1152]{2,1,0:T(8,128)}), f32[2,512,1152]{2,1,0:T(8,128)}) %all-gather.25.cloned.1.call-update) | async-done | bytes 4718608 | tf_op jit(solution)/shard_map/all_gather | solution.py:987
  664.0 2.9 reduce_sum.222
  668.3 3.3 add.269.v2_in
  671.6 600.2 %neumann.1 = (f32[9,16,512]{2,1,0:T(8,128)}, f32[4,64,1152]{2,1,0:T(8,128)}) custom-call(bf16[6,6,48,512]{3,2,1,0:T(8,128)(2,1)} %get-tuple-element.66.x_hi, bf16[6,6,48,512]{3,2,1,0:T(8,128)(2,1)} %get-tuple-element.65.x_lo, bf16[512,1152]{1,0:T(8,128)(2,1)} %get-tuple-element.58.k_hi, bf16[512,1152]{1,0:T(8,128)(2,1)} %get-tuple-element.57.k_lo, ...), custom_call_target="tpu_custom_call" | custom-call | tf_op jit(solution)/shard_map/neumann/pallas_call | solution.py:932
  1271.9 2.9 fusion.17
  1274.8 19.7 %all-to-all-start.2 = ((f32[4,64,1152]{2,1,0:T(8,128)}), f32[4,64,1152]{2,1,0:T(8,128)S(1)}, u32[]{:S(2)}, u32[]{:S(2)}) async-start(f32[4,64,1152]{2,1,0:T(8,128)} %fusion.17), calls=%async_computation.3 | async-start | bytes 2359296 | tf_op jit(solution)/shard_map/all_to_all | solution.py:1017
  1296.4 5.2 all-reduce.11
  1305.1 3.5 copy.323
  1308.6 2.8 stack_reshape.11
  1312.5 2.0 copy.342
  1315.8 7.5 all-to-all-done.2
  1324.7 2.5 copy.299
  1328.8 6.9 multiply_subtract_fusion
  (285 shorter events, 104.7 us)
Async XLA Ops:
  7.2 74.2 %all-gather.17.cloned.1.call-start = ((), (), s32[]{:S(2)}) async-start(), calls=%async_computation.4 | async-start | bytes 1966080 | tf_op jit(solution)/shard_map/all_gather | solution.py:994
  7.9 2.5 copy-start.61
  7.9 2.5 copy-start.62
  10.4 4.5 copy-start.5
  14.9 102.2 %all-gather.29.cloned.1.call-start = ((), (), s32[]{:S(2)}) async-start(), calls=%async_computation.11 | async-start | bytes 3538944 | tf_op jit(solution)/shard_map/all_gather | solution.py:997
  18.2 7.5 copy-start.38
  19.4 60.1 %all-to-all-start = ((f32[4,64,9,128]{3,1,2,0:T(8,128)}), f32[4,64,9,128]{3,1,2,0:T(8,128)S(1)}, u32[]{:S(2)}, u32[]{:S(2)}) async-start(f32[4,64,9,128]{3,1,2,0:T(8,128)} %copy.281), calls=%async_computation | async-start | bytes 2359296 | tf_op jit(solution)/shard_map/all_to_all | solution.py:1008
  25.7 144.5 %all-gather.19.cloned.1.call-start = ((), (), s32[]{:S(2)}) async-start(), calls=%async_computation.5 | async-start | bytes 3538944 | tf_op jit(solution)/shard_map/all_gather | solution.py:997
  30.1 118.5 %copy-start.30 = (f32[128,4]{0,1:T(4,128)}, f32[128,4]{0,1:T(4,128)S(1)}, u32[]{:S(2)}) copy-start(f32[128,4]{0,1:T(4,128)S(1)} %reshape.195) | copy-start | bytes 6148
  81.3 167.7 %reduce-scatter.2.cloned.1.call-start = ((), (), s32[]{:S(2)}) async-start(), calls=%async_computation.6 | async-start | bytes 1966080 | tf_op jit(solution)/shard_map/reduce_scatter | solution.py:1000
  150.2 5.4 copy-start.11
  155.6 3.0 copy-start.20
  160.1 5.4 copy-start.19
  174.5 7.6 copy-start.65
  174.5 8.9 copy-start.60
  174.5 51.8 %copy-start.27 = (f32[64,10]{0,1:T(8,128)S(1)}, f32[64,10]{0,1:T(8,128)}, u32[]{:S(2)}) copy-start(f32[64,10]{0,1:T(8,128)} %param.24) | copy-start | bytes 7684
  174.5 56.5 %copy-start.63 = (s32[12]{0:T(128)S(1)}, s32[12]{0:T(128)}, u32[]{:S(2)}) copy-start(s32[12]{0:T(128)} %param.20) | copy-start | bytes 148
  182.0 78.9 %copy-start.50 = (f32[128]{0:T(128)S(1)}, f32[128]{0:T(128)}, u32[]{:S(2)}) copy-start(f32[128]{0:T(128)} %get-tuple-element.83) | copy-start | bytes 1540
  182.0 78.9 %copy-start.51 = (f32[128]{0:T(128)S(1)}, f32[128]{0:T(128)}, u32[]{:S(2)}) copy-start(f32[128]{0:T(128)} %get-tuple-element.84) | copy-start | bytes 1540
  182.0 145.2 %all-gather.21.cloned.1.call-start = ((), (), s32[]{:S(2)}) async-start(), calls=%async_computation.7 | async-start | bytes 1966080 | tf_op jit(solution)/shard_map/all_gather | solution.py:994
  263.3 31.9 %copy-start.25 = (f32[48,128]{1,0:T(8,128)}, f32[48,128]{1,0:T(8,128)S(1)}, u32[]{:S(2)}) copy-start(f32[48,128]{1,0:T(8,128)S(1)} %reduce_sum.208) | copy-start | bytes 73732
  278.1 13.7 %copy-start.44 = (f32[48]{0:T(128)}, f32[48]{0:T(128)S(1)}, u32[]{:S(2)}) copy-start(f32[48]{0:T(128)S(1)} %get-tuple-element.97) | copy-start | bytes 580
  278.8 16.4 %copy-start.26 = (f32[48,10]{1,0:T(8,128)}, f32[48,10]{1,0:T(8,128)S(1)}, u32[]{:S(2)}) copy-start(f32[48,10]{1,0:T(8,128)S(1)} %get-tuple-element.52) | copy-start | bytes 5764
  280.2 15.0 %copy-start.12 = (f32[768,128]{0,1:T(8,128)}, f32[768,128]{0,1:T(8,128)S(1)}, u32[]{:S(2)}) copy-start(f32[768,128]{0,1:T(8,128)S(1)} %get-tuple-element.51) | copy-start | bytes 1179652
  290.2 5.0 copy-start.31
  291.8 167.7 %all-reduce.16.cloned.1.call-start = ((), (), s32[]{:S(2)}) async-start(), calls=%async_computation.14 | async-start | bytes 9437184 | tf_op jit(solution)/shard_map/psum | solution.py:986
  336.5 12.8 copy-start.14
  349.3 10.9 copy-start.16
  349.3 10.9 copy-start.3
  367.0 130.9 %all-gather.31.cloned.1.call-start = ((), (), s32[]{:S(2)}) async-start(), calls=%async_computation.12 | async-start | bytes 3538944 | tf_op jit(solution)/shard_map/all_gather | solution.py:997
  370.3 165.2 %all-gather.27.cloned.1.call-start = ((), (), s32[]{:S(2)}) async-start(), calls=%async_computation.10 | async-start | bytes 3538944 | tf_op jit(solution)/shard_map/all_gather | solution.py:997
  405.5 194.5 %all-gather.23.cloned.1.call-start = ((), (), s32[]{:S(2)}) async-start(), calls=%async_computation.8 | async-start | bytes 7077888 | tf_op jit(solution)/shard_map/all_gather | solution.py:987
  459.6 204.5 %all-gather.25.cloned.1.call-start = ((), (), s32[]{:S(2)}) async-start(), calls=%async_computation.9 | async-start | bytes 7077888 | tf_op jit(solution)/shard_map/all_gather | solution.py:987
  460.1 852.4 %all-gather.33.cloned.1.call-start = ((), (), s32[]{:S(2)}) async-start(), calls=%async_computation.13 | async-start | bytes 1474560 | tf_op jit(solution)/shard_map/all_gather | solution.py:946
  557.3 5.3 copy-start.18
  557.3 7.6 copy-start.45
  557.3 10.6 copy-start.17
  557.3 11.5 copy-start.15
  558.2 7.3 copy-start.21
  559.6 10.0 copy-start.32
  560.6 11.3 copy-start.22
  563.5 7.5 copy-start.23
  566.5 6.3 copy-start.36
  578.2 21.8 %copy-start.7 = (bf16[768,512]{0,1:T(8,128)(2,1)}, bf16[768,512]{0,1:T(8,128)(2,1)S(1)}, u32[]{:S(2)}) copy-start(bf16[768,512]{0,1:T(8,128)(2,1)S(1)} %get-tuple-element.63) | copy-start | bytes 2359300
  578.2 21.8 %copy-start.8 = (bf16[768,512]{0,1:T(8,128)(2,1)}, bf16[768,512]{0,1:T(8,128)(2,1)S(1)}, u32[]{:S(2)}) copy-start(bf16[768,512]{0,1:T(8,128)(2,1)S(1)} %get-tuple-element.64) | copy-start | bytes 2359300
  578.2 2.6 copy-start.47
  578.2 2.6 copy-start.49
  578.2 2.6 copy-start.52
  578.2 2.6 copy-start.53
  578.2 2.5 copy-start.54
  578.2 2.5 copy-start.55
  578.2 2.5 copy-start.58
  578.3 2.5 copy-start.59
  1271.8 22.7 %copy-start.64 = (u32[32]{0:T(128)S(1)}, u32[32]{0:T(128)}, u32[]{:S(2)}) copy-start(u32[32]{0:T(128)} %constant.176) | copy-start | bytes 388
  1271.8 30.3 %copy-start.29 = (f32[4,128]{1,0:T(4,128)S(1)}, f32[4,128]{1,0:T(4,128)}, u32[]{:S(2)}) copy-start(f32[4,128]{1,0:T(4,128)} %copy-done.28) | copy-start | bytes 6148
  1271.9 30.3 %copy-start.39 = (f32[4,64]{1,0:T(4,128)S(1)}, f32[4,64]{1,0:T(4,128)}, u32[]{:S(2)}) copy-start(f32[4,64]{1,0:T(4,128)} %param.23) | copy-start | bytes 3076
  1271.9 30.3 %copy-start.56 = (f32[4,64]{1,0:T(4,128)S(1)}, f32[4,64]{1,0:T(4,128)}, u32[]{:S(2)}) copy-start(f32[4,64]{1,0:T(4,128)} %param.28) | copy-start | bytes 3076
  1271.9 30.3 %copy-start.57 = (f32[4,64]{1,0:T(4,128)S(1)}, f32[4,64]{1,0:T(4,128)}, u32[]{:S(2)}) copy-start(f32[4,64]{1,0:T(4,128)} %param.29) | copy-start | bytes 3076
  1271.9 30.9 %copy-start.34 = (f32[64,10]{0,1:T(8,128)S(1)}, f32[64,10]{0,1:T(8,128)}, u32[]{:S(2)}) copy-start(f32[64,10]{0,1:T(8,128)} %param.30) | copy-start | bytes 7684
  1271.9 30.9 %copy-start.35 = (f32[64,10]{0,1:T(8,128)S(1)}, f32[64,10]{0,1:T(8,128)}, u32[]{:S(2)}) copy-start(f32[64,10]{0,1:T(8,128)} %param.31) | copy-start | bytes 7684
  1271.9 31.6 %copy-start.24 = (f32[4,64,1152]{2,1,0:T(8,128)S(1)}, f32[4,64,1152]{2,1,0:T(8,128)}, u32[]{:S(2)}) copy-start(f32[4,64,1152]{2,1,0:T(8,128)} %get-tuple-element.15) | copy-start | bytes 3538948
  1274.8 48.4 %all-to-all-start.2 = ((f32[4,64,1152]{2,1,0:T(8,128)}), f32[4,64,1152]{2,1,0:T(8,128)S(1)}, u32[]{:S(2)}, u32[]{:S(2)}) async-start(f32[4,64,1152]{2,1,0:T(8,128)} %fusion.17), calls=%async_computation.3 | async-start | bytes 2359296 | tf_op jit(solution)/shard_map/all_to_all | solution.py:1017
  1305.1 6.3 copy-start.2
  1324.7 4.0 copy-start.6
  (15 other events, 22.5 us)
Sparse Core Ops, SparseCore 0:
  15.0 64.6 all-gather.16
  81.9 35.2 all-gather.28
  119.2 36.0 all-gather.18
  182.1 35.3 reduce-scatter.1
  292.0 35.2 all-gather.20
  367.1 92.3 all-reduce.15
  461.6 36.1 all-gather.30
  499.4 36.0 all-gather.26
  537.1 62.8 all-gather.22
  601.3 62.6 all-gather.24
  1272.0 33.8 all-gather.32

commit v3 on v1

--- a/solution.py
+++ b/solution.py
@@ -1,6 +1,10 @@
+import functools
+
 import jax
 import jax.numpy as jnp
 from jax import lax
+from jax.experimental import pallas as pl
+from jax.experimental.pallas import tpu as pltpu
 from jax.sharding import PartitionSpec as P
 
 MAP = 4
@@ -46,6 +50,1211 @@
     return lax.dot_general(
         left, right, ((dims[0], dims[1]), ((), ())), precision=HIGH, preferred_element_type=jnp.float32
     )
+
+
+MESH_ID = pl.DeviceIdType.MESH
+LANES = 128
+GROUPS = 3
+
+
+def halves(value):
+    high = value.astype(jnp.bfloat16)
+    return high, (value - high.astype(jnp.float32)).astype(jnp.bfloat16)
+
+
+def mul(left, right, dims=((1,), (0,))):
+    return lax.dot_general(left, right, (dims, ((), ())), preferred_element_type=jnp.float32)
+
+
+def mul_exact(left, right, dims=((1,), (0,))):
+    return lax.dot_general(
+        left,
+        right,
+        (dims, ((), ())),
+        precision=lax.Precision.HIGHEST,
+        preferred_element_type=jnp.float32,
+    )
+
+
+def silu_pieces(value):
+    gate = 1.0 / (1.0 + jnp.exp(-value))
+    slope = gate * (1.0 - gate)
+    return value * gate, gate + value * slope, slope * (2.0 + value * (1.0 - 2.0 * gate))
+
+
+def step_kernel(
+    rows,
+    members,
+    copies,
+    classes,
+    x_in,
+    k1_in,
+    k2_in,
+    d2_in,
+    d1,
+    pair_in,
+    label_in,
+    series_one,
+    gathered_two,
+    grad_one,
+    grad_two,
+    grad_small,
+    series_two,
+    grad_source,
+    d2,
+    v1,
+    v2,
+    v1_hi,
+    v1_lo,
+    v2_hi,
+    v2_lo,
+    k_hi,
+    k_lo,
+    x_box,
+    x_row,
+    x_both,
+    x_own,
+    a_both,
+    b_both,
+    g_left,
+    g_turned,
+    t_left,
+    t_turned,
+    slots,
+    partial,
+    from_low,
+    from_high,
+    flow,
+    n1,
+    s1,
+    pb1,
+    pull1,
+    c1,
+    n2,
+    s2,
+    pb2,
+    pull2,
+    c2,
+    nt1,
+    in1,
+    nt2,
+    in2,
+    fold_sum,
+    sum_one,
+    sum_two,
+    half_one,
+    half_two,
+    piece_one,
+    piece_two,
+    stats_box,
+    stats_own,
+    logit_box,
+    logit_own,
+    pair_box,
+    label_box,
+    turned,
+    channel,
+    move_norm,
+    move_head,
+    head,
+    pooled,
+    chances,
+    weights,
+    pull_logits,
+    load_sem,
+    k1_load,
+    k1_send,
+    k1_recv,
+    first_send,
+    first_recv,
+    label_send,
+    label_recv,
+    x_send,
+    x_recv,
+    stats_send,
+    stats_recv,
+    logit_send,
+    logit_recv,
+    up_send,
+    up_recv,
+    down_send,
+    down_recv,
+    ring_send,
+    ring_recv,
+    pair_send,
+    pair_recv,
+    plane_send,
+    plane_recv,
+    back_send,
+    back_recv,
+    swap_send,
+    swap_recv,
+    grad_send,
+    grad_recv,
+    last_send,
+    last_recv,
+):
+    shard = lax.axis_index("shard")
+    copy = lax.axis_index("dp")
+    part = shard // members
+    member = shard % members
+    me = member * copies + copy
+    place, core = me // 2, me % 2
+    last = 3
+    count = flow.shape[1]
+    own_count = x_in.shape[1]
+    inverse = 1.0 / rows
+    zero = jnp.zeros((count, LANES), jnp.float32)
+
+    def row_peer(other):
+        return (part * members + other // copies, other % copies)
+
+    def part_peer(other):
+        return (other * members + member, copy)
+
+    def owner(other):
+        return (me, other)
+
+    def holder(other):
+        return (other * members + shard // copies, shard % copies)
+
+    owns = shard == me
+
+    def remote(source, target, send, recv, device):
+        return pltpu.make_async_remote_copy(
+            src_ref=source,
+            dst_ref=target,
+            send_sem=send,
+            recv_sem=recv,
+            device_id=device,
+            device_id_type=MESH_ID,
+        )
+
+    def greet(device):
+        pl.semaphore_signal(barrier, inc=1, device_id=device, device_id_type=MESH_ID)
+
+    barrier = pltpu.get_barrier_semaphore()
+    for step in range(1, 8):
+        greet(row_peer(me ^ step))
+    for step in range(1, 4):
+        greet(part_peer(part ^ step))
+    for step in range(4):
+
+        @pl.when(jnp.logical_not(owns & (step == copy)))
+        def _():
+            greet(owner(step))
+
+        @pl.when(jnp.logical_not(owns & (step == part)))
+        def _():
+            greet(holder(step))
+
+    own_places = pl.ds(pl.multiple_of(member * 2, 2), 2)
+
+    def tap_lanes(tap, width):
+        return pl.ds(pl.multiple_of(tap * width, width), width)
+
+    channels = x_in.shape[2]
+    x_load = pltpu.make_async_copy(x_in, x_box.at[part], load_sem.at[0])
+    x_load.start()
+    k1_loads = [
+        pltpu.make_async_copy(
+            k1_in.at[:, :, :, pl.ds(tap * channels, channels)], v1.at[tap, own_places], k1_load.at[tap]
+        )
+        for tap in range(TAPS)
+    ]
+    for load in k1_loads:
+        load.start()
+    stats_own[...] = jnp.zeros_like(stats_own)
+    channel[...] = jnp.zeros_like(channel)
+    x_both[...] = jnp.zeros_like(x_both)
+    a_both[...] = jnp.zeros_like(a_both)
+    b_both[...] = jnp.zeros_like(b_both)
+    label_box[0] = label_in[...]
+    x_load.wait()
+    pl.semaphore_wait(barrier, 18 - 2 * owns.astype(jnp.int32))
+
+    def ring_move(box, send, recv, block, step, way):
+        return remote(
+            box.at[block],
+            box.at[block],
+            send.at[0 if way > 0 else 1, step],
+            recv.at[block],
+            part_peer(part + way),
+        )
+
+    def ring_start(box, send, recv):
+        @pl.when(part < last)
+        def _():
+            ring_move(box, send, recv, part, 0, 1).start()
+
+        @pl.when(part > 0)
+        def _():
+            ring_move(box, send, recv, part, 0, -1).start()
+
+    def ring_step(box, send, recv, step, use=None):
+        @pl.when(part >= step)
+        def _():
+            ring_move(box, send, recv, part - step, step, -1).wait_recv()
+
+            @pl.when(part < last)
+            def _():
+                ring_move(box, send, recv, part - step, step, 1).start()
+
+        @pl.when(part + step <= last)
+        def _():
+            ring_move(box, send, recv, part + step, step, 1).wait_recv()
+
+            @pl.when(part > 0)
+            def _():
+                ring_move(box, send, recv, part + step, step, -1).start()
+
+        if use is not None:
+
+            @pl.when(part >= step)
+            def _():
+                use(part - step)
+
+            @pl.when(part + step <= last)
+            def _():
+                use(part + step)
+
+    def ring_end(box, send, recv):
+        for step in range(0, 3):
+
+            @pl.when((part >= step) & (part < last))
+            def _():
+                ring_move(box, send, recv, part - step, step, 1).wait_send()
+
+            @pl.when((part + step <= last) & (part > 0))
+            def _():
+                ring_move(box, send, recv, part + step, step, -1).wait_send()
+
+    ring_start(x_box, x_send, x_recv)
+    partner = row_peer(me ^ copies)
+    k1_moves = [
+        remote(
+            k1_in.at[:, :, :, pl.ds(tap * channels, channels)],
+            v1.at[tap, own_places],
+            k1_send.at[tap],
+            k1_recv.at[tap],
+            partner,
+        )
+        for tap in range(TAPS)
+    ]
+    for move in k1_moves:
+        move.start()
+
+    target = holder(copy)
+    own_piece = owns & (part == copy)
+    k2_move = remote(k2_in, v2.at[shard], first_send.at[0], first_recv.at[0], target)
+    d2_move = remote(d2_in, d2, first_send.at[1], first_recv.at[1], target)
+    k2_here = pltpu.make_async_copy(k2_in, v2.at[shard], load_sem.at[1])
+    d2_here = pltpu.make_async_copy(d2_in, d2, load_sem.at[2])
+
+    @pl.when(own_piece)
+    def _():
+        k2_here.start()
+        d2_here.start()
+
+    @pl.when(jnp.logical_not(own_piece))
+    def _():
+        k2_move.start()
+        d2_move.start()
+
+    pair_move = remote(pair_in, pair_box, first_send.at[2], first_recv.at[2], partner)
+    pair_move.start()
+    label_moves = [
+        remote(
+            label_in,
+            label_box.at[step],
+            label_send.at[step],
+            label_recv.at[step],
+            part_peer(part ^ step),
+        )
+        for step in range(1, 4)
+    ]
+    for move in label_moves:
+        move.start()
+
+    pair = row_peer(me ^ 1)
+
+    def piece_of(which, other):
+        if which < GROUPS:
+            return v1.at[pl.ds(which * 3, 3), other // 2, other % 2]
+        return v2.at[other]
+
+    def to_plane(which, step):
+        piece = piece_of(which, me)
+        return remote(
+            piece, piece, back_send.at[which, step], back_recv.at[which, step], row_peer(me ^ (2 * step))
+        )
+
+    def to_pair(which, step):
+        piece = piece_of(which, me ^ (2 * step))
+        return remote(piece, piece, swap_send.at[which, step], swap_recv.at[which, step], pair)
+
+    def back_start(which):
+        for step in range(1, 4):
+            to_plane(which, step).start()
+        to_pair(which, 0).start()
+
+    def back_forward(which):
+        for step in range(1, 4):
+            piece = piece_of(which, me ^ (2 * step))
+            remote(
+                piece, piece, back_send.at[which, step], back_recv.at[which, step], pair
+            ).wait_recv()
+            to_pair(which, step).start()
+
+    def back_arrived(which):
+        for step in range(0, 4):
+            piece = piece_of(which, me ^ 1 ^ (2 * step))
+            remote(
+                piece, piece, swap_send.at[which, step], swap_recv.at[which, step], pair
+            ).wait_recv()
+
+    def back_end(which):
+        for step in range(1, 4):
+            to_plane(which, step).wait_send()
+        for step in range(0, 4):
+            to_pair(which, step).wait_send()
+
+    @pl.when(own_piece)
+    def _():
+        k2_here.wait()
+        d2_here.wait()
+
+    @pl.when(jnp.logical_not(own_piece))
+    def _():
+        k2_move.wait_send()
+        d2_move.wait_send()
+        remote(k2_in, v2.at[me], first_send.at[0], first_recv.at[0], target).wait_recv()
+        d2_move.wait_recv()
+
+    back_start(GROUPS)
+
+    pair_move.wait()
+    small = pair_in[...] + pair_box[...]
+    move_norm[...] = small[0:8]
+    head[...] = jnp.zeros_like(head)
+    move_head[...] = jnp.zeros_like(move_head)
+    head[0:16] = small[8:24]
+    for move in label_moves:
+        move.wait()
+    tags = label_box[0] + label_box[1] + label_box[2] + label_box[3]
+    chosen, valid = tags[:count], tags[count:]
+
+    def each_cell(body, init=None):
+        return lax.fori_loop(0, 16, body, init)
+
+    def window(ref, tap, lanes=slice(None)):
+        seen = ref[pl.ds(tap // 3, 4), pl.ds(tap % 3, 4), :, lanes]
+        return seen.reshape(16 * seen.shape[2], seen.shape[3])
+
+    def row(ref, index):
+        return ref[index : index + 1, :]
+
+    def put_sums(site, first, second):
+        stats_own[site, 0:1, :] = jnp.sum(first, axis=0, keepdims=True)
+        stats_own[site, 1:2, :] = jnp.sum(second, axis=0, keepdims=True)
+
+    def sum_start(site, size):
+        moves = []
+        for step in range(1, 8):
+            move = remote(
+                stats_own.at[site, pl.ds(0, size)],
+                stats_box.at[site, step, pl.ds(0, size)],
+                stats_send.at[site, step],
+                stats_recv.at[site, step],
+                row_peer(me ^ step),
+            )
+            move.start()
+            moves.append(move)
+        stats_box[site, 0, pl.ds(0, size)] = stats_own[site, pl.ds(0, size)]
+        return moves
+
+    def sum_end(site, size, moves):
+        for move in moves:
+            move.wait()
+        total = stats_box[site, me, pl.ds(0, size)]
+        for other in range(1, 8):
+            total = total + stats_box[site, other ^ me, pl.ds(0, size)]
+        return total
+
+    def sum_parts(value):
+        logit_own[...] = value
+        moves = []
+        for step in range(1, 4):
+            move = remote(
+                logit_own,
+                logit_box.at[step],
+                logit_send.at[step],
+                logit_recv.at[step],
+                part_peer(part ^ step),
+            )
+            move.start()
+            moves.append(move)
+        logit_box[0] = value
+        for move in moves:
+            move.wait()
+        total = logit_box[part]
+        for other in range(1, 4):
+            total = total + logit_box[other ^ part]
+        return total
+
+    def split_one(tap, _):
+        for place_of in range(4):
+            for core_of in range(2):
+                start = (place_of * 2 + core_of) * 16
+                v1_hi[tap, start : start + 16], v1_lo[tap, start : start + 16] = halves(
+                    v1[tap, place_of, core_of]
+                )
+
+    def split_two(high, low):
+        def body(block, _):
+            at = pl.ds(pl.multiple_of(block * 64, 64), 64)
+            high[at], low[at] = halves(v2[block])
+
+        lax.fori_loop(0, 8, body, None)
+
+    def tap_forward(tap, _):
+        weight = jnp.concatenate([v1_hi[tap], v1_lo[tap]], axis=0)
+        weight = jnp.concatenate([weight, weight], axis=1)
+        out = mul(window(x_both, tap), weight, ((1,), (1,)))
+        flow[...] += (out[:, :LANES] + out[:, LANES:]).reshape(flow.shape)
+
+    def part_of_second(maps, high, low, half):
+        at = pl.ds(pl.multiple_of(half * 256, 256), 256)
+
+        def body(tap, _):
+            lanes = tap_lanes(tap, LANES)
+            left = window(maps, tap)
+            weight_hi, weight_lo = high[at, lanes], low[at, lanes]
+            out = mul(
+                jnp.concatenate([left, left], axis=1),
+                jnp.concatenate([weight_hi, weight_hi, weight_lo, weight_lo], axis=1),
+                ((1,), (1,)),
+            )
+            partial[half * 2] += out[:, :LANES].reshape(flow.shape)
+            partial[half * 2 + 1] += out[:, LANES:].reshape(flow.shape)
+
+        lax.fori_loop(0, TAPS, body, None)
+
+    def up(block):
+        return remote(
+            partial.at[block], from_low.at[block], up_send.at[block], up_recv.at[block], part_peer(part + 1)
+        )
+
+    def down(block):
+        return remote(
+            partial.at[block],
+            from_high.at[block],
+            down_send.at[block],
+            down_recv.at[block],
+            part_peer(part - 1),
+        )
+
+    def scatter(maps, high, low, aside):
+        near = jnp.where(part < 2, 1, 0)
+        part_of_second(maps, high, low, near)
+
+        @pl.when(part == 0)
+        def _():
+            up(3).start()
+            up(2).start()
+
+        @pl.when(part == last)
+        def _():
+            down(0).start()
+            down(1).start()
+
+        part_of_second(maps, high, low, 1 - near)
+        for block in (3, 2, 1):
+            goal = last - block
+
+            @pl.when((part < block) & (part > 0))
+            def _():
+                up(block).wait_recv()
+                partial[block] += from_low[block]
+                up(block).start()
+
+            @pl.when((part > goal) & (part < last))
+            def _():
+                down(goal).wait_recv()
+                partial[goal] += from_high[goal]
+                down(goal).start()
+
+            if block == 1:
+
+                @pl.when(part == 0)
+                def _():
+                    up(1).start()
+
+                @pl.when(part == last)
+                def _():
+                    down(2).start()
+
+            aside(3 - block)
+        aside(3)
+        for block in range(4):
+
+            @pl.when(part == block)
+            def _():
+                total = partial[block]
+                if block > 0:
+                    up(block).wait_recv()
+                    total = total + from_low[block]
+                if block < last:
+                    down(block).wait_recv()
+                    total = total + from_high[block]
+                flow[...] = total
+
+        for block in (3, 2, 1):
+            goal = last - block
+
+            @pl.when(part < block)
+            def _():
+                up(block).wait_send()
+
+            @pl.when(part > goal)
+            def _():
+                down(goal).wait_send()
+
+    def turn_block(block, left, turned_block):
+        value = slots[block].reshape(16 * count, LANES)
+        left[...] = jnp.concatenate(halves(value), axis=1)
+        turned_block[...] = jnp.concatenate(halves(value.T), axis=0)
+
+    def use_block(block, left, turned_block, high, low, maps):
+        at = pl.ds(pl.multiple_of(block * LANES, LANES), LANES)
+
+        def body(tap, _):
+            lanes = tap_lanes(tap, LANES)
+            weight = jnp.concatenate([high[at, lanes], low[at, lanes]], axis=1)
+            out = mul(left[...], jnp.concatenate([weight, weight], axis=0))
+            out = out[:, :LANES] + out[:, LANES:]
+            fold_sum[pl.ds(tap // 3, 4), pl.ds(tap % 3, 4)] += out.reshape(4, 4, count, LANES)
+            out = mul(turned_block[...], window(maps, tap))
+            out = (out[:LANES, :LANES] + out[LANES:, :LANES]) + (
+                out[:LANES, LANES:] + out[LANES:, LANES:]
+            )
+            sum_two[block, :, :, lanes] += out.reshape(2, 64, LANES)
+
+        lax.fori_loop(0, TAPS, body, None)
+
+    def gather_and_use(block_of):
+        ring_start(slots, ring_send, ring_recv)
+        block_of(part)
+        for step in range(1, 4):
+            ring_step(slots, ring_send, ring_recv, step, block_of)
+        ring_end(slots, ring_send, ring_recv)
+
+    def pair_two():
+        return remote(sum_two.at[:, 1 - core], half_two, pair_send.at[GROUPS], pair_recv.at[GROUPS], pair)
+
+    def pair_one(group):
+        return remote(
+            sum_one.at[pl.ds(group * 3, 3), :, 1 - core],
+            half_one.at[pl.ds(group * 3, 3)],
+            pair_send.at[group],
+            pair_recv.at[group],
+            pair,
+        )
+
+    def plane_two(step):
+        other = place ^ step
+        return remote(
+            half_two.at[other],
+            piece_two.at[step],
+            plane_send.at[GROUPS, step],
+            plane_recv.at[GROUPS, step],
+            row_peer(other * 2 + core),
+        )
+
+    def plane_one(group, step):
+        other = place ^ step
+        return remote(
+            half_one.at[pl.ds(group * 3, 3), other],
+            piece_one.at[step, pl.ds(group * 3, 3)],
+            plane_send.at[group, step],
+            plane_recv.at[group, step],
+            row_peer(other * 2 + core),
+        )
+
+    def finish_gradients(new_of):
+        pair_two().wait()
+        for place_of in range(4):
+            half_two[place_of] += sum_two[place_of, core]
+        for step in range(1, 4):
+            plane_two(step).start()
+
+        def tap_weight(tap, _):
+            out = mul(turned[...], window(x_both, tap, slice(0, channels)))
+            out = out + mul(turned[...], window(x_both, tap, slice(channels, 2 * channels)))
+            sum_one[tap] = (out[:LANES] + out[LANES:]).reshape(sum_one.shape[1:])
+
+        def plane_go(group):
+            pair_one(group).wait()
+
+            def body(tap, _):
+                for place_of in range(4):
+                    half_one[tap, place_of] += sum_one[tap, place_of, core]
+
+            lax.fori_loop(group * 3, group * 3 + 3, body, None)
+            for step in range(1, 4):
+                plane_one(group, step).start()
+
+        for group in range(GROUPS):
+            lax.fori_loop(group * 3, group * 3 + 3, tap_weight, None)
+            pair_one(group).start()
+            if group > 0:
+                plane_go(group - 1)
+        plane_go(GROUPS - 1)
+        for step in range(1, 4):
+            plane_two(step).wait()
+        change = half_two[place] + piece_two[1] + piece_two[2] + piece_two[3]
+        new = new_of(v2[me], change, d2[...])
+        v2[me] = new
+        series_two[...] += new
+        return new
+
+    def step_group(group, new_of):
+        for step in range(1, 4):
+            plane_one(group, step).wait()
+
+        def body(tap, _):
+            change = (
+                half_one[tap, place] + piece_one[1, tap] + piece_one[2, tap] + piece_one[3, tap]
+            )
+            new = new_of(v1[tap, place, core], change, d1[tap])
+            v1[tap, place, core] = new
+            series_one[tap] += new
+
+        lax.fori_loop(group * 3, group * 3 + 3, body, None)
+
+    def no_aside(index):
+        pass
+
+    for load in k1_loads:
+        load.wait()
+    for move in k1_moves:
+        move.wait()
+    lax.fori_loop(0, TAPS, split_one, None)
+    for step in range(1, 4):
+        ring_step(x_box, x_send, x_recv, step)
+    ring_end(x_box, x_send, x_recv)
+
+    def place_images(cell, _):
+        for block in range(4):
+            x_row[block * own_count : (block + 1) * own_count] = x_box[block, cell]
+        high, low = halves(x_row[...])
+        x_both[cell // 4 + 1, cell % 4 + 1, :, 0:channels] = high
+        x_both[cell // 4 + 1, cell % 4 + 1, :, channels : 2 * channels] = low
+        x_own[cell] = x_row[:, pl.ds(pl.multiple_of(part * LANES, LANES), LANES)]
+
+    each_cell(place_images)
+    flow[...] = jnp.zeros_like(flow)
+    lax.fori_loop(0, TAPS, tap_forward, None)
+
+    def sums_primal(cell, carry):
+        value = flow[cell]
+        return carry[0] + value, carry[1] + value * value
+
+    put_sums(0, *each_cell(sums_primal, (zero, zero)))
+    stats_own[0, 2:3, :] = jnp.sum(valid, axis=0, keepdims=True)
+    moves = sum_start(0, 8)
+    back_forward(GROUPS)
+    back_arrived(GROUPS)
+    back_end(GROUPS)
+    split_two(k_hi, k_lo)
+    partial[...] = jnp.zeros_like(partial)
+    total = sum_end(0, 8, moves)
+    label_total = total[2:3]
+    average = total[0:1] * inverse
+    scale = lax.rsqrt(total[1:2] * inverse - average * average + norm_eps)
+    gain, shift = row(move_norm, 0), row(move_norm, 1)
+    gain2, shift2 = row(move_norm, 2), row(move_norm, 3)
+
+    def first_primal(cell, _):
+        normal = (flow[cell] - average) * scale
+        value, slope, bend = silu_pieces(normal * gain + shift)
+        n1[cell] = normal
+        s1[cell] = slope
+        pb1[cell] = bend
+        a_both[cell // 4 + 1, cell % 4 + 1] = jnp.concatenate(halves(value), axis=1)
+
+    each_cell(first_primal)
+    scatter(a_both, k_hi, k_lo, no_aside)
+    put_sums(1, *each_cell(sums_primal, (zero, zero)))
+    total = sum_end(1, 8, sum_start(1, 8))
+    average = total[0:1] * inverse
+    scale2 = lax.rsqrt(total[1:2] * inverse - average * average + norm_eps)
+
+    def second_primal(cell, carry):
+        normal = (flow[cell] - average) * scale2
+        value, slope, bend = silu_pieces(normal * gain2 + shift2 + x_own[cell])
+        n2[cell] = normal
+        s2[cell] = slope
+        pb2[cell] = bend
+        return carry + value
+
+    pooled[...] = each_cell(second_primal, zero) * (1.0 / 16.0)
+    logits = sum_parts(mul_exact(pooled[...], head[...], ((1,), (1,))))
+    real = lax.broadcasted_iota(jnp.int32, logits.shape, 1) < classes
+    highest = jnp.max(jnp.where(real, logits, -jnp.inf), axis=1, keepdims=True)
+    powers = jnp.where(real, jnp.exp(logits - highest), 0.0)
+    sum_powers = jnp.sum(powers, axis=1, keepdims=True)
+    chances[...] = powers / sum_powers
+    target_logit = jnp.sum(chosen * logits, axis=1, keepdims=True)
+    cross = (highest + jnp.log(sum_powers) - target_logit) * valid
+    weights[...] = valid / label_total
+    pull_logits[...] = weights[...] * (chances[...] - chosen)
+    out_head = mul_exact(pull_logits[...], pooled[...], ((0,), (0,)))
+    pull_block = mul_exact(pull_logits[...], head[...]) * (1.0 / 16.0)
+
+    def back_two_primal(cell, carry):
+        pull = pull_block * s2[cell]
+        pull2[cell] = pull
+        pb2[cell] = pull_block * pb2[cell]
+        return carry[0] + pull * n2[cell], carry[1] + pull
+
+    put_sums(2, *each_cell(back_two_primal, (zero, zero)))
+    stats_own[2, 2:3, :] = jnp.sum(cross, axis=0, keepdims=True)
+    stats_own[2, 8:24, :] = out_head[0:16]
+    total = sum_end(2, 24, sum_start(2, 24))
+    grad_small[0:1, :] = total[2:3]
+    grad_small[1:2, :] = label_total
+    grad_small[2:8, :] = jnp.zeros((6, LANES), jnp.float32)
+    grad_small[16:32, :] = total[8:24]
+    out_gain2, out_shift2 = total[0:1], total[1:2]
+    factor2 = scale2 * gain2
+
+    def pull_two_primal(cell, _):
+        centred = pull2[cell] - out_shift2 * inverse - n2[cell] * (out_gain2 * inverse)
+        c2[cell] = centred
+        slots[part, cell] = factor2 * centred
+
+    each_cell(pull_two_primal)
+    fold_sum[...] = jnp.zeros_like(fold_sum)
+    sum_two[...] = jnp.zeros_like(sum_two)
+
+    def primal_block(block):
+        turn_block(block, g_left.at[block], g_turned.at[block])
+        use_block(block, g_left.at[block], g_turned.at[block], k_hi, k_lo, a_both)
+
+    gather_and_use(primal_block)
+    pair_two().start()
+
+    def back_one_primal(cell, carry):
+        seen = fold_sum[cell // 4 + 1, cell % 4 + 1]
+        pull = seen * s1[cell]
+        pull1[cell] = pull
+        pb1[cell] = seen * pb1[cell]
+        return carry[0] + pull * n1[cell], carry[1] + pull
+
+    put_sums(3, *each_cell(back_one_primal, (zero, zero)))
+    total = sum_end(3, 8, sum_start(3, 8))
+    out_gain, out_shift = total[0:1], total[1:2]
+    factor = scale * gain
+
+    def pull_one_primal(cell, _):
+        centred = pull1[cell] - out_shift * inverse - n1[cell] * (out_gain * inverse)
+        c1[cell] = centred
+        flow[cell] = factor * centred
+
+    each_cell(pull_one_primal)
+    turned[...] = jnp.concatenate(halves(flow[...].reshape(16 * count, LANES).T), axis=0)
+
+    channel[0:1, :] = scale
+    channel[1:2, :] = gain
+    channel[2:3, :] = scale2
+    channel[3:4, :] = gain2
+    channel[4:5, :] = out_gain * inverse
+    channel[5:6, :] = out_gain2 * inverse
+    move_norm[0:1, :] = out_gain
+    move_norm[1:2, :] = out_shift
+    move_norm[2:3, :] = out_gain2
+    move_norm[3:4, :] = out_shift2
+    grad_small[8:16, :] = move_norm[...]
+    move_head[0:16] = grad_small[16:32, :]
+
+    series_one[...] = jnp.zeros_like(series_one)
+    series_two[...] = jnp.zeros_like(series_two)
+
+    def first_vector(old, change, decay):
+        return change + decay * old
+
+    def next_vector(old, change, decay):
+        return old - neumann_rate * (change + decay * old)
+
+    grad_source[...] = finish_gradients(first_vector)
+
+    def grad_move(other):
+        return remote(
+            grad_source, grad_two.at[part], grad_send.at[other], grad_recv.at[part], owner(other)
+        )
+
+    for other in range(4):
+
+        @pl.when(jnp.logical_not(owns & (copy == other)))
+        def _():
+            grad_move(other).start()
+
+    @pl.when(owns)
+    def _():
+        grad_two[part] = grad_source[...]
+
+    for group in range(GROUPS):
+        step_group(group, first_vector)
+        back_start(group)
+
+    def turn_body(turn, nothing):
+        for group in range(GROUPS):
+            back_forward(group)
+        back_start(GROUPS)
+        flow[...] = jnp.zeros_like(flow)
+        for group in range(GROUPS):
+            back_arrived(group)
+            lax.fori_loop(group * 3, group * 3 + 3, split_one, None)
+            lax.fori_loop(group * 3, group * 3 + 3, tap_forward, None)
+        for group in range(GROUPS):
+            back_end(group)
+
+        @pl.when(turn == 0)
+        def _():
+            grad_one[...] = v1[:, own_places]
+
+        def sums_forward(normal):
+            def body(cell, carry):
+                value = flow[cell]
+                return carry[0] + value, carry[1] + value * normal[cell]
+
+            return each_cell(body, (zero, zero))
+
+        put_sums(0, *sums_forward(n1))
+        moves = sum_start(0, 8)
+        back_forward(GROUPS)
+        partial[...] = jnp.zeros_like(partial)
+        fold_sum[...] = jnp.zeros_like(fold_sum)
+        sum_two[...] = jnp.zeros_like(sum_two)
+        back_arrived(GROUPS)
+        back_end(GROUPS)
+        split_two(v2_hi, v2_lo)
+        part_of_second(a_both, v2_hi, v2_lo, 0)
+        part_of_second(a_both, v2_hi, v2_lo, 1)
+        total = sum_end(0, 8, moves) * inverse
+        average, cross = total[0:1], total[1:2]
+        scale, gain = row(channel, 0), row(channel, 1)
+        tan_scale_one = -scale * scale * cross
+        move_gain, move_shift = row(move_norm, 0), row(move_norm, 1)
+
+        def forward_one(cell, _):
+            normal = n1[cell]
+            tangent = scale * (flow[cell] - average - normal * cross)
+            inner = move_gain * normal + gain * tangent + move_shift
+            nt1[cell] = tangent
+            in1[cell] = inner
+            b_both[cell // 4 + 1, cell % 4 + 1] = jnp.concatenate(halves(s1[cell] * inner), axis=1)
+
+        each_cell(forward_one)
+
+        def aside(block):
+            use_block(block, g_left.at[block], g_turned.at[block], v2_hi, v2_lo, b_both)
+
+        scatter(b_both, k_hi, k_lo, aside)
+
+        put_sums(1, *sums_forward(n2))
+        total = sum_end(1, 8, sum_start(1, 8)) * inverse
+        average2, cross2 = total[0:1], total[1:2]
+        scale2, gain2 = row(channel, 2), row(channel, 3)
+        tan_scale_two = -scale2 * scale2 * cross2
+        move_gain2, move_shift2 = row(move_norm, 2), row(move_norm, 3)
+
+        def forward_two(cell, carry):
+            normal = n2[cell]
+            tangent = scale2 * (flow[cell] - average2 - normal * cross2)
+            inner = move_gain2 * normal + gain2 * tangent + move_shift2
+            nt2[cell] = tangent
+            in2[cell] = inner
+            return carry + s2[cell] * inner
+
+        tan_pooled = each_cell(forward_two, zero) * (1.0 / 16.0)
+        tan_logits = sum_parts(
+            mul_exact(tan_pooled, head[...], ((1,), (1,)))
+            + mul_exact(pooled[...], move_head[...], ((1,), (1,)))
+        )
+        chance = chances[...]
+        tan_pull = (
+            weights[...]
+            * chance
+            * (tan_logits - jnp.sum(chance * tan_logits, axis=1, keepdims=True))
+        )
+        out_head = mul_exact(pull_logits[...], tan_pooled, ((0,), (0,))) + mul_exact(
+            tan_pull, pooled[...], ((0,), (0,))
+        )
+        tan_block = (
+            mul_exact(tan_pull, head[...]) + mul_exact(pull_logits[...], move_head[...])
+        ) * (1.0 / 16.0)
+
+        def back_two(cell, carry):
+            tangent = tan_block * s2[cell] + pb2[cell] * in2[cell]
+            flow[cell] = tangent
+            return (
+                carry[0] + tangent * n2[cell] + pull2[cell] * nt2[cell],
+                carry[1] + tangent,
+            )
+
+        put_sums(2, *each_cell(back_two, (zero, zero)))
+        stats_own[2, 8:24, :] = out_head[0:16]
+        total = sum_end(2, 24, sum_start(2, 24))
+        out_gain2, out_shift2 = total[0:1], total[1:2]
+        move_head[0:16] = move_head[0:16] - neumann_rate * total[8:24]
+        factor2 = scale2 * gain2
+        tan_factor2 = tan_scale_two * gain2 + scale2 * move_gain2
+
+        def pull_two_body(cell, _):
+            slots[part, cell] = tan_factor2 * c2[cell] + factor2 * (
+                flow[cell]
+                - out_shift2 * inverse
+                - nt2[cell] * row(channel, 5)
+                - n2[cell] * (out_gain2 * inverse)
+            )
+
+        each_cell(pull_two_body)
+
+        def turn_of_block(block):
+            turn_block(block, t_left, t_turned)
+            use_block(block, t_left, t_turned, k_hi, k_lo, a_both)
+
+        gather_and_use(turn_of_block)
+        pair_two().start()
+
+        def back_one(cell, carry):
+            pull = fold_sum[cell // 4 + 1, cell % 4 + 1]
+            tangent = pull * s1[cell] + pb1[cell] * in1[cell]
+            flow[cell] = tangent
+            return (
+                carry[0] + tangent * n1[cell] + pull1[cell] * nt1[cell],
+                carry[1] + tangent,
+            )
+
+        put_sums(3, *each_cell(back_one, (zero, zero)))
+        total = sum_end(3, 8, sum_start(3, 8))
+        out_gain, out_shift = total[0:1], total[1:2]
+        factor = scale * gain
+        tan_factor = tan_scale_one * gain + scale * move_gain
+
+        def pull_one_body(cell, _):
+            flow[cell] = tan_factor * c1[cell] + factor * (
+                flow[cell]
+                - out_shift * inverse
+                - nt1[cell] * row(channel, 4)
+                - n1[cell] * (out_gain * inverse)
+            )
+
+        each_cell(pull_one_body)
+        turned[...] = jnp.concatenate(halves(flow[...].reshape(16 * count, LANES).T), axis=0)
+        move_norm[0:1, :] = move_gain - neumann_rate * out_gain
+        move_norm[1:2, :] = move_shift - neumann_rate * out_shift
+        move_norm[2:3, :] = move_gain2 - neumann_rate * out_gain2
+        move_norm[3:4, :] = move_shift2 - neumann_rate * out_shift2
+        finish_gradients(next_vector)
+        for group in range(GROUPS):
+            step_group(group, next_vector)
+
+            @pl.when(turn < NEUMANN - 1)
+            def _():
+                back_start(group)
+
+    lax.fori_loop(0, NEUMANN, turn_body, None)
+
+    def last_move(other):
+        return remote(
+            series_two, gathered_two.at[part], last_send.at[other], last_recv.at[part], owner(other)
+        )
+
+    for other in range(4):
+
+        @pl.when(jnp.logical_not(owns & (copy == other)))
+        def _():
+            last_move(other).start()
+
+    @pl.when(owns)
+    def _():
+        gathered_two[part] = series_two[...]
+
+    for other in range(4):
+
+        @pl.when(jnp.logical_not(owns & (copy == other)))
+        def _():
+            grad_move(other).wait_send()
+            last_move(other).wait_send()
+
+        @pl.when(jnp.logical_not(owns & (part == other)))
+        def _():
+            for box, send, recv in ((grad_two, grad_send, grad_recv), (gathered_two, last_send, last_recv)):
+                remote(
+                    series_two, box.at[other], send.at[other], recv.at[other], owner(other)
+                ).wait_recv()
+
+
+def step_fused(links, rows, images, conv_weights, decay_rates, norm_params, head_weights, labels, valid):
+    own_count, channels = images.shape[2:]
+    cells, count = MAP * MAP, own_count * 4
+    width, group = channels // 4, 8
+    piece, block = width // group, channels // group
+    classes = head_weights.shape[1]
+    copy = lax.axis_index("dp")
+    f32, b16 = jnp.float32, jnp.bfloat16
+
+    def inner(value):
+        cut = value.reshape(block, TAPS, 4, width)
+        return lax.dynamic_index_in_dim(cut, copy, 2, keepdims=False).reshape(block, TAPS * width)
+
+    d1 = lax.dynamic_slice_in_dim(decay_rates[0], copy * piece, piece, 0)
+    d1 = d1.reshape(piece, TAPS, channels).transpose(1, 0, 2)
+    small = jnp.zeros((24, width), f32)
+    lane = links.member * block
+    small = lax.dynamic_update_slice(small, norm_params, (0, lane))
+    small = lax.dynamic_update_slice(small, head_weights.T, (8, lane))
+    chosen = (labels[:, None] == jnp.arange(LANES, dtype=jnp.int32)[None, :]).astype(f32)
+    tags = jnp.zeros((2, count, LANES), f32)
+    tags = lax.dynamic_update_slice(
+        tags,
+        jnp.stack([chosen, jnp.broadcast_to(valid[:, None], chosen.shape)]),
+        (0, links.part * own_count, 0),
+    )
+    operands = (
+        images.reshape(cells, own_count, channels),
+        conv_weights[0].reshape(2, 2, piece, TAPS * channels),
+        inner(conv_weights[1]),
+        inner(decay_rates[1]),
+        d1,
+        small,
+        tags.reshape(2 * count, LANES),
+    )
+    vmem = pl.BlockSpec(memory_space=pltpu.VMEM)
+    anywhere = pl.BlockSpec(memory_space=pl.ANY)
+    row_map = pltpu.VMEM((cells, count, width), f32)
+    four_maps = pltpu.VMEM((4, cells, count, width), f32)
+    whole_one = pltpu.VMEM((TAPS, 4, 2, piece, channels), f32)
+    inner_piece = pltpu.VMEM((block, TAPS * width), f32)
+    inner_half = pltpu.VMEM((4, block, TAPS * width), f32)
+    inner_part = pltpu.VMEM((channels, TAPS * width), b16)
+    outer_part = pltpu.VMEM((TAPS, width, channels), b16)
+    both = pltpu.VMEM((MAP + 2, MAP + 2, count, 2 * width), b16)
+    logit = pltpu.VMEM((count, LANES), f32)
+    dma = pltpu.SemaphoreType.DMA
+    scratch = [
+        inner_piece,
+        inner_piece,
+        inner_piece,
+        whole_one,
+        pltpu.VMEM((group, block, TAPS * width), f32),
+        outer_part,
+        outer_part,
+        inner_part,
+        inner_part,
+        inner_part,
+        inner_part,
+        pltpu.VMEM((4, cells, own_count, channels), f32),
+        pltpu.VMEM((count, channels), f32),
+        pltpu.VMEM((MAP + 2, MAP + 2, count, 2 * channels), b16),
+        row_map,
+        both,
+        both,
+        pltpu.VMEM((4, cells * count, 2 * width), b16),
+        pltpu.VMEM((4, 2 * width, cells * count), b16),
+        pltpu.VMEM((cells * count, 2 * width), b16),
+        pltpu.VMEM((2 * width, cells * count), b16),
+        four_maps,
+        four_maps,
+        four_maps,
+        four_maps,
+        *[row_map] * 15,
+        pltpu.VMEM((MAP + 2, MAP + 2, count, width), f32),
+        whole_one,
+        pltpu.VMEM((4, 2, block, TAPS * width), f32),
+        pltpu.VMEM((TAPS, 4, piece, channels), f32),
+        inner_half,
+        pltpu.VMEM((4, TAPS, piece, channels), f32),
+        inner_half,
+        pltpu.VMEM((4, 8, 24, width), f32),
+        pltpu.VMEM((4, 24, width), f32),
+        pltpu.VMEM((4, count, LANES), f32),
+        logit,
+        pltpu.VMEM((24, width), f32),
+        pltpu.VMEM((4, 2 * count, LANES), f32),
+        pltpu.VMEM((2 * width, cells * count), b16),
+        pltpu.VMEM((8, width), f32),
+        pltpu.VMEM((8, width), f32),
+        pltpu.VMEM((LANES, width), f32),
+        pltpu.VMEM((LANES, width), f32),
+        logit,
+        logit,
+        logit,
+        logit,
+        dma((3,)),
+        dma((TAPS,)),
+        dma((TAPS,)),
+        dma((TAPS,)),
+        dma((3,)),
+        dma((3,)),
+        dma((4,)),
+        dma((4,)),
+        dma((2, 4)),
+        dma((4,)),
+        dma((4, 8)),
+        dma((4, 8)),
+        dma((4,)),
+        dma((4,)),
+        dma((4,)),
+        dma((4,)),
+        dma((4,)),
+        dma((4,)),
+        dma((2, 4)),
+        dma((4,)),
+        dma((GROUPS + 1,)),
+        dma((GROUPS + 1,)),
+        dma((GROUPS + 1, 4)),
+        dma((GROUPS + 1, 4)),
+        dma((GROUPS + 1, 4)),
+        dma((GROUPS + 1, 4)),
+        dma((GROUPS + 1, 4)),
+        dma((GROUPS + 1, 4)),
+        dma((4,)),
+        dma((4,)),
+        dma((4,)),
+        dma((4,)),
+    ]
+    series_one, series_two, grad_one, grad_two, grad_small = pl.pallas_call(
+        functools.partial(step_kernel, rows, links.members, links.copies, classes),
+        out_shape=(
+            jax.ShapeDtypeStruct((TAPS, piece, channels), f32),
+            jax.ShapeDtypeStruct((4, block, TAPS * width), f32),
+            jax.ShapeDtypeStruct((TAPS, 2, 2, piece, channels), f32),
+            jax.ShapeDtypeStruct((4, block, TAPS * width), f32),
+            jax.ShapeDtypeStruct((32, width), f32),
+        ),
+        in_specs=[anywhere] * 4 + [vmem] * 3,
+        out_specs=(vmem,) * 5,
+        scratch_shapes=scratch,
+        compiler_params=pltpu.CompilerParams(
+            collective_id=1, has_side_effects=True, vmem_limit_bytes=63 * 1024 * 1024
+        ),
+        name="train_step",
+    )(*operands)
+
+    def outer(value):
+        value = value.reshape(4, block, TAPS, width).transpose(1, 2, 0, 3)
+        return value.reshape(block, TAPS * channels)
+
+    series_one = lax.all_gather(series_one, "dp").transpose(0, 2, 1, 3)
+    series = jnp.stack([series_one.reshape(block, TAPS * channels), outer(series_two)])
+    grad_one = grad_one.reshape(TAPS, block, channels).transpose(1, 0, 2)
+    grads = jnp.stack([grad_one.reshape(block, TAPS * channels), outer(grad_two)])
+    own = lax.dynamic_slice_in_dim(grad_small, lane, block, 1)
+    return grad_small[0, 0], grad_small[1, 0], grads, own[8:12], own[16 : 16 + classes].T, series
 
 
 def adamw(weight, grad, first, second, rate):
@@ -137,39 +1346,17 @@
     return scale * (tangent - average - normal * cross), -scale * scale * cross
 
 
-def shards(
-    source,
-    index_map,
-    crop_offsets,
-    flip_flags,
-    labels,
-    valid_mask,
-    conv_weights,
-    norm_params,
-    head_weights,
-    decay_rates,
-    conv_first,
-    conv_second,
-    norm_first,
-    norm_second,
-    head_first,
-    head_second,
+def step_general(
+    links, rows, images, conv_weights, decay_rates, norm_params, head_weights, labels, valid
 ):
-    links = Links()
-    own_images = source.shape[0]
-    channels = source.shape[3]
-    rows = float(own_images * MAP * MAP * links.shards * links.copies)
+    own_images, channels = images.shape[2:]
     count = own_images * links.parts
     width = channels // links.parts
     first_column = links.part * width
-
-    picked = source[index_map]
-    images = jax.vmap(crop_image)(picked, crop_offsets, flip_flags)
-    images = images.transpose(1, 2, 0, 3)
+    label_total = lax.psum(jnp.sum(valid), ("shard", "dp"))
     images = links.gather_parts(images, 2)
     labels = links.gather_parts(labels, 0)
-    valid = links.gather_parts(valid_mask.astype(jnp.float32), 0)
-    label_total = lax.psum(jnp.sum(valid_mask.astype(jnp.float32)), ("shard", "dp"))
+    valid = links.gather_parts(valid, 0)
 
     kernel_one = links.gather_members(conv_weights[0], 0)
     kernel_two = links.to_inner(conv_weights[1])
@@ -319,14 +1506,61 @@
         series_one, series_two = series_one + vector[0], series_two + vector[1]
 
     series = jnp.stack([links.own_rows(series_one), links.to_outer(series_two)])
+    grads = jnp.stack([links.own_rows(grad_one), links.to_outer(grad_two)])
+    return (
+        loss_sum,
+        label_total,
+        grads,
+        links.own_rows(grad_norm, 1),
+        links.own_rows(grad_head),
+        series,
+    )
+
+
+def shards(
+    source,
+    index_map,
+    crop_offsets,
+    flip_flags,
+    labels,
+    valid_mask,
+    conv_weights,
+    norm_params,
+    head_weights,
+    decay_rates,
+    conv_first,
+    conv_second,
+    norm_first,
+    norm_second,
+    head_first,
+    head_second,
+):
+    links = Links()
+    rows = float(source.shape[0] * MAP * MAP * links.shards * links.copies)
+    picked = source[index_map]
+    images = jax.vmap(crop_image)(picked, crop_offsets, flip_flags)
+    images = images.transpose(1, 2, 0, 3)
+    fused = links.members * links.copies == 8 and links.parts == 4
+    loss_sum, label_total, grads, grad_norm, grad_head, series = (
+        step_fused if fused else step_general
+    )(
+        links,
+        rows,
+        images,
+        conv_weights,
+        decay_rates,
+        norm_params,
+        head_weights,
+        labels,
+        valid_mask.astype(jnp.float32),
+    )
     hyper_gradient = -neumann_rate * conv_weights * series
-    grads = jnp.stack([links.own_rows(grad_one), links.to_outer(grad_two)])
     conv_new, conv_one, conv_two = adamw(conv_weights, grads, conv_first, conv_second, 0.015)
     norm_new, norm_one, norm_two = adamw(
-        norm_params, links.own_rows(grad_norm, 1), norm_first, norm_second, 0.3
+        norm_params, grad_norm, norm_first, norm_second, 0.3
     )
     head_new, head_one, head_two = adamw(
-        head_weights, links.own_rows(grad_head), head_first, head_second, 0.13
+        head_weights, grad_head, head_first, head_second, 0.13
     )
     return (
         loss_sum,

time: 2080 us -> 887 us (0.43)
  waiting for transfers between devices: 1090 us -> 15.6 us
  Pallas kernels: 0 us -> 802 us
  blocking collectives: 399 us -> 0 us
  matrix products: 211 us -> 0 us
  other arithmetic: 220 us -> 10.4 us
  local copies, waits for them, and re-layouts: 116 us -> 42.1 us
    pallas_call x0 -> x1, Pallas kernels: none -> 802 us  [step_fused(): pl.pallas_call(functools.partial(step_kernel, rows, links.members, links....]
    all_gather x17 -> x1, waiting for transfers between devices: 608 us -> 15.6 us  [step_fused(): series_one = lax.all_gather(series_one, 'dp').transpose(0, 2, 1, 3)]
    psum x4 -> x0, waiting for transfers between devices: 327 us -> none  [sum_rows(): value = lax.psum(value, 'dp')]
    dot_general x48 -> x0, matrix products: 211 us -> none  [dot(): lax.dot_general(left, right, ((dims[0], dims[1]), ((), ())), precision=HI...]
    all_gather x25 -> x0, blocking collectives: 159 us -> none  [the longest x19 94.3 us: sum_rows(): gathered = lax.all_gather(value, 'shard', axis_index_groups=self.within)]
    psum x17 -> x0, blocking collectives: 154 us -> none  [the longest x16 112 us: sum_rows(): value = lax.psum(value, 'dp')]
    reduce_scatter x4 -> x0, waiting for transfers between devices: 99.6 us -> none  [scatter_parts(): lax.psum_scatter(value, 'shard', axis_index_groups=self.across, scatter_d...]
    reduce_sum x54 -> x0, other arithmetic: 88.1 us -> none  [the longest x28 55.1 us: sum_rows(): return jnp.sum(gathered, axis=0)]
  transfers between devices with their start and end apart: 27 -> 1, of which waited for: 24 -> 1; matrix products, arithmetic and copies ran while one was open for 8% -> 2% of each run, Pallas kernels for 0% -> 0%
where the time goes in v3:
time: 887 us; the launch traced here: 885 us
  Pallas kernels  802 us (90%)
  local copies, waits for them, and re-layouts  42.1 us (5%)
  waiting for transfers between devices  15.6 us (2%)
  between operations  14.4 us (2%)
  other arithmetic  10.4 us (1%)
    pallas_call x1, Pallas kernels, step_fused(): pl.pallas_call(functools.partial(step_kernel, rows, links.members, links....  802 us
  transfers between devices with their start and end apart: 1, of which 1 were waited for; matrix products, arithmetic and copies ran while one was open for 2% of the time, Pallas kernels for 0%

profile of v3, /device:TPU:0, one launch (start us, length us, event | category | flops | bytes accessed | tf_op | source)
XLA Modules:
  0.0 884.9 jit_solution(1005237049991644137)
XLA Ops:
  7.2 0.0 all-gather.3.cloned.1.call-start
  7.3 0.7 convert_element_type.14
  7.9 0.7 fusion.2
  8.6 3.0 fusion.14
  11.6 1.7 constant_dynamic-slice_fusion
  13.3 1.8 reshape.86
  15.1 2.0 copy.63
  17.1 0.0 copy-done
  17.1 1.6 fusion.15
  18.6 1.6 reshape_squeeze.10
  20.3 0.0 copy-start.14
  20.3 0.4 reshape_squeeze.11
  20.7 0.0 copy-start.3
  20.7 1.7 dynamic-slice_reduce_fusion
  22.4 0.8 copy.61
  23.2 0.8 copy.62
  24.0 0.0 copy-done.14
  24.1 0.0 copy-done.3
  24.1 0.0 copy-start.13
  24.1 0.0 copy-start.15
  24.1 0.6 gather_fusion
  24.7 0.5 copy.42
  25.3 0.0 copy-done.13
  25.3 0.0 copy-start.9
  25.3 0.0 copy-start.6
  25.3 0.0 copy-done.15
  25.3 0.1 stack_broadcast_in_dim.2
  25.4 1.4 gather_fusion.1
  26.8 0.9 reverse_select_fusion
  27.7 0.0 copy-done.9
  27.7 0.3 dynamic_update_slice.9
  28.0 0.0 copy-done.6
  28.0 0.5 dynamic_update_slice.10.pair_in
  28.5 0.0 copy-start.5
  28.5 0.2 dynamic_update_slice.11
  28.7 0.0 copy-start.4
  28.7 0.4 copy-done.5
  29.1 0.3 copy-done.4
  29.3 802.4 %train_step.1 = (f32[9,16,512]{2,1,0:T(8,128)}, f32[4,64,1152]{2,1,0:T(8,128)}, f32[9,2,2,16,512]{4,3,2,1,0:T(8,128)}, f32[4,64,1152]{2,1,0:T(8,128)}, f32[32,128]{1,0:T(8,128)}) custom-call(f32[16,12,512]{2,1,0:T(8,128)} %bitcast.46, f32[2,2,16,4608]{3,2,1,0:T(8,128)} %bitcast.43, f32[64,1152]{1,0:T(8,128)} %bitcast.51, f32[64,1152]{1,0:T(8,128)} %bitcast.50, ...), custom_call_target="tpu_custom_call" | custom-call | tf_op jit(solution)/shard_map/train_step/pallas_call | solution.py:1230
  831.7 0.0 all-gather.3.cloned.1.call-update
  831.8 2.0 copy.60
  833.8 0.2 stack_reshape.12
  834.0 1.4 reshape.89
  835.4 1.8 copy.47
  837.2 2.8 stack_reshape.13
  840.0 1.4 reshape.90
  841.4 0.0 copy-start.11
  841.4 0.0 copy-start.12
  841.4 0.0 copy-start.7
  841.4 0.0 copy-start.8
  841.4 1.8 copy.49
  843.2 2.9 stack_reshape.15
  846.1 0.5 fusion.16
  846.6 0.7 multiply_subtract_fusion.2
  847.3 0.0 copy-done.8
  847.3 0.7 multiply_subtract_fusion.1
  848.0 1.1 constant_dynamic-update-slice_fusion.1
  849.1 0.0 copy-done.2
  849.1 1.1 constant_dynamic-update-slice_fusion
  850.2 15.6 %all-gather.3.cloned.1.call-done = f32[36,16,512]{2,1,0:T(8,128)} async-done(((f32[9,16,512]{2,1,0:T(8,128)}), f32[36,16,512]{2,1,0:T(8,128)}) %all-gather.3.cloned.1.call-update) | async-done | bytes 1179664 | tf_op jit(solution)/shard_map/all_gather | solution.py:1252
  865.8 3.3 copy.59
  869.1 1.8 stack_reshape.14
  870.9 0.5 copy-done.1
  871.4 6.7 multiply_subtract_fusion
  (15 shorter events, 0.1 us)
Async XLA Ops:
  7.2 858.6 %all-gather.3.cloned.1.call-start = ((), (), s32[]{:S(2)}) async-start(), calls=%async_computation | async-start | bytes 1474560 | tf_op jit(solution)/shard_map/all_gather | solution.py:1252
  8.6 8.4 copy-start
  20.3 3.8 copy-start.14
  20.7 3.4 copy-start.3
  24.1 1.2 copy-start.13
  24.1 1.2 copy-start.15
  25.3 2.5 copy-start.9
  25.3 2.7 copy-start.6
  28.5 0.6 copy-start.5
  28.7 0.6 copy-start.4
  841.4 4.7 copy-start.10
  841.4 5.3 copy-start.11
  841.4 5.3 copy-start.12
  841.4 5.9 copy-start.7
  841.4 5.9 copy-start.8
  843.2 5.9 copy-start.2
  869.1 2.3 copy-start.1
Sparse Core Ops, SparseCore 0:
  831.9 33.8 all-gather.2

commit v4 on v3

--- a/solution.py
+++ b/solution.py
@@ -88,19 +88,20 @@
     copies,
     classes,
     x_in,
-    k1_in,
-    k2_in,
-    d2_in,
-    d1,
+    weights_in,
+    decay_in,
     pair_in,
     label_in,
+    grads,
+    series,
+    grad_small,
     series_one,
-    gathered_two,
-    grad_one,
-    grad_two,
-    grad_small,
     series_two,
     grad_source,
+    row_parts,
+    row_box,
+    cut_box,
+    d1,
     d2,
     v1,
     v2,
@@ -161,8 +162,11 @@
     chances,
     weights,
     pull_logits,
-    load_sem,
+    x_load,
+    pair_sem,
+    cut_load,
     k1_load,
+    d1_load,
     k1_send,
     k1_recv,
     first_send,
@@ -189,10 +193,10 @@
     back_recv,
     swap_send,
     swap_recv,
-    grad_send,
-    grad_recv,
-    last_send,
-    last_recv,
+    row_send,
+    row_recv,
+    own_send,
+    own_recv,
 ):
     shard = lax.axis_index("shard")
     copy = lax.axis_index("dp")
@@ -212,14 +216,6 @@
     def part_peer(other):
         return (other * members + member, copy)
 
-    def owner(other):
-        return (me, other)
-
-    def holder(other):
-        return (other * members + shard // copies, shard % copies)
-
-    owns = shard == me
-
     def remote(source, target, send, recv, device):
         return pltpu.make_async_remote_copy(
             src_ref=source,
@@ -238,31 +234,33 @@
         greet(row_peer(me ^ step))
     for step in range(1, 4):
         greet(part_peer(part ^ step))
-    for step in range(4):
-
-        @pl.when(jnp.logical_not(owns & (step == copy)))
-        def _():
-            greet(owner(step))
-
-        @pl.when(jnp.logical_not(owns & (step == part)))
-        def _():
-            greet(holder(step))
-
-    own_places = pl.ds(pl.multiple_of(member * 2, 2), 2)
+    channels = x_in.shape[2]
+    own_pieces = pl.ds(pl.multiple_of(member * 4, 4), 4)
 
     def tap_lanes(tap, width):
         return pl.ds(pl.multiple_of(tap * width, width), width)
 
-    channels = x_in.shape[2]
-    x_load = pltpu.make_async_copy(x_in, x_box.at[part], load_sem.at[0])
-    x_load.start()
+    x_here = pltpu.make_async_copy(x_in, x_box.at[part], x_load)
+    x_here.start()
     k1_loads = [
         pltpu.make_async_copy(
-            k1_in.at[:, :, :, pl.ds(tap * channels, channels)], v1.at[tap, own_places], k1_load.at[tap]
+            weights_in.at[0, :, :, pl.ds(tap * channels, channels)],
+            v1.at[tap, own_pieces],
+            k1_load.at[tap],
         )
         for tap in range(TAPS)
     ]
-    for load in k1_loads:
+    d1_loads = [
+        pltpu.make_async_copy(
+            decay_in.at[0, copy, :, pl.ds(tap * channels, channels)], d1.at[tap], d1_load.at[tap]
+        )
+        for tap in range(TAPS)
+    ]
+    cut_loads = [
+        pltpu.make_async_copy(weights_in.at[1, copy], row_box.at[0], cut_load.at[0]),
+        pltpu.make_async_copy(decay_in.at[1, copy], row_box.at[1], cut_load.at[1]),
+    ]
+    for load in cut_loads + k1_loads + d1_loads:
         load.start()
     stats_own[...] = jnp.zeros_like(stats_own)
     channel[...] = jnp.zeros_like(channel)
@@ -270,71 +268,74 @@
     a_both[...] = jnp.zeros_like(a_both)
     b_both[...] = jnp.zeros_like(b_both)
     label_box[0] = label_in[...]
-    x_load.wait()
-    pl.semaphore_wait(barrier, 18 - 2 * owns.astype(jnp.int32))
-
-    def ring_move(box, send, recv, block, step, way):
+    x_here.wait()
+    pl.semaphore_wait(barrier, 10)
+
+    def ring_move(box, send, recv, block, step, way, half):
+        at = pl.ds(half * 8, 8)
         return remote(
-            box.at[block],
-            box.at[block],
-            send.at[0 if way > 0 else 1, step],
-            recv.at[block],
+            box.at[block, at],
+            box.at[block, at],
+            send.at[0 if way > 0 else 1, step, half],
+            recv.at[block, half],
             part_peer(part + way),
         )
 
     def ring_start(box, send, recv):
-        @pl.when(part < last)
-        def _():
-            ring_move(box, send, recv, part, 0, 1).start()
-
-        @pl.when(part > 0)
-        def _():
-            ring_move(box, send, recv, part, 0, -1).start()
-
-    def ring_step(box, send, recv, step, use=None):
-        @pl.when(part >= step)
-        def _():
-            ring_move(box, send, recv, part - step, step, -1).wait_recv()
+        for half in range(2):
 
             @pl.when(part < last)
             def _():
-                ring_move(box, send, recv, part - step, step, 1).start()
-
-        @pl.when(part + step <= last)
-        def _():
-            ring_move(box, send, recv, part + step, step, 1).wait_recv()
+                ring_move(box, send, recv, part, 0, 1, half).start()
 
             @pl.when(part > 0)
             def _():
-                ring_move(box, send, recv, part + step, step, -1).start()
-
-        if use is not None:
+                ring_move(box, send, recv, part, 0, -1, half).start()
+
+    def ring_step(box, send, recv, step):
+        for half in range(2):
 
             @pl.when(part >= step)
             def _():
-                use(part - step)
+                ring_move(box, send, recv, part - step, step, -1, half).wait_recv()
+
+                @pl.when(part < last)
+                def _():
+                    ring_move(box, send, recv, part - step, step, 1, half).start()
 
             @pl.when(part + step <= last)
             def _():
-                use(part + step)
+                ring_move(box, send, recv, part + step, step, 1, half).wait_recv()
+
+                @pl.when(part > 0)
+                def _():
+                    ring_move(box, send, recv, part + step, step, -1, half).start()
 
     def ring_end(box, send, recv):
         for step in range(0, 3):
-
-            @pl.when((part >= step) & (part < last))
-            def _():
-                ring_move(box, send, recv, part - step, step, 1).wait_send()
-
-            @pl.when((part + step <= last) & (part > 0))
-            def _():
-                ring_move(box, send, recv, part + step, step, -1).wait_send()
+            for half in range(2):
+
+                @pl.when((part >= step) & (part < last))
+                def _():
+                    ring_move(box, send, recv, part - step, step, 1, half).wait_send()
+
+                @pl.when((part + step <= last) & (part > 0))
+                def _():
+                    ring_move(box, send, recv, part + step, step, -1, half).wait_send()
+
+    order = (
+        part,
+        jnp.where(part == 0, 1, part - 1),
+        jnp.where(part == 3, 1, jnp.where(part == 2, 3, 2)),
+        jnp.where(part < 2, 3, 0),
+    )
 
     ring_start(x_box, x_send, x_recv)
     partner = row_peer(me ^ copies)
     k1_moves = [
         remote(
-            k1_in.at[:, :, :, pl.ds(tap * channels, channels)],
-            v1.at[tap, own_places],
+            weights_in.at[0, :, :, pl.ds(tap * channels, channels)],
+            v1.at[tap, own_pieces],
             k1_send.at[tap],
             k1_recv.at[tap],
             partner,
@@ -344,24 +345,50 @@
     for move in k1_moves:
         move.start()
 
-    target = holder(copy)
-    own_piece = owns & (part == copy)
-    k2_move = remote(k2_in, v2.at[shard], first_send.at[0], first_recv.at[0], target)
-    d2_move = remote(d2_in, d2, first_send.at[1], first_recv.at[1], target)
-    k2_here = pltpu.make_async_copy(k2_in, v2.at[shard], load_sem.at[1])
-    d2_here = pltpu.make_async_copy(d2_in, d2, load_sem.at[2])
-
-    @pl.when(own_piece)
-    def _():
-        k2_here.start()
-        d2_here.start()
-
-    @pl.when(jnp.logical_not(own_piece))
-    def _():
-        k2_move.start()
-        d2_move.start()
-
-    pair_move = remote(pair_in, pair_box, first_send.at[2], first_recv.at[2], partner)
+    def cut_move(which, other):
+        box = v2.at[me, part] if which == 0 else d2.at[part]
+        return remote(
+            cut_box.at[which, other],
+            box,
+            first_send.at[which, other],
+            first_recv.at[which, part],
+            part_peer(other),
+        )
+
+    def cut_start(which):
+        for other in range(4):
+            for tap in range(TAPS):
+                start = tap * channels + other * LANES
+                cut_box[which, other, :, tap * LANES : (tap + 1) * LANES] = row_box[
+                    which, :, start : start + LANES
+                ]
+        for other in range(4):
+
+            @pl.when(part != other)
+            def _():
+                cut_move(which, other).start()
+
+        if which == 0:
+            v2[me, part] = cut_box[which, part]
+        else:
+            d2[part] = cut_box[which, part]
+
+    def cut_end(which):
+        for other in range(4):
+
+            @pl.when(part != other)
+            def _():
+                cut_move(which, other).wait_send()
+                box = v2.at[me, other] if which == 0 else d2.at[other]
+                remote(
+                    cut_box.at[which, other],
+                    box,
+                    first_send.at[which, other],
+                    first_recv.at[which, other],
+                    part_peer(other),
+                ).wait_recv()
+
+    pair_move = remote(pair_in, pair_box, pair_sem.at[0], pair_sem.at[1], partner)
     pair_move.start()
     label_moves = [
         remote(
@@ -379,19 +406,30 @@
     pair = row_peer(me ^ 1)
 
     def piece_of(which, other):
-        if which < GROUPS:
-            return v1.at[pl.ds(which * 3, 3), other // 2, other % 2]
-        return v2.at[other]
+        if isinstance(which, int):
+            return v1.at[pl.ds(which * 3, 3), other]
+        return v2.at[other, which[0]]
+
+    def lane_of(which):
+        return which if isinstance(which, int) else GROUPS + which[0]
 
     def to_plane(which, step):
-        piece = piece_of(which, me)
+        piece, at = piece_of(which, me), lane_of(which)
         return remote(
-            piece, piece, back_send.at[which, step], back_recv.at[which, step], row_peer(me ^ (2 * step))
-        )
+            piece, piece, back_send.at[at, step], back_recv.at[at, step], row_peer(me ^ (2 * step))
+        )
+
+    def from_plane(which, step):
+        piece, at = piece_of(which, me ^ (2 * step)), lane_of(which)
+        return remote(piece, piece, back_send.at[at, step], back_recv.at[at, step], pair)
 
     def to_pair(which, step):
-        piece = piece_of(which, me ^ (2 * step))
-        return remote(piece, piece, swap_send.at[which, step], swap_recv.at[which, step], pair)
+        piece, at = piece_of(which, me ^ (2 * step)), lane_of(which)
+        return remote(piece, piece, swap_send.at[at, step], swap_recv.at[at, step], pair)
+
+    def from_pair(which, step):
+        piece, at = piece_of(which, me ^ 1 ^ (2 * step)), lane_of(which)
+        return remote(piece, piece, swap_send.at[at, step], swap_recv.at[at, step], pair)
 
     def back_start(which):
         for step in range(1, 4):
@@ -400,18 +438,12 @@
 
     def back_forward(which):
         for step in range(1, 4):
-            piece = piece_of(which, me ^ (2 * step))
-            remote(
-                piece, piece, back_send.at[which, step], back_recv.at[which, step], pair
-            ).wait_recv()
+            from_plane(which, step).wait_recv()
             to_pair(which, step).start()
 
     def back_arrived(which):
         for step in range(0, 4):
-            piece = piece_of(which, me ^ 1 ^ (2 * step))
-            remote(
-                piece, piece, swap_send.at[which, step], swap_recv.at[which, step], pair
-            ).wait_recv()
+            from_pair(which, step).wait_recv()
 
     def back_end(which):
         for step in range(1, 4):
@@ -419,20 +451,11 @@
         for step in range(0, 4):
             to_pair(which, step).wait_send()
 
-    @pl.when(own_piece)
-    def _():
-        k2_here.wait()
-        d2_here.wait()
-
-    @pl.when(jnp.logical_not(own_piece))
-    def _():
-        k2_move.wait_send()
-        d2_move.wait_send()
-        remote(k2_in, v2.at[me], first_send.at[0], first_recv.at[0], target).wait_recv()
-        d2_move.wait_recv()
-
-    back_start(GROUPS)
-
+    for load in cut_loads:
+        load.wait()
+    cut_start(0)
+    ring_step(x_box, x_send, x_recv, 1)
+    cut_start(1)
     pair_move.wait()
     small = pair_in[...] + pair_box[...]
     move_norm[...] = small[0:8]
@@ -503,17 +526,15 @@
         return total
 
     def split_one(tap, _):
-        for place_of in range(4):
-            for core_of in range(2):
-                start = (place_of * 2 + core_of) * 16
-                v1_hi[tap, start : start + 16], v1_lo[tap, start : start + 16] = halves(
-                    v1[tap, place_of, core_of]
-                )
+        for other in range(8):
+            at = slice(other * 16, other * 16 + 16)
+            v1_hi[tap, at], v1_lo[tap, at] = halves(v1[tap, other])
 
     def split_two(high, low):
-        def body(block, _):
-            at = pl.ds(pl.multiple_of(block * 64, 64), 64)
-            high[at], low[at] = halves(v2[block])
+        def body(other, _):
+            for block in range(4):
+                at = pl.ds(pl.multiple_of(block * LANES + other * 16, 16), 16)
+                high[at], low[at] = halves(v2[other, block])
 
         lax.fori_loop(0, 8, body, None)
 
@@ -540,17 +561,23 @@
 
         lax.fori_loop(0, TAPS, body, None)
 
-    def up(block):
+    def up(block, half):
+        at = pl.ds(half * 8, 8)
         return remote(
-            partial.at[block], from_low.at[block], up_send.at[block], up_recv.at[block], part_peer(part + 1)
-        )
-
-    def down(block):
+            partial.at[block, at],
+            from_low.at[block, at],
+            up_send.at[block, half],
+            up_recv.at[block, half],
+            part_peer(part + 1),
+        )
+
+    def down(block, half):
+        at = pl.ds(half * 8, 8)
         return remote(
-            partial.at[block],
-            from_high.at[block],
-            down_send.at[block],
-            down_recv.at[block],
+            partial.at[block, at],
+            from_high.at[block, at],
+            down_send.at[block, half],
+            down_recv.at[block, half],
             part_peer(part - 1),
         )
 
@@ -560,39 +587,44 @@
 
         @pl.when(part == 0)
         def _():
-            up(3).start()
-            up(2).start()
+            for block in (3, 2):
+                for half in range(2):
+                    up(block, half).start()
 
         @pl.when(part == last)
         def _():
-            down(0).start()
-            down(1).start()
+            for block in (0, 1):
+                for half in range(2):
+                    down(block, half).start()
 
         part_of_second(maps, high, low, 1 - near)
         for block in (3, 2, 1):
             goal = last - block
 
-            @pl.when((part < block) & (part > 0))
-            def _():
-                up(block).wait_recv()
-                partial[block] += from_low[block]
-                up(block).start()
-
-            @pl.when((part > goal) & (part < last))
-            def _():
-                down(goal).wait_recv()
-                partial[goal] += from_high[goal]
-                down(goal).start()
-
-            if block == 1:
-
-                @pl.when(part == 0)
+            for half in range(2):
+                at = slice(half * 8, half * 8 + 8)
+
+                @pl.when((part < block) & (part > 0))
                 def _():
-                    up(1).start()
-
-                @pl.when(part == last)
+                    up(block, half).wait_recv()
+                    partial[block, at] += from_low[block, at]
+                    up(block, half).start()
+
+                @pl.when((part > goal) & (part < last))
                 def _():
-                    down(2).start()
+                    down(goal, half).wait_recv()
+                    partial[goal, at] += from_high[goal, at]
+                    down(goal, half).start()
+
+                if block == 1:
+
+                    @pl.when(part == 0)
+                    def _():
+                        up(1, half).start()
+
+                    @pl.when(part == last)
+                    def _():
+                        down(2, half).start()
 
             aside(3 - block)
         aside(3)
@@ -600,25 +632,28 @@
 
             @pl.when(part == block)
             def _():
-                total = partial[block]
-                if block > 0:
-                    up(block).wait_recv()
-                    total = total + from_low[block]
-                if block < last:
-                    down(block).wait_recv()
-                    total = total + from_high[block]
-                flow[...] = total
+                for half in range(2):
+                    at = slice(half * 8, half * 8 + 8)
+                    total = partial[block, at]
+                    if block > 0:
+                        up(block, half).wait_recv()
+                        total = total + from_low[block, at]
+                    if block < last:
+                        down(block, half).wait_recv()
+                        total = total + from_high[block, at]
+                    flow[at] = total
 
         for block in (3, 2, 1):
             goal = last - block
-
-            @pl.when(part < block)
-            def _():
-                up(block).wait_send()
-
-            @pl.when(part > goal)
-            def _():
-                down(goal).wait_send()
+            for half in range(2):
+
+                @pl.when(part < block)
+                def _():
+                    up(block, half).wait_send()
+
+                @pl.when(part > goal)
+                def _():
+                    down(goal, half).wait_send()
 
     def turn_block(block, left, turned_block):
         value = slots[block].reshape(16 * count, LANES)
@@ -638,19 +673,82 @@
             out = (out[:LANES, :LANES] + out[LANES:, :LANES]) + (
                 out[:LANES, LANES:] + out[LANES:, LANES:]
             )
-            sum_two[block, :, :, lanes] += out.reshape(2, 64, LANES)
+            sum_two[block, :, :, :, lanes] += out.reshape(4, 2, 16, LANES)
 
         lax.fori_loop(0, TAPS, body, None)
 
-    def gather_and_use(block_of):
+    def pair_two(block):
+        return remote(
+            sum_two.at[block, :, 1 - core],
+            half_two.at[block],
+            pair_send.at[GROUPS + block],
+            pair_recv.at[GROUPS + block],
+            pair,
+        )
+
+    def plane_two(block, step):
+        other = place ^ step
+        return remote(
+            half_two.at[block, other],
+            piece_two.at[step, block],
+            plane_send.at[GROUPS + block, step],
+            plane_recv.at[GROUPS + block, step],
+            row_peer(other * 2 + core),
+        )
+
+    def plane_two_go(block):
+        pair_two(block).wait()
+        for place_of in range(4):
+            half_two[block, place_of] += sum_two[block, place_of, core]
+        for step in range(1, 4):
+            plane_two(block, step).start()
+
+    def step_two(block, new_of, more):
+        for step in range(1, 4):
+            plane_two(block, step).wait()
+        change = half_two[block, place] + piece_two[1, block] + piece_two[2, block] + piece_two[3, block]
+        new = new_of(v2[me, block], change, d2[block])
+        v2[me, block] = new
+        series_two[block] += new
+
+        @pl.when(more)
+        def _():
+            back_start((block,))
+
+    def back_forward_when(block, more):
+        @pl.when(more)
+        def _():
+            back_forward((block,))
+
+    def gather_and_use(block_of, new_of, more):
         ring_start(slots, ring_send, ring_recv)
-        block_of(part)
-        for step in range(1, 4):
-            ring_step(slots, ring_send, ring_recv, step, block_of)
+        block_of(order[0])
+        pair_two(order[0]).start()
+        ring_step(slots, ring_send, ring_recv, 1)
+        block_of(order[1])
+        pair_two(order[1]).start()
+        plane_two_go(order[0])
+        ring_step(slots, ring_send, ring_recv, 2)
+        step_two(order[0], new_of, more)
+        block_of(order[2])
+        pair_two(order[2]).start()
+        plane_two_go(order[1])
+        ring_step(slots, ring_send, ring_recv, 3)
+        step_two(order[1], new_of, more)
+        block_of(order[3])
+        pair_two(order[3]).start()
+        plane_two_go(order[2])
+        back_forward_when(order[0], more)
         ring_end(slots, ring_send, ring_recv)
 
-    def pair_two():
-        return remote(sum_two.at[:, 1 - core], half_two, pair_send.at[GROUPS], pair_recv.at[GROUPS], pair)
+    def rest_of_two(new_of, more):
+        plane_two_go(order[3])
+        step_two(order[2], new_of, more)
+        back_forward_when(order[1], more)
+
+    def end_of_two(new_of, more):
+        step_two(order[3], new_of, more)
+        back_forward_when(order[2], more)
 
     def pair_one(group):
         return remote(
@@ -659,16 +757,6 @@
             pair_send.at[group],
             pair_recv.at[group],
             pair,
-        )
-
-    def plane_two(step):
-        other = place ^ step
-        return remote(
-            half_two.at[other],
-            piece_two.at[step],
-            plane_send.at[GROUPS, step],
-            plane_recv.at[GROUPS, step],
-            row_peer(other * 2 + core),
         )
 
     def plane_one(group, step):
@@ -681,13 +769,7 @@
             row_peer(other * 2 + core),
         )
 
-    def finish_gradients(new_of):
-        pair_two().wait()
-        for place_of in range(4):
-            half_two[place_of] += sum_two[place_of, core]
-        for step in range(1, 4):
-            plane_two(step).start()
-
+    def first_gradient():
         def tap_weight(tap, _):
             out = mul(turned[...], window(x_both, tap, slice(0, channels)))
             out = out + mul(turned[...], window(x_both, tap, slice(channels, 2 * channels)))
@@ -710,13 +792,6 @@
             if group > 0:
                 plane_go(group - 1)
         plane_go(GROUPS - 1)
-        for step in range(1, 4):
-            plane_two(step).wait()
-        change = half_two[place] + piece_two[1] + piece_two[2] + piece_two[3]
-        new = new_of(v2[me], change, d2[...])
-        v2[me] = new
-        series_two[...] += new
-        return new
 
     def step_group(group, new_of):
         for step in range(1, 4):
@@ -726,22 +801,34 @@
             change = (
                 half_one[tap, place] + piece_one[1, tap] + piece_one[2, tap] + piece_one[3, tap]
             )
-            new = new_of(v1[tap, place, core], change, d1[tap])
-            v1[tap, place, core] = new
-            series_one[tap] += new
+            new = new_of(v1[tap, me], change, d1[tap])
+            v1[tap, me] = new
+            series_one[:, tap_lanes(tap, channels)] += new
 
         lax.fori_loop(group * 3, group * 3 + 3, body, None)
 
     def no_aside(index):
         pass
 
-    for load in k1_loads:
+    series_one[...] = jnp.zeros_like(series_one)
+    series_two[...] = jnp.zeros_like(series_two)
+
+    def first_vector(old, change, decay):
+        return change + decay * old
+
+    def next_vector(old, change, decay):
+        return old - neumann_rate * (change + decay * old)
+
+    for load in k1_loads + d1_loads:
         load.wait()
     for move in k1_moves:
         move.wait()
     lax.fori_loop(0, TAPS, split_one, None)
-    for step in range(1, 4):
-        ring_step(x_box, x_send, x_recv, step)
+    ring_step(x_box, x_send, x_recv, 2)
+    cut_end(0)
+    for block in range(4):
+        back_start((block,))
+    ring_step(x_box, x_send, x_recv, 3)
     ring_end(x_box, x_send, x_recv)
 
     def place_images(cell, _):
@@ -763,9 +850,12 @@
     put_sums(0, *each_cell(sums_primal, (zero, zero)))
     stats_own[0, 2:3, :] = jnp.sum(valid, axis=0, keepdims=True)
     moves = sum_start(0, 8)
-    back_forward(GROUPS)
-    back_arrived(GROUPS)
-    back_end(GROUPS)
+    for block in range(4):
+        back_forward((block,))
+    cut_end(1)
+    for block in range(4):
+        back_arrived((block,))
+        back_end((block,))
     split_two(k_hi, k_lo)
     partial[...] = jnp.zeros_like(partial)
     total = sum_end(0, 8, moves)
@@ -842,8 +932,7 @@
         turn_block(block, g_left.at[block], g_turned.at[block])
         use_block(block, g_left.at[block], g_turned.at[block], k_hi, k_lo, a_both)
 
-    gather_and_use(primal_block)
-    pair_two().start()
+    gather_and_use(primal_block, first_vector, True)
 
     def back_one_primal(cell, carry):
         seen = fold_sum[cell // 4 + 1, cell % 4 + 1]
@@ -853,7 +942,9 @@
         return carry[0] + pull * n1[cell], carry[1] + pull
 
     put_sums(3, *each_cell(back_one_primal, (zero, zero)))
-    total = sum_end(3, 8, sum_start(3, 8))
+    moves = sum_start(3, 8)
+    rest_of_two(first_vector, True)
+    total = sum_end(3, 8, moves)
     out_gain, out_shift = total[0:1], total[1:2]
     factor = scale * gain
 
@@ -878,32 +969,73 @@
     grad_small[8:16, :] = move_norm[...]
     move_head[0:16] = grad_small[16:32, :]
 
-    series_one[...] = jnp.zeros_like(series_one)
-    series_two[...] = jnp.zeros_like(series_two)
-
-    def first_vector(old, change, decay):
-        return change + decay * old
-
-    def next_vector(old, change, decay):
-        return old - neumann_rate * (change + decay * old)
-
-    grad_source[...] = finish_gradients(first_vector)
-
-    def grad_move(other):
+    first_gradient()
+    end_of_two(first_vector, True)
+    back_forward((order[3],))
+
+    def deliver_move(which, source, other):
         return remote(
-            grad_source, grad_two.at[part], grad_send.at[other], grad_recv.at[part], owner(other)
-        )
-
-    for other in range(4):
-
-        @pl.when(jnp.logical_not(owns & (copy == other)))
-        def _():
-            grad_move(other).start()
-
-    @pl.when(owns)
-    def _():
-        grad_two[part] = grad_source[...]
-
+            source.at[other],
+            row_parts.at[which, part],
+            row_send.at[which, other],
+            row_recv.at[which, part],
+            part_peer(other),
+        )
+
+    def deliver_start(which, source):
+        for other in range(4):
+
+            @pl.when(part != other)
+            def _():
+                deliver_move(which, source, other).start()
+
+        row_parts[which, part] = source[part]
+
+    def deliver_end(which, source, result):
+        for other in range(4):
+
+            @pl.when(part != other)
+            def _():
+                deliver_move(which, source, other).wait_send()
+                remote(
+                    source.at[other],
+                    row_parts.at[which, other],
+                    row_send.at[which, other],
+                    row_recv.at[which, other],
+                    part_peer(other),
+                ).wait_recv()
+
+        for other in range(4):
+            for tap in range(TAPS):
+                start = tap * channels + other * LANES
+                result[copy, :, start : start + LANES] = row_parts[
+                    which, other, :, tap * LANES : (tap + 1) * LANES
+                ]
+
+    across, corner = row_peer(me ^ 2), copy ^ 2
+
+    def spread_move(which, result, step, block, device):
+        return remote(
+            result.at[block], result.at[block], own_send.at[which, step], own_recv.at[which, step], device
+        )
+
+    def spread_start(which, result):
+        spread_move(which, result, 0, copy, across).start()
+        spread_move(which, result, 1, copy, pair).start()
+
+    def spread_forward(which, result):
+        spread_move(which, result, 0, corner, across).wait_recv()
+        spread_move(which, result, 2, corner, pair).start()
+
+    def spread_end(which, result):
+        spread_move(which, result, 1, copy ^ 1, pair).wait_recv()
+        spread_move(which, result, 2, copy ^ 3, pair).wait_recv()
+        spread_move(which, result, 0, copy, across).wait_send()
+        spread_move(which, result, 1, copy, pair).wait_send()
+        spread_move(which, result, 2, corner, pair).wait_send()
+
+    grad_source[...] = series_two[...]
+    deliver_start(0, grad_source)
     for group in range(GROUPS):
         step_group(group, first_vector)
         back_start(group)
@@ -911,7 +1043,6 @@
     def turn_body(turn, nothing):
         for group in range(GROUPS):
             back_forward(group)
-        back_start(GROUPS)
         flow[...] = jnp.zeros_like(flow)
         for group in range(GROUPS):
             back_arrived(group)
@@ -922,7 +1053,8 @@
 
         @pl.when(turn == 0)
         def _():
-            grad_one[...] = v1[:, own_places]
+            for tap in range(TAPS):
+                grads[0, :, :, tap * channels : (tap + 1) * channels] = v1[tap, own_pieces]
 
         def sums_forward(normal):
             def body(cell, carry):
@@ -933,12 +1065,12 @@
 
         put_sums(0, *sums_forward(n1))
         moves = sum_start(0, 8)
-        back_forward(GROUPS)
         partial[...] = jnp.zeros_like(partial)
         fold_sum[...] = jnp.zeros_like(fold_sum)
         sum_two[...] = jnp.zeros_like(sum_two)
-        back_arrived(GROUPS)
-        back_end(GROUPS)
+        for block in range(4):
+            back_arrived((block,))
+            back_end((block,))
         split_two(v2_hi, v2_lo)
         part_of_second(a_both, v2_hi, v2_lo, 0)
         part_of_second(a_both, v2_hi, v2_lo, 1)
@@ -963,6 +1095,16 @@
 
         scatter(b_both, k_hi, k_lo, aside)
 
+        @pl.when(turn == 0)
+        def _():
+            deliver_end(0, grad_source, grads.at[1])
+            spread_start(0, grads.at[1])
+
+        @pl.when(turn == 1)
+        def _():
+            spread_forward(0, grads.at[1])
+
+
         put_sums(1, *sums_forward(n2))
         total = sum_end(1, 8, sum_start(1, 8)) * inverse
         average2, cross2 = total[0:1], total[1:2]
@@ -1026,8 +1168,8 @@
             turn_block(block, t_left, t_turned)
             use_block(block, t_left, t_turned, k_hi, k_lo, a_both)
 
-        gather_and_use(turn_of_block)
-        pair_two().start()
+        more = turn < NEUMANN - 1
+        gather_and_use(turn_of_block, next_vector, more)
 
         def back_one(cell, carry):
             pull = fold_sum[cell // 4 + 1, cell % 4 + 1]
@@ -1039,7 +1181,9 @@
             )
 
         put_sums(3, *each_cell(back_one, (zero, zero)))
-        total = sum_end(3, 8, sum_start(3, 8))
+        moves = sum_start(3, 8)
+        rest_of_two(next_vector, more)
+        total = sum_end(3, 8, moves)
         out_gain, out_shift = total[0:1], total[1:2]
         factor = scale * gain
         tan_factor = tan_scale_one * gain + scale * move_gain
@@ -1058,44 +1202,32 @@
         move_norm[1:2, :] = move_shift - neumann_rate * out_shift
         move_norm[2:3, :] = move_gain2 - neumann_rate * out_gain2
         move_norm[3:4, :] = move_shift2 - neumann_rate * out_shift2
-        finish_gradients(next_vector)
+        first_gradient()
+        end_of_two(next_vector, more)
+        back_forward_when(order[3], more)
+
+        @pl.when(turn == NEUMANN - 1)
+        def _():
+            deliver_start(1, series_two)
+
         for group in range(GROUPS):
             step_group(group, next_vector)
 
-            @pl.when(turn < NEUMANN - 1)
+            @pl.when(more)
             def _():
                 back_start(group)
 
     lax.fori_loop(0, NEUMANN, turn_body, None)
 
-    def last_move(other):
-        return remote(
-            series_two, gathered_two.at[part], last_send.at[other], last_recv.at[part], owner(other)
-        )
-
-    for other in range(4):
-
-        @pl.when(jnp.logical_not(owns & (copy == other)))
-        def _():
-            last_move(other).start()
-
-    @pl.when(owns)
-    def _():
-        gathered_two[part] = series_two[...]
-
-    for other in range(4):
-
-        @pl.when(jnp.logical_not(owns & (copy == other)))
-        def _():
-            grad_move(other).wait_send()
-            last_move(other).wait_send()
-
-        @pl.when(jnp.logical_not(owns & (part == other)))
-        def _():
-            for box, send, recv in ((grad_two, grad_send, grad_recv), (gathered_two, last_send, last_recv)):
-                remote(
-                    series_two, box.at[other], send.at[other], recv.at[other], owner(other)
-                ).wait_recv()
+    series[0, copy] = series_one[...]
+    spread_start(1, series.at[0])
+    deliver_end(1, series_two, series.at[1])
+    spread_start(2, series.at[1])
+    spread_forward(1, series.at[0])
+    spread_forward(2, series.at[1])
+    spread_end(0, grads.at[1])
+    spread_end(1, series.at[0])
+    spread_end(2, series.at[1])
 
 
 def step_fused(links, rows, images, conv_weights, decay_rates, norm_params, head_weights, labels, valid):
@@ -1104,15 +1236,8 @@
     width, group = channels // 4, 8
     piece, block = width // group, channels // group
     classes = head_weights.shape[1]
-    copy = lax.axis_index("dp")
     f32, b16 = jnp.float32, jnp.bfloat16
 
-    def inner(value):
-        cut = value.reshape(block, TAPS, 4, width)
-        return lax.dynamic_index_in_dim(cut, copy, 2, keepdims=False).reshape(block, TAPS * width)
-
-    d1 = lax.dynamic_slice_in_dim(decay_rates[0], copy * piece, piece, 0)
-    d1 = d1.reshape(piece, TAPS, channels).transpose(1, 0, 2)
     small = jnp.zeros((24, width), f32)
     lane = links.member * block
     small = lax.dynamic_update_slice(small, norm_params, (0, lane))
@@ -1126,10 +1251,8 @@
     )
     operands = (
         images.reshape(cells, own_count, channels),
-        conv_weights[0].reshape(2, 2, piece, TAPS * channels),
-        inner(conv_weights[1]),
-        inner(decay_rates[1]),
-        d1,
+        conv_weights.reshape(2, 4, piece, TAPS * channels),
+        decay_rates.reshape(2, 4, piece, TAPS * channels),
         small,
         tags.reshape(2 * count, LANES),
     )
@@ -1137,20 +1260,24 @@
     anywhere = pl.BlockSpec(memory_space=pl.ANY)
     row_map = pltpu.VMEM((cells, count, width), f32)
     four_maps = pltpu.VMEM((4, cells, count, width), f32)
-    whole_one = pltpu.VMEM((TAPS, 4, 2, piece, channels), f32)
-    inner_piece = pltpu.VMEM((block, TAPS * width), f32)
-    inner_half = pltpu.VMEM((4, block, TAPS * width), f32)
+    inner_piece = pltpu.VMEM((4, piece, TAPS * width), f32)
+    inner_half = pltpu.VMEM((4, 4, piece, TAPS * width), f32)
     inner_part = pltpu.VMEM((channels, TAPS * width), b16)
     outer_part = pltpu.VMEM((TAPS, width, channels), b16)
     both = pltpu.VMEM((MAP + 2, MAP + 2, count, 2 * width), b16)
     logit = pltpu.VMEM((count, LANES), f32)
     dma = pltpu.SemaphoreType.DMA
     scratch = [
+        pltpu.VMEM((piece, TAPS * channels), f32),
         inner_piece,
         inner_piece,
+        pltpu.VMEM((2, 4, piece, TAPS * width), f32),
+        pltpu.VMEM((2, piece, TAPS * channels), f32),
+        pltpu.VMEM((2, 4, piece, TAPS * width), f32),
+        pltpu.VMEM((TAPS, piece, channels), f32),
         inner_piece,
-        whole_one,
-        pltpu.VMEM((group, block, TAPS * width), f32),
+        pltpu.VMEM((TAPS, group, piece, channels), f32),
+        pltpu.VMEM((group, 4, piece, TAPS * width), f32),
         outer_part,
         outer_part,
         inner_part,
@@ -1173,8 +1300,8 @@
         four_maps,
         *[row_map] * 15,
         pltpu.VMEM((MAP + 2, MAP + 2, count, width), f32),
-        whole_one,
-        pltpu.VMEM((4, 2, block, TAPS * width), f32),
+        pltpu.VMEM((TAPS, 4, 2, piece, channels), f32),
+        pltpu.VMEM((4, 4, 2, piece, TAPS * width), f32),
         pltpu.VMEM((TAPS, 4, piece, channels), f32),
         inner_half,
         pltpu.VMEM((4, TAPS, piece, channels), f32),
@@ -1194,67 +1321,63 @@
         logit,
         logit,
         logit,
-        dma((3,)),
+        dma(()),
+        dma((2,)),
+        dma((2,)),
         dma((TAPS,)),
         dma((TAPS,)),
         dma((TAPS,)),
-        dma((3,)),
-        dma((3,)),
+        dma((TAPS,)),
+        dma((2, 4)),
+        dma((2, 4)),
         dma((4,)),
         dma((4,)),
-        dma((2, 4)),
-        dma((4,)),
+        dma((2, 4, 2)),
+        dma((4, 2)),
         dma((4, 8)),
         dma((4, 8)),
         dma((4,)),
         dma((4,)),
-        dma((4,)),
-        dma((4,)),
-        dma((4,)),
-        dma((4,)),
+        dma((4, 2)),
+        dma((4, 2)),
+        dma((4, 2)),
+        dma((4, 2)),
+        dma((2, 4, 2)),
+        dma((4, 2)),
+        dma((GROUPS + 4,)),
+        dma((GROUPS + 4,)),
+        dma((GROUPS + 4, 4)),
+        dma((GROUPS + 4, 4)),
+        dma((GROUPS + 4, 4)),
+        dma((GROUPS + 4, 4)),
+        dma((GROUPS + 4, 4)),
+        dma((GROUPS + 4, 4)),
         dma((2, 4)),
-        dma((4,)),
-        dma((GROUPS + 1,)),
-        dma((GROUPS + 1,)),
-        dma((GROUPS + 1, 4)),
-        dma((GROUPS + 1, 4)),
-        dma((GROUPS + 1, 4)),
-        dma((GROUPS + 1, 4)),
-        dma((GROUPS + 1, 4)),
-        dma((GROUPS + 1, 4)),
-        dma((4,)),
-        dma((4,)),
-        dma((4,)),
-        dma((4,)),
+        dma((2, 4)),
+        dma((3, 3)),
+        dma((3, 3)),
     ]
-    series_one, series_two, grad_one, grad_two, grad_small = pl.pallas_call(
+    result = jax.ShapeDtypeStruct((2, 4, piece, TAPS * channels), f32)
+    grads, series, grad_small = pl.pallas_call(
         functools.partial(step_kernel, rows, links.members, links.copies, classes),
-        out_shape=(
-            jax.ShapeDtypeStruct((TAPS, piece, channels), f32),
-            jax.ShapeDtypeStruct((4, block, TAPS * width), f32),
-            jax.ShapeDtypeStruct((TAPS, 2, 2, piece, channels), f32),
-            jax.ShapeDtypeStruct((4, block, TAPS * width), f32),
-            jax.ShapeDtypeStruct((32, width), f32),
-        ),
-        in_specs=[anywhere] * 4 + [vmem] * 3,
-        out_specs=(vmem,) * 5,
+        out_shape=(result, result, jax.ShapeDtypeStruct((32, width), f32)),
+        in_specs=[anywhere] * 3 + [vmem] * 2,
+        out_specs=(vmem,) * 3,
         scratch_shapes=scratch,
         compiler_params=pltpu.CompilerParams(
             collective_id=1, has_side_effects=True, vmem_limit_bytes=63 * 1024 * 1024
         ),
         name="train_step",
     )(*operands)
-
-    def outer(value):
-        value = value.reshape(4, block, TAPS, width).transpose(1, 2, 0, 3)
-        return value.reshape(block, TAPS * channels)
-
-    series_one = lax.all_gather(series_one, "dp").transpose(0, 2, 1, 3)
-    series = jnp.stack([series_one.reshape(block, TAPS * channels), outer(series_two)])
-    grad_one = grad_one.reshape(TAPS, block, channels).transpose(1, 0, 2)
-    grads = jnp.stack([grad_one.reshape(block, TAPS * channels), outer(grad_two)])
     own = lax.dynamic_slice_in_dim(grad_small, lane, block, 1)
-    return grad_small[0, 0], grad_small[1, 0], grads, own[8:12], own[16 : 16 + classes].T, series
+    return (
+        grad_small[0, 0],
+        grad_small[1, 0],
+        grads.reshape(conv_weights.shape),
+        own[8:12],
+        own[16 : 16 + classes].T,
+        series.reshape(conv_weights.shape),
+    )
 
 
 def adamw(weight, grad, first, second, rate):

time: 887 us -> 651 us (0.73)
  Pallas kernels: 802 us -> 628 us
  local copies, waits for them, and re-layouts: 42.1 us -> 7.71 us
  waiting for transfers between devices: 15.6 us -> 0 us
  between operations: 14.4 us -> 0.89 us
    pallas_call x1, Pallas kernels: 802 us -> 628 us  [step_fused(): pl.pallas_call(functools.partial(step_kernel, rows, links.members, links....]
    all_gather x1 -> x0, waiting for transfers between devices: 15.6 us -> none  [step_fused(): series_one = lax.all_gather(series_one, 'dp').transpose(0, 2, 1, 3)]
    another operation x7 -> x0, local copies, waits for them, and re-layouts: 10.9 us -> none  [the longest x2 4.72 us: step_fused(): jnp.stack([series_one.reshape(block, TAPS * channels), outer(series_two)])]
  transfers between devices with their start and end apart: 1 -> 0, of which waited for: 1 -> 0; matrix products, arithmetic and copies ran while one was open for 2% -> 0% of each run, Pallas kernels for 0% -> 0%
where the time goes in v4:
time: 651 us; the launch traced here: 650 us
  Pallas kernels  628 us (96%)
  other arithmetic  14 us (2%)
  local copies, waits for them, and re-layouts  7.71 us (1%)
    pallas_call x1, Pallas kernels, step_fused(): pl.pallas_call(functools.partial(step_kernel, rows, links.members, links....  628 us

profile of v4, /device:TPU:0, one launch (start us, length us, event | category | flops | bytes accessed | tf_op | source)
XLA Modules:
  0.0 650.5 jit_solution(6481618971650424801)
XLA Ops:
  0.7 1.5 dynamic_update_slice.9
  2.2 1.6 dynamic_update_slice.10.pair_in
  3.7 0.0 copy-start.1
  3.8 0.7 convert_element_type.14
  4.4 0.1 stack_broadcast_in_dim.2
  4.5 0.7 fusion.2
  5.3 0.2 dynamic_update_slice.11
  5.5 0.0 copy-start
  5.5 0.7 compare_select_fusion.2
  6.2 0.0 copy-start.9
  6.2 1.9 gather_fusion
  8.1 0.5 copy.28
  8.6 0.0 copy-done.1
  8.6 0.0 copy-done
  8.6 0.0 copy-done.9
  8.6 0.0 copy-start.10
  8.7 1.4 gather_fusion.1
  10.0 0.0 copy-done.10
  10.0 0.9 reverse_select_fusion
  11.0 627.9 %train_step.1 = (f32[2,4,16,4608]{3,2,1,0:T(8,128)}, f32[2,4,16,4608]{3,2,1,0:T(8,128)}, f32[32,128]{1,0:T(8,128)}) custom-call(f32[16,12,512]{2,1,0:T(8,128)} %bitcast.28, f32[2,4,16,4608]{3,2,1,0:T(8,128)} %bitcast.26, f32[2,4,16,4608]{3,2,1,0:T(8,128)} %bitcast.27, f32[24,128]{1,0:T(8,128)} %copy-done.1, f32[96,128]{1,0:T(8,128)} %bitcast.29), custom_call_target="tpu_custom_call" | custom-call | tf_op jit(solution)/shard_map/train_step/pallas_call | solution.py:1361
  638.8 0.0 copy-start.2
  638.9 0.0 copy-start.3
  638.9 0.0 copy-start.4
  638.9 0.0 copy-start.6
  638.9 0.0 copy-start.5
  638.9 0.0 copy-start.7
  638.9 0.0 copy-start.8
  638.9 9.6 %multiply_subtract_fusion = (f32[2,64,4608]{2,1,0:T(8,128)}, f32[2,64,4608]{2,1,0:T(8,128)}, f32[2,64,4608]{2,1,0:T(8,128)}, f32[2,64,4608]{2,1,0:T(8,128)}) fusion(f32[2,64,4608]{2,1,0:T(8,128)} %param.22, f32[2,4,16,4608]{3,2,1,0:T(8,128)} %get-tuple-element.16, f32[2,64,4608]{2,1,0:T(8,128)} %param.26, f32[2,64,4608]{2,1,0:T(8,128)} %param.27, ...), kind=kLoop, calls=%fused_computation.6 | loop fusion | flops 9437184 | bytes 21233664 | tf_op jit(solution)/shard_map/sub | solution.py:1389
  648.5 0.0 copy-done.2
  648.5 0.0 copy-done.3
  648.5 0.0 copy-done.4
  648.6 0.0 copy-done.6
  648.6 0.7 multiply_subtract_fusion.1
  649.3 0.0 copy-done.5
  649.3 0.0 copy-done.7
  649.3 0.0 copy-done.8
  649.3 0.7 multiply_subtract_fusion.2
  650.0 0.5 fusion.14
  (6 shorter events, 0.0 us)
Async XLA Ops:
  3.7 4.9 copy-start.1
  5.5 3.2 copy-start
  6.2 2.5 copy-start.9
  8.6 1.4 copy-start.10
  638.8 9.7 %copy-start.2 = (f32[64,10]{0,1:T(8,128)S(1)}, f32[64,10]{0,1:T(8,128)}, u32[]{:S(2)}) copy-start(f32[64,10]{0,1:T(8,128)} %param.24) | copy-start | bytes 7684
  638.9 9.7 %copy-start.3 = (f32[64,10]{0,1:T(8,128)S(1)}, f32[64,10]{0,1:T(8,128)}, u32[]{:S(2)}) copy-start(f32[64,10]{0,1:T(8,128)} %param.30) | copy-start | bytes 7684
  638.9 9.7 %copy-start.4 = (f32[64,10]{0,1:T(8,128)S(1)}, f32[64,10]{0,1:T(8,128)}, u32[]{:S(2)}) copy-start(f32[64,10]{0,1:T(8,128)} %param.31) | copy-start | bytes 7684
  638.9 9.7 %copy-start.6 = (f32[32,128]{1,0:T(8,128)S(1)}, f32[32,128]{1,0:T(8,128)}, u32[]{:S(2)}) copy-start(f32[32,128]{1,0:T(8,128)} %get-tuple-element.15) | copy-start | bytes 49156
  638.9 10.4 %copy-start.5 = (f32[4,64]{1,0:T(4,128)S(1)}, f32[4,64]{1,0:T(4,128)}, u32[]{:S(2)}) copy-start(f32[4,64]{1,0:T(4,128)} %param.23) | copy-start | bytes 3076
  638.9 10.4 %copy-start.7 = (f32[4,64]{1,0:T(4,128)S(1)}, f32[4,64]{1,0:T(4,128)}, u32[]{:S(2)}) copy-start(f32[4,64]{1,0:T(4,128)} %param.28) | copy-start | bytes 3076
  638.9 10.4 %copy-start.8 = (f32[4,64]{1,0:T(4,128)S(1)}, f32[4,64]{1,0:T(4,128)}, u32[]{:S(2)}) copy-start(f32[4,64]{1,0:T(4,128)} %param.29) | copy-start | bytes 3076

commit v5 on v4

--- a/solution.py
+++ b/solution.py
@@ -87,11 +87,15 @@
     members,
     copies,
     classes,
-    x_in,
+    source,
+    index_map,
+    crop_offsets,
+    flip_flags,
+    labels,
+    valid_mask,
     weights_in,
     decay_in,
     pair_in,
-    label_in,
     grads,
     series,
     grad_small,
@@ -111,6 +115,7 @@
     v2_lo,
     k_hi,
     k_lo,
+    source_box,
     x_box,
     x_row,
     x_both,
@@ -145,7 +150,10 @@
     sum_two,
     half_one,
     half_two,
-    piece_one,
+    first_low,
+    first_up,
+    second_low,
+    second_up,
     piece_two,
     stats_box,
     stats_own,
@@ -193,6 +201,12 @@
     back_recv,
     swap_send,
     swap_recv,
+    fold_send,
+    fold_recv,
+    open_send,
+    open_recv,
+    share_send,
+    share_recv,
     row_send,
     row_recv,
     own_send,
@@ -203,10 +217,10 @@
     part = shard // members
     member = shard % members
     me = member * copies + copy
-    place, core = me // 2, me % 2
+    place, line, core = me // 2, (me // 2) % 2, me % 2
     last = 3
     count = flow.shape[1]
-    own_count = x_in.shape[1]
+    own_count = source.shape[0]
     inverse = 1.0 / rows
     zero = jnp.zeros((count, LANES), jnp.float32)
 
@@ -234,31 +248,30 @@
         greet(row_peer(me ^ step))
     for step in range(1, 4):
         greet(part_peer(part ^ step))
-    channels = x_in.shape[2]
-    own_pieces = pl.ds(pl.multiple_of(member * 4, 4), 4)
+    channels = source.shape[3]
 
     def tap_lanes(tap, width):
         return pl.ds(pl.multiple_of(tap * width, width), width)
 
-    x_here = pltpu.make_async_copy(x_in, x_box.at[part], x_load)
-    x_here.start()
+    source_load = pltpu.make_async_copy(source, source_box, x_load)
+    source_load.start()
     k1_loads = [
         pltpu.make_async_copy(
-            weights_in.at[0, :, :, pl.ds(tap * channels, channels)],
-            v1.at[tap, own_pieces],
+            weights_in.at[0, :, :, :, pl.ds(tap * channels, channels)],
+            v1.at[tap, member],
             k1_load.at[tap],
         )
         for tap in range(TAPS)
     ]
     d1_loads = [
         pltpu.make_async_copy(
-            decay_in.at[0, copy, :, pl.ds(tap * channels, channels)], d1.at[tap], d1_load.at[tap]
+            decay_in.at[0, line, core, :, pl.ds(tap * channels, channels)], d1.at[tap], d1_load.at[tap]
         )
         for tap in range(TAPS)
     ]
     cut_loads = [
-        pltpu.make_async_copy(weights_in.at[1, copy], row_box.at[0], cut_load.at[0]),
-        pltpu.make_async_copy(decay_in.at[1, copy], row_box.at[1], cut_load.at[1]),
+        pltpu.make_async_copy(weights_in.at[1, line, core], row_box.at[0], cut_load.at[0]),
+        pltpu.make_async_copy(decay_in.at[1, line, core], row_box.at[1], cut_load.at[1]),
     ]
     for load in cut_loads + k1_loads + d1_loads:
         load.start()
@@ -267,8 +280,29 @@
     x_both[...] = jnp.zeros_like(x_both)
     a_both[...] = jnp.zeros_like(a_both)
     b_both[...] = jnp.zeros_like(b_both)
-    label_box[0] = label_in[...]
-    x_here.wait()
+    label_box[0] = jnp.zeros(label_box.shape[1:], jnp.float32)
+    lane = lax.broadcasted_iota(jnp.int32, (1, LANES), 1)
+
+    def tag_image(image, _):
+        at = part * own_count + image
+        label_box[0, pl.ds(at, 1), :] = (lane == labels[image]).astype(jnp.float32)
+        label_box[0, pl.ds(count + at, 1), :] = jnp.full(
+            (1, LANES), valid_mask[image].astype(jnp.float32)
+        )
+
+    lax.fori_loop(0, own_count, tag_image, None)
+    source_load.wait()
+
+    def crop(image, _):
+        picked, flipped = index_map[image], flip_flags[image]
+        top, left = crop_offsets[image, 0], crop_offsets[image, 1]
+        for cell in range(16):
+            column = left + jnp.where(flipped == 1, 3 - cell % 4, cell % 4)
+            x_box[part, cell, pl.ds(image, 1), :] = source_box[
+                picked, top + cell // 4, pl.ds(column, 1), :
+            ]
+
+    lax.fori_loop(0, own_count, crop, None)
     pl.semaphore_wait(barrier, 10)
 
     def ring_move(box, send, recv, block, step, way, half):
@@ -334,8 +368,8 @@
     partner = row_peer(me ^ copies)
     k1_moves = [
         remote(
-            weights_in.at[0, :, :, pl.ds(tap * channels, channels)],
-            v1.at[tap, own_pieces],
+            weights_in.at[0, :, :, :, pl.ds(tap * channels, channels)],
+            v1.at[tap, member],
             k1_send.at[tap],
             k1_recv.at[tap],
             partner,
@@ -392,7 +426,7 @@
     pair_move.start()
     label_moves = [
         remote(
-            label_in,
+            label_box.at[0],
             label_box.at[step],
             label_send.at[step],
             label_recv.at[step],
@@ -406,12 +440,10 @@
     pair = row_peer(me ^ 1)
 
     def piece_of(which, other):
-        if isinstance(which, int):
-            return v1.at[pl.ds(which * 3, 3), other]
         return v2.at[other, which[0]]
 
     def lane_of(which):
-        return which if isinstance(which, int) else GROUPS + which[0]
+        return which[0]
 
     def to_plane(which, step):
         piece, at = piece_of(which, me), lane_of(which)
@@ -470,8 +502,8 @@
     def each_cell(body, init=None):
         return lax.fori_loop(0, 16, body, init)
 
-    def window(ref, tap, lanes=slice(None)):
-        seen = ref[pl.ds(tap // 3, 4), pl.ds(tap % 3, 4), :, lanes]
+    def window(ref, down, right, lanes=slice(None)):
+        seen = ref[pl.ds(down, 4), right : right + 4, :, lanes]
         return seen.reshape(16 * seen.shape[2], seen.shape[3])
 
     def row(ref, index):
@@ -528,7 +560,7 @@
     def split_one(tap, _):
         for other in range(8):
             at = slice(other * 16, other * 16 + 16)
-            v1_hi[tap, at], v1_lo[tap, at] = halves(v1[tap, other])
+            v1_hi[tap, at], v1_lo[tap, at] = halves(v1[tap, other // 4, other // 2 % 2, other % 2])
 
     def split_two(high, low):
         def body(other, _):
@@ -538,28 +570,35 @@
 
         lax.fori_loop(0, 8, body, None)
 
-    def tap_forward(tap, _):
-        weight = jnp.concatenate([v1_hi[tap], v1_lo[tap]], axis=0)
-        weight = jnp.concatenate([weight, weight], axis=1)
-        out = mul(window(x_both, tap), weight, ((1,), (1,)))
+    def taps_forward(down):
+        left, right = [], []
+        for step in range(3):
+            weight = jnp.concatenate([v1_hi[down * 3 + step], v1_lo[down * 3 + step]], axis=0)
+            left.append(window(x_both, down, step))
+            right += [weight, weight]
+        out = mul(
+            jnp.concatenate(left, axis=1), jnp.concatenate(right, axis=1), ((1,), (1,))
+        )
         flow[...] += (out[:, :LANES] + out[:, LANES:]).reshape(flow.shape)
 
     def part_of_second(maps, high, low, half):
         at = pl.ds(pl.multiple_of(half * 256, 256), 256)
 
-        def body(tap, _):
-            lanes = tap_lanes(tap, LANES)
-            left = window(maps, tap)
-            weight_hi, weight_lo = high[at, lanes], low[at, lanes]
+        def body(down, _):
+            left, right = [], []
+            for step in range(3):
+                lanes = tap_lanes(down * 3 + step, LANES)
+                seen = window(maps, down, step)
+                weight_hi, weight_lo = high[at, lanes], low[at, lanes]
+                left += [seen, seen[:, :LANES]]
+                right += [weight_hi, weight_hi, weight_lo]
             out = mul(
-                jnp.concatenate([left, left], axis=1),
-                jnp.concatenate([weight_hi, weight_hi, weight_lo, weight_lo], axis=1),
-                ((1,), (1,)),
+                jnp.concatenate(left, axis=1), jnp.concatenate(right, axis=1), ((1,), (1,))
             )
             partial[half * 2] += out[:, :LANES].reshape(flow.shape)
             partial[half * 2 + 1] += out[:, LANES:].reshape(flow.shape)
 
-        lax.fori_loop(0, TAPS, body, None)
+        lax.fori_loop(0, 3, body, None)
 
     def up(block, half):
         at = pl.ds(half * 8, 8)
@@ -663,26 +702,37 @@
     def use_block(block, left, turned_block, high, low, maps):
         at = pl.ds(pl.multiple_of(block * LANES, LANES), LANES)
 
-        def body(tap, _):
-            lanes = tap_lanes(tap, LANES)
-            weight = jnp.concatenate([high[at, lanes], low[at, lanes]], axis=1)
-            out = mul(left[...], jnp.concatenate([weight, weight], axis=0))
-            out = out[:, :LANES] + out[:, LANES:]
-            fold_sum[pl.ds(tap // 3, 4), pl.ds(tap % 3, 4)] += out.reshape(4, 4, count, LANES)
-            out = mul(turned_block[...], window(maps, tap))
-            out = (out[:LANES, :LANES] + out[LANES:, :LANES]) + (
-                out[:LANES, LANES:] + out[LANES:, LANES:]
+        def body(down, _):
+            right = []
+            for step in range(3):
+                lanes = tap_lanes(down * 3 + step, LANES)
+                weight = jnp.concatenate([high[at, lanes], low[at, lanes]], axis=1)
+                right.append(jnp.concatenate([weight, weight], axis=0))
+            out = mul(left[...], jnp.concatenate(right, axis=1))
+            for step in range(3):
+                first = 2 * step * LANES
+                fold_sum[pl.ds(down, 4), step : step + 4] += (
+                    out[:, first : first + LANES] + out[:, first + LANES : first + 2 * LANES]
+                ).reshape(4, 4, count, LANES)
+            out = mul(
+                turned_block[...],
+                jnp.concatenate([window(maps, down, step) for step in range(3)], axis=1),
             )
-            sum_two[block, :, :, :, lanes] += out.reshape(4, 2, 16, LANES)
-
-        lax.fori_loop(0, TAPS, body, None)
+            out = out[:LANES] + out[LANES:]
+            for step in range(3):
+                first = 2 * step * LANES
+                sum_two[block, :, :, :, tap_lanes(down * 3 + step, LANES)] += (
+                    out[:, first : first + LANES] + out[:, first + LANES : first + 2 * LANES]
+                ).reshape(4, 2, 16, LANES)
+
+        lax.fori_loop(0, 3, body, None)
 
     def pair_two(block):
         return remote(
             sum_two.at[block, :, 1 - core],
             half_two.at[block],
-            pair_send.at[GROUPS + block],
-            pair_recv.at[GROUPS + block],
+            pair_send.at[block],
+            pair_recv.at[block],
             pair,
         )
 
@@ -691,8 +741,8 @@
         return remote(
             half_two.at[block, other],
             piece_two.at[step, block],
-            plane_send.at[GROUPS + block, step],
-            plane_recv.at[GROUPS + block, step],
+            plane_send.at[block, step],
+            plane_recv.at[block, step],
             row_peer(other * 2 + core),
         )
 
@@ -752,57 +802,150 @@
 
     def pair_one(group):
         return remote(
-            sum_one.at[pl.ds(group * 3, 3), :, 1 - core],
+            sum_one.at[pl.ds(group * 3, 3), :, :, 1 - core],
             half_one.at[pl.ds(group * 3, 3)],
-            pair_send.at[group],
-            pair_recv.at[group],
+            pair_send.at[4 + group],
+            pair_recv.at[4 + group],
             pair,
         )
 
-    def plane_one(group, step):
-        other = place ^ step
-        return remote(
-            half_one.at[pl.ds(group * 3, 3), other],
-            piece_one.at[step, pl.ds(group * 3, 3)],
-            plane_send.at[group, step],
-            plane_recv.at[group, step],
-            row_peer(other * 2 + core),
-        )
+    across_x, across_y = row_peer(me ^ copies), row_peer(me ^ 2)
+    lower, upper = pl.ds(0, channels // 2), pl.ds(channels // 2, channels // 2)
+
+    def taps_of(group):
+        return pl.ds(group * 3, 3)
+
+    def fold_one(group, step):
+        taps = taps_of(group)
+        source, goal, device = (
+            (half_one.at[taps, 1 - member, :, :, lower], first_low.at[taps], across_x),
+            (half_one.at[taps, :, 1 - line, :, upper], first_up.at[taps], across_y),
+            (half_one.at[taps, member, 1 - line, :, lower], second_low.at[taps], across_y),
+            (half_one.at[taps, 1 - member, line, :, upper], second_up.at[taps], across_x),
+        )[step]
+        return remote(source, goal, fold_send.at[group, step], fold_recv.at[group, step], device)
+
+    def spread_one(group, step, arriving=False):
+        taps = taps_of(group)
+        x, y = member, line
+        if arriving:
+            x, y = (x, 1 - y) if step in (0, 3) else (1 - x, y)
+        piece = (
+            v1.at[taps, x, y, core, :, lower],
+            v1.at[taps, x, y, core, :, upper],
+            v1.at[taps, x, :, core, :, lower],
+            v1.at[taps, :, y, core, :, upper],
+        )[step]
+        device = across_y if step in (0, 3) else across_x
+        return remote(piece, piece, open_send.at[group, step], open_recv.at[group, step], device)
+
+    def share_one(group, step, arriving=False):
+        taps = taps_of(group)
+        side = 1 - core if arriving else core
+        piece = (
+            v1.at[taps, member, line, side],
+            v1.at[taps, member, 1 - line, side, :, lower],
+            v1.at[taps, 1 - member, line, side, :, upper],
+            v1.at[taps, 1 - member, :, side, :, lower],
+            v1.at[taps, :, 1 - line, side, :, upper],
+        )[step]
+        return remote(piece, piece, share_send.at[group, step], share_recv.at[group, step], pair)
+
+    def open_first(group):
+        spread_one(group, 0).start()
+        spread_one(group, 1).start()
+        share_one(group, 0).start()
+
+    def open_second(group):
+        spread_one(group, 0, True).wait_recv()
+        spread_one(group, 2).start()
+        spread_one(group, 1, True).wait_recv()
+        spread_one(group, 3).start()
+        share_one(group, 1).start()
+        share_one(group, 2).start()
+
+    def open_third(group):
+        spread_one(group, 2, True).wait_recv()
+        share_one(group, 3).start()
+        spread_one(group, 3, True).wait_recv()
+        share_one(group, 4).start()
+
+    def open_arrived(group):
+        for step in range(5):
+            share_one(group, step, True).wait_recv()
+
+    def open_end(group):
+        for step in range(4):
+            spread_one(group, step).wait_send()
+        for step in range(5):
+            share_one(group, step).wait_send()
+
+    def pair_add(group):
+        pair_one(group).wait()
+
+        def body(tap, _):
+            half_one[tap] += sum_one[tap, :, :, core]
+
+        lax.fori_loop(group * 3, group * 3 + 3, body, None)
+        fold_one(group, 0).start()
+        fold_one(group, 1).start()
+
+    def fold_add(group):
+        fold_one(group, 0).wait()
+        fold_one(group, 1).wait()
+
+        def body(tap, _):
+            half_one[tap, member, :, :, lower] += first_low[tap]
+            half_one[tap, :, line, :, upper] += first_up[tap]
+
+        lax.fori_loop(group * 3, group * 3 + 3, body, None)
+        fold_one(group, 2).start()
+        fold_one(group, 3).start()
 
     def first_gradient():
-        def tap_weight(tap, _):
-            out = mul(turned[...], window(x_both, tap, slice(0, channels)))
-            out = out + mul(turned[...], window(x_both, tap, slice(channels, 2 * channels)))
-            sum_one[tap] = (out[:LANES] + out[LANES:]).reshape(sum_one.shape[1:])
-
-        def plane_go(group):
-            pair_one(group).wait()
-
-            def body(tap, _):
-                for place_of in range(4):
-                    half_one[tap, place_of] += sum_one[tap, place_of, core]
-
-            lax.fori_loop(group * 3, group * 3 + 3, body, None)
-            for step in range(1, 4):
-                plane_one(group, step).start()
+        def taps_weight(down):
+            out = mul(
+                turned[...],
+                jnp.concatenate(
+                    [window(x_both, down, step, slice(0, channels)) for step in range(3)], axis=1
+                ),
+            )
+            out = out + mul(
+                turned[...],
+                jnp.concatenate(
+                    [
+                        window(x_both, down, step, slice(channels, 2 * channels))
+                        for step in range(3)
+                    ],
+                    axis=1,
+                ),
+            )
+            out = out[:LANES] + out[LANES:]
+            for step in range(3):
+                sum_one[down * 3 + step] = out[:, step * channels : (step + 1) * channels].reshape(
+                    sum_one.shape[1:]
+                )
 
         for group in range(GROUPS):
-            lax.fori_loop(group * 3, group * 3 + 3, tap_weight, None)
+            taps_weight(group)
             pair_one(group).start()
             if group > 0:
-                plane_go(group - 1)
-        plane_go(GROUPS - 1)
+                pair_add(group - 1)
+            if group > 1:
+                fold_add(group - 2)
+        pair_add(GROUPS - 1)
+        fold_add(GROUPS - 2)
 
     def step_group(group, new_of):
-        for step in range(1, 4):
-            plane_one(group, step).wait()
+        fold_one(group, 2).wait()
+        fold_one(group, 3).wait()
 
         def body(tap, _):
-            change = (
-                half_one[tap, place] + piece_one[1, tap] + piece_one[2, tap] + piece_one[3, tap]
+            change = half_one[tap, member, line] + jnp.concatenate(
+                [second_low[tap], second_up[tap]], axis=1
             )
-            new = new_of(v1[tap, me], change, d1[tap])
-            v1[tap, me] = new
+            new = new_of(v1[tap, member, line, core], change, d1[tap])
+            v1[tap, member, line, core] = new
             series_one[:, tap_lanes(tap, channels)] += new
 
         lax.fori_loop(group * 3, group * 3 + 3, body, None)
@@ -841,7 +984,7 @@
 
     each_cell(place_images)
     flow[...] = jnp.zeros_like(flow)
-    lax.fori_loop(0, TAPS, tap_forward, None)
+    lax.fori_loop(0, 3, lambda down, _: taps_forward(down), None)
 
     def sums_primal(cell, carry):
         value = flow[cell]
@@ -971,6 +1114,7 @@
 
     first_gradient()
     end_of_two(first_vector, True)
+    fold_add(GROUPS - 1)
     back_forward((order[3],))
 
     def deliver_move(which, source, other):
@@ -1038,23 +1182,34 @@
     deliver_start(0, grad_source)
     for group in range(GROUPS):
         step_group(group, first_vector)
-        back_start(group)
+        open_first(group)
 
     def turn_body(turn, nothing):
+        flow[...] = jnp.zeros_like(flow)
+
+        def forward_group(group):
+            open_arrived(group)
+            lax.fori_loop(group * 3, group * 3 + 3, split_one, None)
+            taps_forward(group)
+
+        open_second(0)
+        open_second(1)
+        open_third(0)
+        open_second(2)
+        forward_group(0)
+        open_third(1)
+        forward_group(1)
+        open_third(2)
+        forward_group(2)
         for group in range(GROUPS):
-            back_forward(group)
-        flow[...] = jnp.zeros_like(flow)
-        for group in range(GROUPS):
-            back_arrived(group)
-            lax.fori_loop(group * 3, group * 3 + 3, split_one, None)
-            lax.fori_loop(group * 3, group * 3 + 3, tap_forward, None)
-        for group in range(GROUPS):
-            back_end(group)
+            open_end(group)
 
         @pl.when(turn == 0)
         def _():
             for tap in range(TAPS):
-                grads[0, :, :, tap * channels : (tap + 1) * channels] = v1[tap, own_pieces]
+                grads[0, :, :, tap * channels : (tap + 1) * channels] = v1[tap, member].reshape(
+                    4, v1.shape[4], channels
+                )
 
         def sums_forward(normal):
             def body(cell, carry):
@@ -1106,7 +1261,10 @@
 
 
         put_sums(1, *sums_forward(n2))
-        total = sum_end(1, 8, sum_start(1, 8)) * inverse
+        moves = sum_start(1, 8)
+        early_logits = mul_exact(pooled[...], move_head[...], ((1,), (1,)))
+        early_block = mul_exact(pull_logits[...], move_head[...])
+        total = sum_end(1, 8, moves) * inverse
         average2, cross2 = total[0:1], total[1:2]
         scale2, gain2 = row(channel, 2), row(channel, 3)
         tan_scale_two = -scale2 * scale2 * cross2
@@ -1121,22 +1279,14 @@
             return carry + s2[cell] * inner
 
         tan_pooled = each_cell(forward_two, zero) * (1.0 / 16.0)
-        tan_logits = sum_parts(
-            mul_exact(tan_pooled, head[...], ((1,), (1,)))
-            + mul_exact(pooled[...], move_head[...], ((1,), (1,)))
-        )
+        tan_logits = sum_parts(mul_exact(tan_pooled, head[...], ((1,), (1,))) + early_logits)
         chance = chances[...]
         tan_pull = (
             weights[...]
             * chance
             * (tan_logits - jnp.sum(chance * tan_logits, axis=1, keepdims=True))
         )
-        out_head = mul_exact(pull_logits[...], tan_pooled, ((0,), (0,))) + mul_exact(
-            tan_pull, pooled[...], ((0,), (0,))
-        )
-        tan_block = (
-            mul_exact(tan_pull, head[...]) + mul_exact(pull_logits[...], move_head[...])
-        ) * (1.0 / 16.0)
+        tan_block = (mul_exact(tan_pull, head[...]) + early_block) * (1.0 / 16.0)
 
         def back_two(cell, carry):
             tangent = tan_block * s2[cell] + pb2[cell] * in2[cell]
@@ -1147,10 +1297,13 @@
             )
 
         put_sums(2, *each_cell(back_two, (zero, zero)))
-        stats_own[2, 8:24, :] = out_head[0:16]
-        total = sum_end(2, 24, sum_start(2, 24))
+        moves = sum_start(2, 8)
+        out_head = mul_exact(pull_logits[...], tan_pooled, ((0,), (0,))) + mul_exact(
+            tan_pull, pooled[...], ((0,), (0,))
+        )
+        stats_own[3, 8:24, :] = out_head[0:16]
+        total = sum_end(2, 8, moves)
         out_gain2, out_shift2 = total[0:1], total[1:2]
-        move_head[0:16] = move_head[0:16] - neumann_rate * total[8:24]
         factor2 = scale2 * gain2
         tan_factor2 = tan_scale_two * gain2 + scale2 * move_gain2
 
@@ -1181,9 +1334,10 @@
             )
 
         put_sums(3, *each_cell(back_one, (zero, zero)))
-        moves = sum_start(3, 8)
+        moves = sum_start(3, 24)
         rest_of_two(next_vector, more)
-        total = sum_end(3, 8, moves)
+        total = sum_end(3, 24, moves)
+        move_head[0:16] = move_head[0:16] - neumann_rate * total[8:24]
         out_gain, out_shift = total[0:1], total[1:2]
         factor = scale * gain
         tan_factor = tan_scale_one * gain + scale * move_gain
@@ -1204,6 +1358,7 @@
         move_norm[3:4, :] = move_shift2 - neumann_rate * out_shift2
         first_gradient()
         end_of_two(next_vector, more)
+        fold_add(GROUPS - 1)
         back_forward_when(order[3], more)
 
         @pl.when(turn == NEUMANN - 1)
@@ -1215,7 +1370,7 @@
 
             @pl.when(more)
             def _():
-                back_start(group)
+                open_first(group)
 
     lax.fori_loop(0, NEUMANN, turn_body, None)
 
@@ -1230,31 +1385,46 @@
     spread_end(2, series.at[1])
 
 
-def step_fused(links, rows, images, conv_weights, decay_rates, norm_params, head_weights, labels, valid):
-    own_count, channels = images.shape[2:]
+def step_fused(
+    links,
+    rows,
+    source,
+    index_map,
+    crop_offsets,
+    flip_flags,
+    labels,
+    valid_mask,
+    conv_weights,
+    norm_params,
+    head_weights,
+    decay_rates,
+):
+    own_count, channels = source.shape[0], source.shape[3]
     cells, count = MAP * MAP, own_count * 4
     width, group = channels // 4, 8
     piece, block = width // group, channels // group
     classes = head_weights.shape[1]
     f32, b16 = jnp.float32, jnp.bfloat16
-
-    small = jnp.zeros((24, width), f32)
+    small = jnp.concatenate(
+        [
+            norm_params,
+            jnp.zeros((4, block), f32),
+            head_weights.T,
+            jnp.zeros((16 - classes, block), f32),
+        ]
+    )
     lane = links.member * block
-    small = lax.dynamic_update_slice(small, norm_params, (0, lane))
-    small = lax.dynamic_update_slice(small, head_weights.T, (8, lane))
-    chosen = (labels[:, None] == jnp.arange(LANES, dtype=jnp.int32)[None, :]).astype(f32)
-    tags = jnp.zeros((2, count, LANES), f32)
-    tags = lax.dynamic_update_slice(
-        tags,
-        jnp.stack([chosen, jnp.broadcast_to(valid[:, None], chosen.shape)]),
-        (0, links.part * own_count, 0),
-    )
+    here = jnp.arange(2, dtype=jnp.int32)[None, :, None] == links.member
     operands = (
-        images.reshape(cells, own_count, channels),
-        conv_weights.reshape(2, 4, piece, TAPS * channels),
-        decay_rates.reshape(2, 4, piece, TAPS * channels),
-        small,
-        tags.reshape(2 * count, LANES),
+        source,
+        index_map,
+        crop_offsets,
+        flip_flags,
+        labels,
+        valid_mask,
+        conv_weights.reshape(2, 2, 2, piece, TAPS * channels),
+        decay_rates.reshape(2, 2, 2, piece, TAPS * channels),
+        jnp.where(here, small[:, None, :], 0.0).reshape(24, width),
     )
     vmem = pl.BlockSpec(memory_space=pltpu.VMEM)
     anywhere = pl.BlockSpec(memory_space=pl.ANY)
@@ -1276,7 +1446,7 @@
         pltpu.VMEM((2, 4, piece, TAPS * width), f32),
         pltpu.VMEM((TAPS, piece, channels), f32),
         inner_piece,
-        pltpu.VMEM((TAPS, group, piece, channels), f32),
+        pltpu.VMEM((TAPS, 2, 2, 2, piece, channels), f32),
         pltpu.VMEM((group, 4, piece, TAPS * width), f32),
         outer_part,
         outer_part,
@@ -1284,6 +1454,7 @@
         inner_part,
         inner_part,
         inner_part,
+        pltpu.VMEM(source.shape, f32),
         pltpu.VMEM((4, cells, own_count, channels), f32),
         pltpu.VMEM((count, channels), f32),
         pltpu.VMEM((MAP + 2, MAP + 2, count, 2 * channels), b16),
@@ -1300,11 +1471,12 @@
         four_maps,
         *[row_map] * 15,
         pltpu.VMEM((MAP + 2, MAP + 2, count, width), f32),
-        pltpu.VMEM((TAPS, 4, 2, piece, channels), f32),
+        pltpu.VMEM((TAPS, 2, 2, 2, piece, channels), f32),
         pltpu.VMEM((4, 4, 2, piece, TAPS * width), f32),
-        pltpu.VMEM((TAPS, 4, piece, channels), f32),
+        pltpu.VMEM((TAPS, 2, 2, piece, channels), f32),
         inner_half,
-        pltpu.VMEM((4, TAPS, piece, channels), f32),
+        *[pltpu.VMEM((TAPS, 2, piece, channels // 2), f32)] * 2,
+        *[pltpu.VMEM((TAPS, piece, channels // 2), f32)] * 2,
         inner_half,
         pltpu.VMEM((4, 8, 24, width), f32),
         pltpu.VMEM((4, 24, width), f32),
@@ -1346,12 +1518,18 @@
         dma((4, 2)),
         dma((GROUPS + 4,)),
         dma((GROUPS + 4,)),
-        dma((GROUPS + 4, 4)),
-        dma((GROUPS + 4, 4)),
-        dma((GROUPS + 4, 4)),
-        dma((GROUPS + 4, 4)),
-        dma((GROUPS + 4, 4)),
-        dma((GROUPS + 4, 4)),
+        dma((4, 4)),
+        dma((4, 4)),
+        dma((4, 4)),
+        dma((4, 4)),
+        dma((4, 4)),
+        dma((4, 4)),
+        dma((GROUPS, 4)),
+        dma((GROUPS, 4)),
+        dma((GROUPS, 4)),
+        dma((GROUPS, 4)),
+        dma((GROUPS, 5)),
+        dma((GROUPS, 5)),
         dma((2, 4)),
         dma((2, 4)),
         dma((3, 3)),
@@ -1361,7 +1539,7 @@
     grads, series, grad_small = pl.pallas_call(
         functools.partial(step_kernel, rows, links.members, links.copies, classes),
         out_shape=(result, result, jax.ShapeDtypeStruct((32, width), f32)),
-        in_specs=[anywhere] * 3 + [vmem] * 2,
+        in_specs=[anywhere] + [pl.BlockSpec(memory_space=pltpu.SMEM)] * 5 + [anywhere] * 2 + [vmem],
         out_specs=(vmem,) * 3,
         scratch_shapes=scratch,
         compiler_params=pltpu.CompilerParams(
@@ -1470,8 +1648,22 @@
 
 
 def step_general(
-    links, rows, images, conv_weights, decay_rates, norm_params, head_weights, labels, valid
+    links,
+    rows,
+    source,
+    index_map,
+    crop_offsets,
+    flip_flags,
+    labels,
+    valid_mask,
+    conv_weights,
+    norm_params,
+    head_weights,
+    decay_rates,
 ):
+    images = jax.vmap(crop_image)(source[index_map], crop_offsets, flip_flags)
+    images = images.transpose(1, 2, 0, 3)
+    valid = valid_mask.astype(jnp.float32)
     own_images, channels = images.shape[2:]
     count = own_images * links.parts
     width = channels // links.parts
@@ -1660,22 +1852,22 @@
 ):
     links = Links()
     rows = float(source.shape[0] * MAP * MAP * links.shards * links.copies)
-    picked = source[index_map]
-    images = jax.vmap(crop_image)(picked, crop_offsets, flip_flags)
-    images = images.transpose(1, 2, 0, 3)
-    fused = links.members * links.copies == 8 and links.parts == 4
+    fused = links.members * links.copies == 8 and links.members == 2 and links.parts == 4
     loss_sum, label_total, grads, grad_norm, grad_head, series = (
         step_fused if fused else step_general
     )(
         links,
         rows,
-        images,
+        source,
+        index_map,
+        crop_offsets,
+        flip_flags,
+        labels,
+        valid_mask,
         conv_weights,
-        decay_rates,
         norm_params,
         head_weights,
-        labels,
-        valid_mask.astype(jnp.float32),
+        decay_rates,
     )
     hyper_gradient = -neumann_rate * conv_weights * series
     conv_new, conv_one, conv_two = adamw(conv_weights, grads, conv_first, conv_second, 0.015)

time: 651 us -> 605 us (0.929)
  Pallas kernels: 628 us -> 589 us
    pallas_call x1, Pallas kernels: 628 us -> 589 us  [step_fused(): pl.pallas_call(functools.partial(step_kernel, rows, links.members, links....]
where the time goes in v5:
time: 605 us; the launch traced here: 604 us
  Pallas kernels  589 us (97%)
  other arithmetic  12.4 us (2%)
    pallas_call x1, Pallas kernels, step_fused(): pl.pallas_call(functools.partial(step_kernel, rows, links.members, links....  589 us

profile of v5, /device:TPU:0, one launch (start us, length us, event | category | flops | bytes accessed | tf_op | source)
XLA Modules:
  0.0 604.4 jit_solution(2288062126038716601)
XLA Ops:
  0.7 0.1 broadcast_in_dim.34
  0.7 0.1 broadcast_in_dim.35
  0.8 0.1 pad.1.clone
  0.9 0.1 pad.3.clone
  1.0 0.8 maximum_maximum_fusion
  1.8 0.1 broadcast_in_dim.40
  1.9 0.6 broadcast_select_fusion.pair_in
  2.5 1.4 copy.28.crop_offsets
  3.8 589.0 %train_step.1 = (f32[2,4,16,4608]{3,2,1,0:T(8,128)}, f32[2,4,16,4608]{3,2,1,0:T(8,128)}, f32[32,128]{1,0:T(8,128)}) custom-call(f32[12,6,6,512]{3,2,1,0:T(8,128)} %source.1, s32[12]{0:T(128)} %index_map.1, s32[12,2]{1,0:T(8,128)} %copy.28.crop_offsets, s32[12]{0:T(128)} %flip_flags.1, s32[12]{0:T(128)} %labels.1, s32[12]{0:T(128)} %valid_mask.1, ...), custom_call_target="tpu_custom_call" | custom-call | tf_op jit(solution)/shard_map/train_step/pallas_call | solution.py:1539
  592.8 0.0 copy-start
  592.8 0.0 copy-start.1
  592.8 0.0 copy-start.2
  592.8 0.0 copy-start.4
  592.8 0.0 copy-start.3
  592.8 0.0 copy-start.5
  592.9 0.0 copy-start.6
  592.9 9.6 %multiply_subtract_fusion = (f32[2,64,4608]{2,1,0:T(8,128)}, f32[2,64,4608]{2,1,0:T(8,128)}, f32[2,64,4608]{2,1,0:T(8,128)}, f32[2,64,4608]{2,1,0:T(8,128)}) fusion(f32[2,64,4608]{2,1,0:T(8,128)} %param.22, f32[2,4,16,4608]{3,2,1,0:T(8,128)} %get-tuple-element.16, f32[2,64,4608]{2,1,0:T(8,128)} %param.26, f32[2,64,4608]{2,1,0:T(8,128)} %param.27, ...), kind=kLoop, calls=%fused_computation.4 | loop fusion | flops 9437184 | bytes 21233664 | tf_op jit(solution)/shard_map/sub | solution.py:1567
  602.5 0.0 copy-done
  602.5 0.0 copy-done.1
  602.5 0.0 copy-done.2
  602.5 0.0 copy-done.4
  602.5 0.7 multiply_subtract_fusion.1
  603.2 0.0 copy-done.3
  603.2 0.0 copy-done.5
  603.2 0.0 copy-done.6
  603.2 0.7 multiply_subtract_fusion.2
  603.9 0.5 fusion.6
  (4 shorter events, 0.0 us)
Async XLA Ops:
  592.8 9.7 %copy-start = (f32[64,10]{0,1:T(8,128)S(1)}, f32[64,10]{0,1:T(8,128)}, u32[]{:S(2)}) copy-start(f32[64,10]{0,1:T(8,128)} %param.24) | copy-start | bytes 7684
  592.8 9.7 %copy-start.1 = (f32[64,10]{0,1:T(8,128)S(1)}, f32[64,10]{0,1:T(8,128)}, u32[]{:S(2)}) copy-start(f32[64,10]{0,1:T(8,128)} %param.30) | copy-start | bytes 7684
  592.8 9.7 %copy-start.2 = (f32[64,10]{0,1:T(8,128)S(1)}, f32[64,10]{0,1:T(8,128)}, u32[]{:S(2)}) copy-start(f32[64,10]{0,1:T(8,128)} %param.31) | copy-start | bytes 7684
  592.8 9.7 %copy-start.4 = (f32[32,128]{1,0:T(8,128)S(1)}, f32[32,128]{1,0:T(8,128)}, u32[]{:S(2)}) copy-start(f32[32,128]{1,0:T(8,128)} %get-tuple-element.15) | copy-start | bytes 49156
  592.8 10.4 %copy-start.3 = (f32[4,64]{1,0:T(4,128)S(1)}, f32[4,64]{1,0:T(4,128)}, u32[]{:S(2)}) copy-start(f32[4,64]{1,0:T(4,128)} %param.23) | copy-start | bytes 3076
  592.8 10.4 %copy-start.5 = (f32[4,64]{1,0:T(4,128)S(1)}, f32[4,64]{1,0:T(4,128)}, u32[]{:S(2)}) copy-start(f32[4,64]{1,0:T(4,128)} %param.28) | copy-start | bytes 3076
  592.9 10.4 %copy-start.6 = (f32[4,64]{1,0:T(4,128)S(1)}, f32[4,64]{1,0:T(4,128)}, u32[]{:S(2)}) copy-start(f32[4,64]{1,0:T(4,128)} %param.29) | copy-start | bytes 3076

commit v6 on v5

--- a/solution.py
+++ b/solution.py
@@ -177,6 +177,8 @@
     d1_load,
     k1_send,
     k1_recv,
+    half_send,
+    half_recv,
     first_send,
     first_recv,
     label_send,
@@ -303,6 +305,17 @@
             ]
 
     lax.fori_loop(0, own_count, crop, None)
+    for load in cut_loads:
+        load.wait()
+    for which in range(2):
+        for other in range(4):
+            for tap in range(TAPS):
+                start = tap * channels + other * LANES
+                cut_box[which, other, :, tap * LANES : (tap + 1) * LANES] = row_box[
+                    which, :, start : start + LANES
+                ]
+    v2[me, part] = cut_box[0, part]
+    d2[part] = cut_box[1, part]
     pl.semaphore_wait(barrier, 10)
 
     def ring_move(box, send, recv, block, step, way, half):
@@ -364,21 +377,6 @@
         jnp.where(part < 2, 3, 0),
     )
 
-    ring_start(x_box, x_send, x_recv)
-    partner = row_peer(me ^ copies)
-    k1_moves = [
-        remote(
-            weights_in.at[0, :, :, :, pl.ds(tap * channels, channels)],
-            v1.at[tap, member],
-            k1_send.at[tap],
-            k1_recv.at[tap],
-            partner,
-        )
-        for tap in range(TAPS)
-    ]
-    for move in k1_moves:
-        move.start()
-
     def cut_move(which, other):
         box = v2.at[me, part] if which == 0 else d2.at[part]
         return remote(
@@ -391,21 +389,10 @@
 
     def cut_start(which):
         for other in range(4):
-            for tap in range(TAPS):
-                start = tap * channels + other * LANES
-                cut_box[which, other, :, tap * LANES : (tap + 1) * LANES] = row_box[
-                    which, :, start : start + LANES
-                ]
-        for other in range(4):
 
             @pl.when(part != other)
             def _():
                 cut_move(which, other).start()
-
-        if which == 0:
-            v2[me, part] = cut_box[which, part]
-        else:
-            d2[part] = cut_box[which, part]
 
     def cut_end(which):
         for other in range(4):
@@ -422,6 +409,27 @@
                     part_peer(other),
                 ).wait_recv()
 
+    pair = row_peer(me ^ 1)
+    cut_start(0)
+    ring_start(x_box, x_send, x_recv)
+    partner = row_peer(me ^ copies)
+    k1_moves = [
+        remote(
+            weights_in.at[0, :, core, :, pl.ds(tap * channels, channels)],
+            v1.at[tap, member, :, core],
+            k1_send.at[tap],
+            k1_recv.at[tap],
+            partner,
+        )
+        for tap in range(TAPS)
+    ]
+    for move in k1_moves:
+        move.start()
+
+    def k1_share(group, arriving=False):
+        piece = v1.at[pl.ds(group * 3, 3), 1 - member, :, 1 - core if arriving else core]
+        return remote(piece, piece, half_send.at[group], half_recv.at[group], pair)
+
     pair_move = remote(pair_in, pair_box, pair_sem.at[0], pair_sem.at[1], partner)
     pair_move.start()
     label_moves = [
@@ -437,7 +445,7 @@
     for move in label_moves:
         move.start()
 
-    pair = row_peer(me ^ 1)
+    cut_start(1)
 
     def piece_of(which, other):
         return v2.at[other, which[0]]
@@ -483,11 +491,10 @@
         for step in range(0, 4):
             to_pair(which, step).wait_send()
 
-    for load in cut_loads:
-        load.wait()
-    cut_start(0)
+    cut_end(0)
+    for block in range(4):
+        back_start((block,))
     ring_step(x_box, x_send, x_recv, 1)
-    cut_start(1)
     pair_move.wait()
     small = pair_in[...] + pair_box[...]
     move_norm[...] = small[0:8]
@@ -502,9 +509,12 @@
     def each_cell(body, init=None):
         return lax.fori_loop(0, 16, body, init)
 
-    def window(ref, down, right, lanes=slice(None)):
-        seen = ref[pl.ds(down, 4), right : right + 4, :, lanes]
-        return seen.reshape(16 * seen.shape[2], seen.shape[3])
+    def window(ref, down, right, lanes=slice(None), first=0, after=4):
+        seen = ref[pl.ds(down + first, after - first), right : right + 4, :, lanes]
+        return seen.reshape(4 * (after - first) * seen.shape[2], seen.shape[3])
+
+    def reach(down):
+        return (1 if down == 0 else 0), (3 if down == 2 else 4)
 
     def row(ref, index):
         return ref[index : index + 1, :]
@@ -570,35 +580,39 @@
 
         lax.fori_loop(0, 8, body, None)
 
-    def taps_forward(down):
+    def taps_forward(row_of_taps):
         left, right = [], []
         for step in range(3):
-            weight = jnp.concatenate([v1_hi[down * 3 + step], v1_lo[down * 3 + step]], axis=0)
-            left.append(window(x_both, down, step))
+            tap = row_of_taps * 3 + step
+            weight = jnp.concatenate([v1_hi[tap], v1_lo[tap]], axis=0)
+            left.append(window(x_both, row_of_taps, step))
             right += [weight, weight]
-        out = mul(
-            jnp.concatenate(left, axis=1), jnp.concatenate(right, axis=1), ((1,), (1,))
-        )
+        out = mul(jnp.concatenate(left, axis=1), jnp.concatenate(right, axis=1), ((1,), (1,)))
         flow[...] += (out[:, :LANES] + out[:, LANES:]).reshape(flow.shape)
 
-    def part_of_second(maps, high, low, half):
+    def part_of_second(maps, high, low, half, add):
         at = pl.ds(pl.multiple_of(half * 256, 256), 256)
 
-        def body(down, _):
+        for row_of_taps in (1, 0, 2):
             left, right = [], []
+            first, after = reach(row_of_taps)
             for step in range(3):
-                lanes = tap_lanes(down * 3 + step, LANES)
-                seen = window(maps, down, step)
+                tap = row_of_taps * 3 + step
+                lanes = slice(tap * LANES, (tap + 1) * LANES)
+                seen = window(maps, row_of_taps, step, slice(None), first, after)
                 weight_hi, weight_lo = high[at, lanes], low[at, lanes]
                 left += [seen, seen[:, :LANES]]
                 right += [weight_hi, weight_hi, weight_lo]
             out = mul(
                 jnp.concatenate(left, axis=1), jnp.concatenate(right, axis=1), ((1,), (1,))
             )
-            partial[half * 2] += out[:, :LANES].reshape(flow.shape)
-            partial[half * 2 + 1] += out[:, LANES:].reshape(flow.shape)
-
-        lax.fori_loop(0, 3, body, None)
+            lines = slice(first * 4, after * 4)
+            for side in range(2):
+                value = out[:, side * LANES : (side + 1) * LANES].reshape(-1, count, LANES)
+                if add or row_of_taps != 1:
+                    partial[half * 2 + side, lines] += value
+                else:
+                    partial[half * 2 + side, lines] = value
 
     def up(block, half):
         at = pl.ds(half * 8, 8)
@@ -620,23 +634,25 @@
             part_peer(part - 1),
         )
 
-    def scatter(maps, high, low, aside):
+    def scatter(maps, high, low, add, aside):
         near = jnp.where(part < 2, 1, 0)
-        part_of_second(maps, high, low, near)
-
-        @pl.when(part == 0)
-        def _():
-            for block in (3, 2):
-                for half in range(2):
-                    up(block, half).start()
-
-        @pl.when(part == last)
-        def _():
-            for block in (0, 1):
-                for half in range(2):
-                    down(block, half).start()
-
-        part_of_second(maps, high, low, 1 - near)
+
+        def half_body(index, _):
+            part_of_second(maps, high, low, jnp.where(index == 0, near, 1 - near), add)
+
+            @pl.when((index == 0) & (part == 0))
+            def _():
+                for block in (3, 2):
+                    for half in range(2):
+                        up(block, half).start()
+
+            @pl.when((index == 0) & (part == last))
+            def _():
+                for block in (0, 1):
+                    for half in range(2):
+                        down(block, half).start()
+
+        lax.fori_loop(0, 2, half_body, None)
         for block in (3, 2, 1):
             goal = last - block
 
@@ -665,8 +681,7 @@
                     def _():
                         down(2, half).start()
 
-            aside(3 - block)
-        aside(3)
+        aside()
         for block in range(4):
 
             @pl.when(part == block)
@@ -702,30 +717,31 @@
     def use_block(block, left, turned_block, high, low, maps):
         at = pl.ds(pl.multiple_of(block * LANES, LANES), LANES)
 
-        def body(down, _):
+        for down in range(3):
             right = []
-            for step in range(3):
-                lanes = tap_lanes(down * 3 + step, LANES)
+            first, after = reach(down)
+            taps = [slice((down * 3 + step) * LANES, (down * 3 + step + 1) * LANES) for step in range(3)]
+            for lanes in taps:
                 weight = jnp.concatenate([high[at, lanes], low[at, lanes]], axis=1)
                 right.append(jnp.concatenate([weight, weight], axis=0))
-            out = mul(left[...], jnp.concatenate(right, axis=1))
+            out = mul(
+                left[first * 4 * count : after * 4 * count], jnp.concatenate(right, axis=1)
+            )
             for step in range(3):
-                first = 2 * step * LANES
-                fold_sum[pl.ds(down, 4), step : step + 4] += (
-                    out[:, first : first + LANES] + out[:, first + LANES : first + 2 * LANES]
-                ).reshape(4, 4, count, LANES)
+                start = 2 * step * LANES
+                fold_sum[down + first : down + after, step : step + 4] += (
+                    out[:, start : start + LANES] + out[:, start + LANES : start + 2 * LANES]
+                ).reshape(after - first, 4, count, LANES)
             out = mul(
                 turned_block[...],
                 jnp.concatenate([window(maps, down, step) for step in range(3)], axis=1),
             )
             out = out[:LANES] + out[LANES:]
-            for step in range(3):
-                first = 2 * step * LANES
-                sum_two[block, :, :, :, tap_lanes(down * 3 + step, LANES)] += (
-                    out[:, first : first + LANES] + out[:, first + LANES : first + 2 * LANES]
+            for step, lanes in enumerate(taps):
+                start = 2 * step * LANES
+                sum_two[block, :, :, :, lanes] += (
+                    out[:, start : start + LANES] + out[:, start + LANES : start + 2 * LANES]
                 ).reshape(4, 2, 16, LANES)
-
-        lax.fori_loop(0, 3, body, None)
 
     def pair_two(block):
         return remote(
@@ -772,33 +788,36 @@
 
     def gather_and_use(block_of, new_of, more):
         ring_start(slots, ring_send, ring_recv)
-        block_of(order[0])
-        pair_two(order[0]).start()
-        ring_step(slots, ring_send, ring_recv, 1)
-        block_of(order[1])
-        pair_two(order[1]).start()
-        plane_two_go(order[0])
-        ring_step(slots, ring_send, ring_recv, 2)
-        step_two(order[0], new_of, more)
-        block_of(order[2])
-        pair_two(order[2]).start()
-        plane_two_go(order[1])
-        ring_step(slots, ring_send, ring_recv, 3)
+
+        def order_at(index):
+            first = jnp.where(index == 0, order[0], order[1])
+            return jnp.where(index < 2, first, jnp.where(index == 2, order[2], order[3]))
+
+        def body(index, _):
+            @pl.when(index > 0)
+            def _():
+                ring_step(slots, ring_send, ring_recv, index)
+
+            @pl.when(index == 2)
+            def _():
+                step_two(order[0], new_of, more)
+
+            block = order_at(index)
+            block_of(block)
+            pair_two(block).start()
+
+            @pl.when((index == 1) | (index == 2))
+            def _():
+                plane_two_go(order_at(index - 1))
+
+        lax.fori_loop(0, 4, body, None)
+
+    def beside_sums(new_of, more):
         step_two(order[1], new_of, more)
-        block_of(order[3])
-        pair_two(order[3]).start()
         plane_two_go(order[2])
         back_forward_when(order[0], more)
         ring_end(slots, ring_send, ring_recv)
-
-    def rest_of_two(new_of, more):
         plane_two_go(order[3])
-        step_two(order[2], new_of, more)
-        back_forward_when(order[1], more)
-
-    def end_of_two(new_of, more):
-        step_two(order[3], new_of, more)
-        back_forward_when(order[2], more)
 
     def pair_one(group):
         return remote(
@@ -902,7 +921,7 @@
         fold_one(group, 2).start()
         fold_one(group, 3).start()
 
-    def first_gradient():
+    def first_gradient(new_of, more):
         def taps_weight(down):
             out = mul(
                 turned[...],
@@ -926,15 +945,28 @@
                     sum_one.shape[1:]
                 )
 
-        for group in range(GROUPS):
+        def body(group, _):
             taps_weight(group)
             pair_one(group).start()
-            if group > 0:
+
+            @pl.when(group == 0)
+            def _():
+                step_two(order[2], new_of, more)
+
+            @pl.when(group > 0)
+            def _():
                 pair_add(group - 1)
-            if group > 1:
+
+            @pl.when(group > 1)
+            def _():
                 fold_add(group - 2)
+
+        lax.fori_loop(0, GROUPS, body, None)
         pair_add(GROUPS - 1)
+        back_forward_when(order[1], more)
         fold_add(GROUPS - 2)
+        step_two(order[3], new_of, more)
+        fold_add(GROUPS - 1)
 
     def step_group(group, new_of):
         fold_one(group, 2).wait()
@@ -950,7 +982,7 @@
 
         lax.fori_loop(group * 3, group * 3 + 3, body, None)
 
-    def no_aside(index):
+    def no_aside():
         pass
 
     series_one[...] = jnp.zeros_like(series_one)
@@ -964,13 +996,18 @@
 
     for load in k1_loads + d1_loads:
         load.wait()
-    for move in k1_moves:
-        move.wait()
-    lax.fori_loop(0, TAPS, split_one, None)
+    for group in range(GROUPS):
+        for move in k1_moves[group * 3 : group * 3 + 3]:
+            move.wait()
+        k1_share(group).start()
     ring_step(x_box, x_send, x_recv, 2)
-    cut_end(0)
     for block in range(4):
-        back_start((block,))
+        back_forward((block,))
+    for group in range(GROUPS):
+        k1_share(group, True).wait_recv()
+        lax.fori_loop(group * 3, group * 3 + 3, split_one, None)
+    for group in range(GROUPS):
+        k1_share(group).wait_send()
     ring_step(x_box, x_send, x_recv, 3)
     ring_end(x_box, x_send, x_recv)
 
@@ -984,7 +1021,7 @@
 
     each_cell(place_images)
     flow[...] = jnp.zeros_like(flow)
-    lax.fori_loop(0, 3, lambda down, _: taps_forward(down), None)
+    lax.fori_loop(0, 3, lambda row_of_taps, _: taps_forward(row_of_taps), None)
 
     def sums_primal(cell, carry):
         value = flow[cell]
@@ -993,14 +1030,11 @@
     put_sums(0, *each_cell(sums_primal, (zero, zero)))
     stats_own[0, 2:3, :] = jnp.sum(valid, axis=0, keepdims=True)
     moves = sum_start(0, 8)
-    for block in range(4):
-        back_forward((block,))
     cut_end(1)
     for block in range(4):
         back_arrived((block,))
         back_end((block,))
     split_two(k_hi, k_lo)
-    partial[...] = jnp.zeros_like(partial)
     total = sum_end(0, 8, moves)
     label_total = total[2:3]
     average = total[0:1] * inverse
@@ -1017,7 +1051,7 @@
         a_both[cell // 4 + 1, cell % 4 + 1] = jnp.concatenate(halves(value), axis=1)
 
     each_cell(first_primal)
-    scatter(a_both, k_hi, k_lo, no_aside)
+    scatter(a_both, k_hi, k_lo, False, no_aside)
     put_sums(1, *each_cell(sums_primal, (zero, zero)))
     total = sum_end(1, 8, sum_start(1, 8))
     average = total[0:1] * inverse
@@ -1086,7 +1120,7 @@
 
     put_sums(3, *each_cell(back_one_primal, (zero, zero)))
     moves = sum_start(3, 8)
-    rest_of_two(first_vector, True)
+    beside_sums(first_vector, True)
     total = sum_end(3, 8, moves)
     out_gain, out_shift = total[0:1], total[1:2]
     factor = scale * gain
@@ -1112,10 +1146,7 @@
     grad_small[8:16, :] = move_norm[...]
     move_head[0:16] = grad_small[16:32, :]
 
-    first_gradient()
-    end_of_two(first_vector, True)
-    fold_add(GROUPS - 1)
-    back_forward((order[3],))
+    first_gradient(first_vector, True)
 
     def deliver_move(which, source, other):
         return remote(
@@ -1187,20 +1218,34 @@
     def turn_body(turn, nothing):
         flow[...] = jnp.zeros_like(flow)
 
-        def forward_group(group):
+        def forward_group(group, _):
             open_arrived(group)
             lax.fori_loop(group * 3, group * 3 + 3, split_one, None)
             taps_forward(group)
 
+        fold_sum[...] = jnp.zeros_like(fold_sum)
+        sum_two[...] = jnp.zeros_like(sum_two)
         open_second(0)
         open_second(1)
+        back_forward((order[2],))
+        back_forward((order[3],))
+        for block in range(4):
+            back_arrived((block,))
+            back_end((block,))
+        split_two(v2_hi, v2_lo)
         open_third(0)
         open_second(2)
-        forward_group(0)
-        open_third(1)
-        forward_group(1)
-        open_third(2)
-        forward_group(2)
+
+        def vector_half(half, _):
+            part_of_second(a_both, v2_hi, v2_lo, half, False)
+
+            @pl.when(half == 0)
+            def _():
+                open_third(1)
+                open_third(2)
+
+        lax.fori_loop(0, 2, vector_half, None)
+        lax.fori_loop(0, GROUPS, forward_group, None)
         for group in range(GROUPS):
             open_end(group)
 
@@ -1220,15 +1265,6 @@
 
         put_sums(0, *sums_forward(n1))
         moves = sum_start(0, 8)
-        partial[...] = jnp.zeros_like(partial)
-        fold_sum[...] = jnp.zeros_like(fold_sum)
-        sum_two[...] = jnp.zeros_like(sum_two)
-        for block in range(4):
-            back_arrived((block,))
-            back_end((block,))
-        split_two(v2_hi, v2_lo)
-        part_of_second(a_both, v2_hi, v2_lo, 0)
-        part_of_second(a_both, v2_hi, v2_lo, 1)
         total = sum_end(0, 8, moves) * inverse
         average, cross = total[0:1], total[1:2]
         scale, gain = row(channel, 0), row(channel, 1)
@@ -1245,10 +1281,13 @@
 
         each_cell(forward_one)
 
-        def aside(block):
-            use_block(block, g_left.at[block], g_turned.at[block], v2_hi, v2_lo, b_both)
-
-        scatter(b_both, k_hi, k_lo, aside)
+        def aside():
+            def body(block, _):
+                use_block(block, g_left.at[block], g_turned.at[block], v2_hi, v2_lo, b_both)
+
+            lax.fori_loop(0, 4, body, None)
+
+        scatter(b_both, k_hi, k_lo, True, aside)
 
         @pl.when(turn == 0)
         def _():
@@ -1335,7 +1374,7 @@
 
         put_sums(3, *each_cell(back_one, (zero, zero)))
         moves = sum_start(3, 24)
-        rest_of_two(next_vector, more)
+        beside_sums(next_vector, more)
         total = sum_end(3, 24, moves)
         move_head[0:16] = move_head[0:16] - neumann_rate * total[8:24]
         out_gain, out_shift = total[0:1], total[1:2]
@@ -1356,10 +1395,7 @@
         move_norm[1:2, :] = move_shift - neumann_rate * out_shift
         move_norm[2:3, :] = move_gain2 - neumann_rate * out_gain2
         move_norm[3:4, :] = move_shift2 - neumann_rate * out_shift2
-        first_gradient()
-        end_of_two(next_vector, more)
-        fold_add(GROUPS - 1)
-        back_forward_when(order[3], more)
+        first_gradient(next_vector, more)
 
         @pl.when(turn == NEUMANN - 1)
         def _():
@@ -1500,6 +1536,8 @@
         dma((TAPS,)),
         dma((TAPS,)),
         dma((TAPS,)),
+        dma((GROUPS,)),
+        dma((GROUPS,)),
         dma((2, 4)),
         dma((2, 4)),
         dma((4,)),

time: 605 us -> 573 us (0.947)
  Pallas kernels: 589 us -> 557 us
    pallas_call x1, Pallas kernels: 589 us -> 557 us  [step_fused(): pl.pallas_call(functools.partial(step_kernel, rows, links.members, links....]
where the time goes in v6:
time: 573 us; the launch traced here: 572 us
  Pallas kernels  557 us (97%)
  other arithmetic  12.4 us (2%)
    pallas_call x1, Pallas kernels, step_fused(): pl.pallas_call(functools.partial(step_kernel, rows, links.members, links....  557 us

profile of v6, /device:TPU:0, one launch (start us, length us, event | category | flops | bytes accessed | tf_op | source)
XLA Modules:
  0.0 572.4 jit_solution(5556927666280459322)
XLA Ops:
  0.7 0.1 broadcast_in_dim.34
  0.7 0.1 broadcast_in_dim.35
  0.8 0.1 pad.1.clone
  0.9 0.1 pad.3.clone
  1.0 0.8 maximum_maximum_fusion
  1.8 0.1 broadcast_in_dim.40
  1.9 0.6 broadcast_select_fusion.pair_in
  2.5 1.4 copy.28.crop_offsets
  3.8 556.9 %train_step.1 = (f32[2,4,16,4608]{3,2,1,0:T(8,128)}, f32[2,4,16,4608]{3,2,1,0:T(8,128)}, f32[32,128]{1,0:T(8,128)}) custom-call(f32[12,6,6,512]{3,2,1,0:T(8,128)} %source.1, s32[12]{0:T(128)} %index_map.1, s32[12,2]{1,0:T(8,128)} %copy.28.crop_offsets, s32[12]{0:T(128)} %flip_flags.1, s32[12]{0:T(128)} %labels.1, s32[12]{0:T(128)} %valid_mask.1, ...), custom_call_target="tpu_custom_call" | custom-call | tf_op jit(solution)/shard_map/train_step/pallas_call | solution.py:1577
  560.8 0.0 copy-start
  560.8 0.0 copy-start.1
  560.8 0.0 copy-start.2
  560.8 0.0 copy-start.4
  560.8 0.0 copy-start.3
  560.8 0.0 copy-start.5
  560.8 0.0 copy-start.6
  560.9 9.6 %multiply_subtract_fusion = (f32[2,64,4608]{2,1,0:T(8,128)}, f32[2,64,4608]{2,1,0:T(8,128)}, f32[2,64,4608]{2,1,0:T(8,128)}, f32[2,64,4608]{2,1,0:T(8,128)}) fusion(f32[2,64,4608]{2,1,0:T(8,128)} %param.22, f32[2,4,16,4608]{3,2,1,0:T(8,128)} %get-tuple-element.16, f32[2,64,4608]{2,1,0:T(8,128)} %param.26, f32[2,64,4608]{2,1,0:T(8,128)} %param.27, ...), kind=kLoop, calls=%fused_computation.4 | loop fusion | flops 9437184 | bytes 21233664 | tf_op jit(solution)/shard_map/sub | solution.py:1605
  570.5 0.0 copy-done
  570.5 0.0 copy-done.1
  570.5 0.0 copy-done.2
  570.5 0.0 copy-done.4
  570.5 0.7 multiply_subtract_fusion.1
  571.2 0.0 copy-done.3
  571.2 0.0 copy-done.5
  571.2 0.0 copy-done.6
  571.2 0.7 multiply_subtract_fusion.2
  571.9 0.5 fusion.6
  (4 shorter events, 0.0 us)
Async XLA Ops:
  560.8 9.7 %copy-start = (f32[64,10]{0,1:T(8,128)S(1)}, f32[64,10]{0,1:T(8,128)}, u32[]{:S(2)}) copy-start(f32[64,10]{0,1:T(8,128)} %param.24) | copy-start | bytes 7684
  560.8 9.7 %copy-start.1 = (f32[64,10]{0,1:T(8,128)S(1)}, f32[64,10]{0,1:T(8,128)}, u32[]{:S(2)}) copy-start(f32[64,10]{0,1:T(8,128)} %param.30) | copy-start | bytes 7684
  560.8 9.7 %copy-start.2 = (f32[64,10]{0,1:T(8,128)S(1)}, f32[64,10]{0,1:T(8,128)}, u32[]{:S(2)}) copy-start(f32[64,10]{0,1:T(8,128)} %param.31) | copy-start | bytes 7684
  560.8 9.7 %copy-start.4 = (f32[32,128]{1,0:T(8,128)S(1)}, f32[32,128]{1,0:T(8,128)}, u32[]{:S(2)}) copy-start(f32[32,128]{1,0:T(8,128)} %get-tuple-element.15) | copy-start | bytes 49156
  560.8 10.4 %copy-start.3 = (f32[4,64]{1,0:T(4,128)S(1)}, f32[4,64]{1,0:T(4,128)}, u32[]{:S(2)}) copy-start(f32[4,64]{1,0:T(4,128)} %param.23) | copy-start | bytes 3076
  560.8 10.4 %copy-start.5 = (f32[4,64]{1,0:T(4,128)S(1)}, f32[4,64]{1,0:T(4,128)}, u32[]{:S(2)}) copy-start(f32[4,64]{1,0:T(4,128)} %param.28) | copy-start | bytes 3076
  560.8 10.4 %copy-start.6 = (f32[4,64]{1,0:T(4,128)S(1)}, f32[4,64]{1,0:T(4,128)}, u32[]{:S(2)}) copy-start(f32[4,64]{1,0:T(4,128)} %param.29) | copy-start | bytes 3076

commit v7 on v6

--- a/solution.py
+++ b/solution.py
@@ -279,9 +279,6 @@
         load.start()
     stats_own[...] = jnp.zeros_like(stats_own)
     channel[...] = jnp.zeros_like(channel)
-    x_both[...] = jnp.zeros_like(x_both)
-    a_both[...] = jnp.zeros_like(a_both)
-    b_both[...] = jnp.zeros_like(b_both)
     label_box[0] = jnp.zeros(label_box.shape[1:], jnp.float32)
     lane = lax.broadcasted_iota(jnp.int32, (1, LANES), 1)
 
@@ -300,7 +297,7 @@
         top, left = crop_offsets[image, 0], crop_offsets[image, 1]
         for cell in range(16):
             column = left + jnp.where(flipped == 1, 3 - cell % 4, cell % 4)
-            x_box[part, cell, pl.ds(image, 1), :] = source_box[
+            x_box[part, pl.ds(cell * own_count + image, 1), :] = source_box[
                 picked, top + cell // 4, pl.ds(column, 1), :
             ]
 
@@ -319,7 +316,8 @@
     pl.semaphore_wait(barrier, 10)
 
     def ring_move(box, send, recv, block, step, way, half):
-        at = pl.ds(half * 8, 8)
+        size = box.shape[1] // 2
+        at = pl.ds(half * size, size)
         return remote(
             box.at[block, at],
             box.at[block, at],
@@ -491,6 +489,9 @@
         for step in range(0, 4):
             to_pair(which, step).wait_send()
 
+    x_both[...] = jnp.zeros_like(x_both)
+    a_both[...] = jnp.zeros_like(a_both)
+    b_both[...] = jnp.zeros_like(b_both)
     cut_end(0)
     for block in range(4):
         back_start((block,))
@@ -507,7 +508,7 @@
     chosen, valid = tags[:count], tags[count:]
 
     def each_cell(body, init=None):
-        return lax.fori_loop(0, 16, body, init)
+        return lax.fori_loop(0, 16, body, init, unroll=2)
 
     def window(ref, down, right, lanes=slice(None), first=0, after=4):
         seen = ref[pl.ds(down + first, after - first), right : right + 4, :, lanes]
@@ -996,32 +997,36 @@
 
     for load in k1_loads + d1_loads:
         load.wait()
+    ring_step(x_box, x_send, x_recv, 2)
     for group in range(GROUPS):
         for move in k1_moves[group * 3 : group * 3 + 3]:
             move.wait()
         k1_share(group).start()
-    ring_step(x_box, x_send, x_recv, 2)
     for block in range(4):
         back_forward((block,))
-    for group in range(GROUPS):
-        k1_share(group, True).wait_recv()
-        lax.fori_loop(group * 3, group * 3 + 3, split_one, None)
-    for group in range(GROUPS):
-        k1_share(group).wait_send()
     ring_step(x_box, x_send, x_recv, 3)
     ring_end(x_box, x_send, x_recv)
 
-    def place_images(cell, _):
+    for cell in range(16):
         for block in range(4):
-            x_row[block * own_count : (block + 1) * own_count] = x_box[block, cell]
+            x_row[block * own_count : (block + 1) * own_count] = x_box[
+                block, cell * own_count : (cell + 1) * own_count
+            ]
         high, low = halves(x_row[...])
         x_both[cell // 4 + 1, cell % 4 + 1, :, 0:channels] = high
         x_both[cell // 4 + 1, cell % 4 + 1, :, channels : 2 * channels] = low
         x_own[cell] = x_row[:, pl.ds(pl.multiple_of(part * LANES, LANES), LANES)]
 
-    each_cell(place_images)
     flow[...] = jnp.zeros_like(flow)
-    lax.fori_loop(0, 3, lambda row_of_taps, _: taps_forward(row_of_taps), None)
+
+    def primal_group(group, _):
+        k1_share(group, True).wait_recv()
+        lax.fori_loop(group * 3, group * 3 + 3, split_one, None)
+        taps_forward(group)
+
+    lax.fori_loop(0, GROUPS, primal_group, None)
+    for group in range(GROUPS):
+        k1_share(group).wait_send()
 
     def sums_primal(cell, carry):
         value = flow[cell]
@@ -1491,7 +1496,7 @@
         inner_part,
         inner_part,
         pltpu.VMEM(source.shape, f32),
-        pltpu.VMEM((4, cells, own_count, channels), f32),
+        pltpu.VMEM((4, cells * own_count, channels), f32),
         pltpu.VMEM((count, channels), f32),
         pltpu.VMEM((MAP + 2, MAP + 2, count, 2 * channels), b16),
         row_map,

time: 573 us -> 565 us (0.986)
  Pallas kernels: 557 us -> 549 us
    pallas_call x1, Pallas kernels: 557 us -> 549 us  [step_fused(): pl.pallas_call(functools.partial(step_kernel, rows, links.members, links....]
where the time goes in v7:
time: 565 us; the launch traced here: 564 us
  Pallas kernels  549 us (97%)
  other arithmetic  12.4 us (2%)
    pallas_call x1, Pallas kernels, step_fused(): pl.pallas_call(functools.partial(step_kernel, rows, links.members, links....  549 us

profile of v7, /device:TPU:0, one launch (start us, length us, event | category | flops | bytes accessed | tf_op | source)
XLA Modules:
  0.0 564.4 jit_solution(13080388880125668288)
XLA Ops:
  0.7 0.1 broadcast_in_dim.34
  0.7 0.1 broadcast_in_dim.35
  0.8 0.1 pad.1.clone
  0.9 0.1 pad.3.clone
  1.0 0.8 maximum_maximum_fusion
  1.8 0.1 broadcast_in_dim.40
  1.9 0.6 broadcast_select_fusion.pair_in
  2.5 1.4 copy.28.crop_offsets
  3.8 549.0 %train_step.1 = (f32[2,4,16,4608]{3,2,1,0:T(8,128)}, f32[2,4,16,4608]{3,2,1,0:T(8,128)}, f32[32,128]{1,0:T(8,128)}) custom-call(f32[12,6,6,512]{3,2,1,0:T(8,128)} %source.1, s32[12]{0:T(128)} %index_map.1, s32[12,2]{1,0:T(8,128)} %copy.28.crop_offsets, s32[12]{0:T(128)} %flip_flags.1, s32[12]{0:T(128)} %labels.1, s32[12]{0:T(128)} %valid_mask.1, ...), custom_call_target="tpu_custom_call" | custom-call | tf_op jit(solution)/shard_map/train_step/pallas_call | solution.py:1582
  552.8 0.0 copy-start
  552.8 0.0 copy-start.1
  552.8 0.0 copy-start.2
  552.8 0.0 copy-start.4
  552.8 0.0 copy-start.3
  552.9 0.0 copy-start.5
  552.9 0.0 copy-start.6
  552.9 9.6 %multiply_subtract_fusion = (f32[2,64,4608]{2,1,0:T(8,128)}, f32[2,64,4608]{2,1,0:T(8,128)}, f32[2,64,4608]{2,1,0:T(8,128)}, f32[2,64,4608]{2,1,0:T(8,128)}) fusion(f32[2,64,4608]{2,1,0:T(8,128)} %param.22, f32[2,4,16,4608]{3,2,1,0:T(8,128)} %get-tuple-element.16, f32[2,64,4608]{2,1,0:T(8,128)} %param.26, f32[2,64,4608]{2,1,0:T(8,128)} %param.27, ...), kind=kLoop, calls=%fused_computation.4 | loop fusion | flops 9437184 | bytes 21233664 | tf_op jit(solution)/shard_map/sub | solution.py:1610
  562.5 0.0 copy-done
  562.5 0.0 copy-done.1
  562.5 0.0 copy-done.2
  562.5 0.0 copy-done.4
  562.5 0.7 multiply_subtract_fusion.1
  563.2 0.0 copy-done.3
  563.2 0.0 copy-done.5
  563.2 0.0 copy-done.6
  563.2 0.7 multiply_subtract_fusion.2
  563.9 0.5 fusion.6
  (4 shorter events, 0.0 us)
Async XLA Ops:
  552.8 9.7 %copy-start = (f32[64,10]{0,1:T(8,128)S(1)}, f32[64,10]{0,1:T(8,128)}, u32[]{:S(2)}) copy-start(f32[64,10]{0,1:T(8,128)} %param.24) | copy-start | bytes 7684
  552.8 9.7 %copy-start.1 = (f32[64,10]{0,1:T(8,128)S(1)}, f32[64,10]{0,1:T(8,128)}, u32[]{:S(2)}) copy-start(f32[64,10]{0,1:T(8,128)} %param.30) | copy-start | bytes 7684
  552.8 9.7 %copy-start.2 = (f32[64,10]{0,1:T(8,128)S(1)}, f32[64,10]{0,1:T(8,128)}, u32[]{:S(2)}) copy-start(f32[64,10]{0,1:T(8,128)} %param.31) | copy-start | bytes 7684
  552.8 9.7 %copy-start.4 = (f32[32,128]{1,0:T(8,128)S(1)}, f32[32,128]{1,0:T(8,128)}, u32[]{:S(2)}) copy-start(f32[32,128]{1,0:T(8,128)} %get-tuple-element.15) | copy-start | bytes 49156
  552.8 10.4 %copy-start.3 = (f32[4,64]{1,0:T(4,128)S(1)}, f32[4,64]{1,0:T(4,128)}, u32[]{:S(2)}) copy-start(f32[4,64]{1,0:T(4,128)} %param.23) | copy-start | bytes 3076
  552.9 10.4 %copy-start.5 = (f32[4,64]{1,0:T(4,128)S(1)}, f32[4,64]{1,0:T(4,128)}, u32[]{:S(2)}) copy-start(f32[4,64]{1,0:T(4,128)} %param.28) | copy-start | bytes 3076
  552.9 10.4 %copy-start.6 = (f32[4,64]{1,0:T(4,128)S(1)}, f32[4,64]{1,0:T(4,128)}, u32[]{:S(2)}) copy-start(f32[4,64]{1,0:T(4,128)} %param.29) | copy-start | bytes 3076

commit v8 on v7

--- a/solution.py
+++ b/solution.py
@@ -1241,15 +1241,9 @@
         open_third(0)
         open_second(2)
 
-        def vector_half(half, _):
-            part_of_second(a_both, v2_hi, v2_lo, half, False)
-
-            @pl.when(half == 0)
-            def _():
-                open_third(1)
-                open_third(2)
-
-        lax.fori_loop(0, 2, vector_half, None)
+        part_of_second(a_both, v2_hi, v2_lo, 0, False)
+        open_third(1)
+        open_third(2)
         lax.fori_loop(0, GROUPS, forward_group, None)
         for group in range(GROUPS):
             open_end(group)
@@ -1270,6 +1264,7 @@
 
         put_sums(0, *sums_forward(n1))
         moves = sum_start(0, 8)
+        part_of_second(a_both, v2_hi, v2_lo, 1, False)
         total = sum_end(0, 8, moves) * inverse
         average, cross = total[0:1], total[1:2]
         scale, gain = row(channel, 0), row(channel, 1)

time: 565 us -> 560 us (level)
  no operation moved by 1% of the time
where the time goes in v8:
time: 560 us
  Pallas kernels  544 us (97%)
  other arithmetic  12.4 us (2%)
    pallas_call x1, Pallas kernels, step_fused(): pl.pallas_call(functools.partial(step_kernel, rows, links.members, links....  544 us

profile of v8, /device:TPU:0, one launch (start us, length us, event | category | flops | bytes accessed | tf_op | source)
XLA Modules:
  0.0 559.9 jit_solution(15575107190944413009)
XLA Ops:
  0.7 0.1 broadcast_in_dim.34
  0.7 0.1 broadcast_in_dim.35
  0.8 0.1 pad.1.clone
  0.9 0.1 pad.3.clone
  1.0 0.8 maximum_maximum_fusion
  1.8 0.1 broadcast_in_dim.40
  1.9 0.6 broadcast_select_fusion.pair_in
  2.5 1.4 copy.28.crop_offsets
  3.8 544.4 %train_step.1 = (f32[2,4,16,4608]{3,2,1,0:T(8,128)}, f32[2,4,16,4608]{3,2,1,0:T(8,128)}, f32[32,128]{1,0:T(8,128)}) custom-call(f32[12,6,6,512]{3,2,1,0:T(8,128)} %source.1, s32[12]{0:T(128)} %index_map.1, s32[12,2]{1,0:T(8,128)} %copy.28.crop_offsets, s32[12]{0:T(128)} %flip_flags.1, s32[12]{0:T(128)} %labels.1, s32[12]{0:T(128)} %valid_mask.1, ...), custom_call_target="tpu_custom_call" | custom-call | tf_op jit(solution)/shard_map/train_step/pallas_call | solution.py:1577
  548.2 0.0 copy-start
  548.3 0.0 copy-start.1
  548.3 0.0 copy-start.2
  548.3 0.0 copy-start.4
  548.3 0.0 copy-start.3
  548.3 0.0 copy-start.5
  548.3 0.0 copy-start.6
  548.3 9.6 %multiply_subtract_fusion = (f32[2,64,4608]{2,1,0:T(8,128)}, f32[2,64,4608]{2,1,0:T(8,128)}, f32[2,64,4608]{2,1,0:T(8,128)}, f32[2,64,4608]{2,1,0:T(8,128)}) fusion(f32[2,64,4608]{2,1,0:T(8,128)} %param.22, f32[2,4,16,4608]{3,2,1,0:T(8,128)} %get-tuple-element.16, f32[2,64,4608]{2,1,0:T(8,128)} %param.26, f32[2,64,4608]{2,1,0:T(8,128)} %param.27, ...), kind=kLoop, calls=%fused_computation.4 | loop fusion | flops 9437184 | bytes 21233664 | tf_op jit(solution)/shard_map/sub | solution.py:1605
  557.9 0.0 copy-done
  557.9 0.0 copy-done.1
  557.9 0.0 copy-done.2
  558.0 0.0 copy-done.4
  558.0 0.7 multiply_subtract_fusion.1
  558.7 0.0 copy-done.3
  558.7 0.0 copy-done.5
  558.7 0.0 copy-done.6
  558.7 0.7 multiply_subtract_fusion.2
  559.4 0.5 fusion.6
  (4 shorter events, 0.0 us)
Async XLA Ops:
  548.2 9.7 %copy-start = (f32[64,10]{0,1:T(8,128)S(1)}, f32[64,10]{0,1:T(8,128)}, u32[]{:S(2)}) copy-start(f32[64,10]{0,1:T(8,128)} %param.24) | copy-start | bytes 7684
  548.3 9.7 %copy-start.1 = (f32[64,10]{0,1:T(8,128)S(1)}, f32[64,10]{0,1:T(8,128)}, u32[]{:S(2)}) copy-start(f32[64,10]{0,1:T(8,128)} %param.30) | copy-start | bytes 7684
  548.3 9.7 %copy-start.2 = (f32[64,10]{0,1:T(8,128)S(1)}, f32[64,10]{0,1:T(8,128)}, u32[]{:S(2)}) copy-start(f32[64,10]{0,1:T(8,128)} %param.31) | copy-start | bytes 7684
  548.3 9.7 %copy-start.4 = (f32[32,128]{1,0:T(8,128)S(1)}, f32[32,128]{1,0:T(8,128)}, u32[]{:S(2)}) copy-start(f32[32,128]{1,0:T(8,128)} %get-tuple-element.15) | copy-start | bytes 49156
  548.3 10.4 %copy-start.3 = (f32[4,64]{1,0:T(4,128)S(1)}, f32[4,64]{1,0:T(4,128)}, u32[]{:S(2)}) copy-start(f32[4,64]{1,0:T(4,128)} %param.23) | copy-start | bytes 3076
  548.3 10.4 %copy-start.5 = (f32[4,64]{1,0:T(4,128)S(1)}, f32[4,64]{1,0:T(4,128)}, u32[]{:S(2)}) copy-start(f32[4,64]{1,0:T(4,128)} %param.28) | copy-start | bytes 3076
  548.3 10.4 %copy-start.6 = (f32[4,64]{1,0:T(4,128)S(1)}, f32[4,64]{1,0:T(4,128)}, u32[]{:S(2)}) copy-start(f32[4,64]{1,0:T(4,128)} %param.29) | copy-start | bytes 3076
